TPU v7x, 32 devices: a whole 2x2x4 slice. The times are simulated.
32 devices in a mesh: gx: 4 (over y, x), gy: 8 (over z, core).
Axes of the slice: x: 2, y: 2, z: 4, core: 2. Of those that a mesh axis runs over, the one named last changes fastest.
Arguments:
- spatial_factor: float32 [16, 128, 32, 64], P('gx', 'gy'), may hold values from -60 to 60
- coupling: float32 [64, 64], replicated, may hold values from -1 to 5
- orient_factor: float32 [2048, 64], replicated, may hold values from -6 to 6
- directions: float32 [3, 2048], replicated, may hold values from -1 to 1, as said below
Outputs:
- new_spatial: float32 [16, 128, 32, 64], P('gx', 'gy')
- new_coupling: float32 [64, 64], replicated
- new_orient: float32 [2048, 64], replicated
Inputs may be any that keep to these rules, and one draw needn't show every extreme that they name: `directions`: each column is a unit vector.
All inputs are finite; a program needn't handle non-finite values.
Results may differ from a plain program's by a relative error of at most 0.0003.
Values sent between devices are 32-bit elements; how exact they have to be, the bound alone decides.
No kernel may reach another device: no remote copies, remote signals or barrier semaphores. Data moves between devices by JAX's collectives and lax.ppermute only.
A program may use at most 64 MiB of HBM per device.

v0:
```python
import functools

import jax
import jax.numpy as jnp
from jax import lax
from jax.experimental import pallas as pl
from jax.experimental.pallas import tpu as pltpu
from jax.sharding import PartitionSpec as P

STEPS = 2

courant = 0.3
tumble = 0.2
highest = lax.Precision.HIGHEST
half = jnp.bfloat16
LANES = 128
VMEM_BYTES = 32 * 1024 * 1024


def mm(left, right, contract=(1, 0)):
    return lax.dot_general(
        left, right, (((contract[0],), (contract[1],)), ((), ())),
        precision=highest, preferred_element_type=jnp.float32,
    )


def dot(left, right, contract=(1, 0)):
    return lax.dot_general(
        left, right, (((contract[0],), (contract[1],)), ((), ())),
        preferred_element_type=jnp.float32,
    )


def halves(value):
    high = value.astype(half)
    return high, (value - high.astype(jnp.float32)).astype(half)


def three(left, right, contract):
    left_high, left_low = halves(left)
    right_high, right_low = halves(right)
    rows = left.shape[0]
    both = dot(jnp.concatenate([left_high, left_low], axis=0), right_high, contract)
    return both[:rows] + both[rows:] + dot(left_high, right_low, contract)


def lane_index(width):
    return lax.broadcasted_iota(jnp.int32, (1, width), 1)


def roll(value, shift):
    width = value.shape[1]
    shift = shift % width
    return value if shift == 0 else pltpu.roll(value, shift, axis=1)


def slabs_of(value, dims):
    slab = dims[1] * dims[2]
    return [value[:, x * slab:(x + 1) * slab] for x in range(dims[0])]


def y_layers(slabs, dims):
    lx, ly, lz = dims
    width = lx * lz
    owner = lane_index(width) // lz
    first = last = None
    for x in range(lx):
        head = roll(slabs[x][:, :width], lz * x)
        tail = roll(slabs[x][:, -width:], lz * (x + 1))
        first = head if first is None else jnp.where(owner == x, head, first)
        last = tail if last is None else jnp.where(owner == x, tail, last)
    return first, last


def y_ahead(slab, layer, x, dims):
    lz, width = dims[2], layer.shape[1]
    moved = roll(slab, -lz)
    edge = jnp.where(lane_index(width) >= width - lz, roll(layer, -lz * (x + 1)), moved[:, -width:])
    return jnp.concatenate([moved[:, :-width], edge], axis=1)


def y_behind(slab, layer, x, dims):
    lz, width = dims[2], layer.shape[1]
    moved = roll(slab, lz)
    edge = jnp.where(lane_index(width) < lz, roll(layer, -lz * x), moved[:, :width])
    return jnp.concatenate([edge, moved[:, width:]], axis=1)


def z_ahead(slab, dims):
    lz = dims[2]
    place = lane_index(slab.shape[1]) % lz
    return jnp.where(place == lz - 1, roll(slab, lz - 1), roll(slab, -1))


def z_behind(slab, dims):
    lz = dims[2]
    place = lane_index(slab.shape[1]) % lz
    return jnp.where(place == 0, roll(slab, 1 - lz), roll(slab, 1))


def motility(density):
    return 1.0 / (1.0 + density * density)


def speed_of(column, value):
    return motility(jnp.sum(column * value, axis=0, keepdims=True))


def signs(directions):
    return jnp.maximum(directions, 0.0), jnp.maximum(-directions, 0.0)


def tables(orient, directions):
    rank, count = orient.shape
    plus, minus = signs(directions)
    high, low = halves(orient)
    both = jnp.concatenate([high, low], axis=0)
    stack = [orient * part[d:d + 1] for d in range(3) for part in (plus, minus)]
    stack_high, stack_low = halves(jnp.concatenate(stack, axis=0))
    wide = dot(stack_high, both, (1, 1))
    summed = (wide[:, :rank] + wide[:, rank:] + dot(stack_low, high, (1, 1))) * (1.0 / count)
    return summed, jnp.sum(orient, axis=1, keepdims=True) * (1.0 / count)


def unit(rank):
    row = lax.broadcasted_iota(jnp.int32, (rank, rank), 0)
    col = lax.broadcasted_iota(jnp.int32, (rank, rank), 1)
    return jnp.where(row == col, 1.0, 0.0).astype(jnp.float32)


def stage_weights(table, mean, into):
    rank = mean.shape[0]
    blocks = [table[d * rank:(d + 1) * rank] for d in range(6)]
    total = blocks[0] + blocks[1] + blocks[2] + blocks[3] + blocks[4] + blocks[5]
    spread = jnp.broadcast_to(mean, (rank, rank))
    first = (1.0 - tumble) * unit(rank) + tumble * spread * spread.T
    stack = jnp.concatenate([first, -courant * total, courant * table], axis=0)
    column = mm(into, spread, (0, 0))[:, :1]
    return mm(stack, into), column


def factor(gram):
    rank = gram.shape[0]
    wide = jnp.concatenate([gram, unit(rank)], axis=1)
    group = 8
    rows = [wide[b * group:(b + 1) * group] for b in range(rank // group)]
    place = lax.broadcasted_iota(jnp.int32, (group, 1), 0)
    lane = lax.broadcasted_iota(jnp.int32, (group, 2 * rank), 1)
    for k in range(rank):
        b, i = divmod(k, group)
        row = rows[b][i:i + 1]
        scaled = row * (1.0 / row[:, k:k + 1])
        for c in range(b, rank // group):
            col = rows[c][:, k:k + 1]
            if c == b:
                col = jnp.where(place > i, col, 0.0)
            rows[c] = rows[c] - col * scaled
    done = []
    for b, block in enumerate(rows):
        pivot = jnp.sum(jnp.where(lane == place + b * group, block, 0.0), axis=1, keepdims=True)
        done.append(block * lax.rsqrt(pivot))
    done = jnp.concatenate(done, axis=0)
    return done[:, :rank], done[:, rank:]


def flat_weights(weights):
    rank = weights.shape[1]
    return jnp.concatenate([weights[b * rank:(b + 1) * rank] for b in range(weights.shape[0] // rank)], axis=1)


def call(body, outs, *args):
    return pl.pallas_call(
        body,
        out_shape=[jax.ShapeDtypeStruct(shape, jnp.float32) for shape in outs],
        in_specs=[pl.BlockSpec(memory_space=pltpu.VMEM)] * len(args),
        out_specs=[pl.BlockSpec(memory_space=pltpu.VMEM)] * len(outs),
        compiler_params=pltpu.CompilerParams(vmem_limit_bytes=VMEM_BYTES),
    )(*args)


def layer_shapes(rank, dims):
    lx, ly, lz = dims
    return [(rank, ly * lz)] * 2 + [(rank, lx * lz)] * 2


def write_layers(slabs, dims, refs):
    refs[0][...] = slabs[0]
    refs[1][...] = slabs[-1]
    refs[2][...], refs[3][...] = y_layers(slabs, dims)


def enter_kernel(dims, x_ref, field_ref, *layer_refs):
    field = x_ref[...].T
    field_ref[...] = field
    write_layers(slabs_of(field, dims), dims, layer_refs)


def table_kernel(v_ref, e_ref, s_ref, orient_ref, table_ref, mean_ref, weight_ref, column_ref):
    orient = v_ref[...].T
    orient_ref[...] = orient
    table, mean = tables(orient, e_ref[...])
    table_ref[...] = table
    mean_ref[...] = mean
    weights, column_ref[...] = stage_weights(table, mean, s_ref[...].T)
    weight_ref[...] = flat_weights(weights)


def k_kernel(dims, field_ref, xb_ref, xa_ref, yb_ref, ya_ref, weight_ref, column_ref, out_ref, *layer_refs):
    lx, ly, lz = dims
    slab = ly * lz
    column = column_ref[...]
    rank = column.shape[0]

    def flux_of(value):
        return speed_of(column, value) * value

    fields = slabs_of(field_ref[...], dims)
    flux = [flux_of(f) for f in fields]
    before, after = flux_of(xb_ref[...]), flux_of(xa_ref[...])
    layer_before, layer_after = flux_of(yb_ref[...]), flux_of(ya_ref[...])
    w_high, w_low = halves(weight_ref[...])
    w_both = jnp.concatenate([w_high, w_low], axis=0)
    results = []
    for x in range(lx):
        g = flux[x]
        stack = [
            fields[x],
            g,
            flux[x - 1] if x > 0 else before,
            flux[x + 1] if x < lx - 1 else after,
            y_behind(g, layer_before, x, dims),
            y_ahead(g, layer_after, x, dims),
            z_behind(g, dims),
            z_ahead(g, dims),
        ]
        high, low = halves(jnp.concatenate(stack, axis=0))
        wide = dot(w_both, high)
        result = wide[:rank] + wide[rank:] + dot(w_high, low)
        out_ref[:, x * slab:(x + 1) * slab] = result
        results.append(result)
    write_layers(results, dims, layer_refs)


def galerkin_kernel(dims, k_ref, xa_ref, ya_ref, mean_ref, out_ref):
    lx, ly, lz = dims
    mean = mean_ref[...]
    rank = mean.shape[0]
    fields = slabs_of(k_ref[...], dims)
    after, layer = xa_ref[...], ya_ref[...]
    speeds = [speed_of(mean, f) for f in fields] + [speed_of(mean, after)]
    sums = [jnp.zeros((rank, 2 * rank), jnp.float32) for _ in range(4)]
    for x in range(lx):
        k = fields[x]
        q = speeds[x] * k
        pairs = [(k, k)]
        moved = fields[x + 1] if x < lx - 1 else after
        pairs.append((moved, speeds[x + 1] * k))
        for moved in (y_ahead(k, layer, x, dims), z_ahead(k, dims)):
            pairs.append((moved, speed_of(mean, moved) * k))
        for n, (left, right) in enumerate(pairs):
            sums[n] = sums[n] + three(left, jnp.concatenate([right, q], axis=0), (1, 1))
    for n in range(4):
        out_ref[n * rank:(n + 1) * rank] = sums[n]


def orient_stage(cells, sums, orient, table, mean, directions):
    rank, count = orient.shape
    plus, minus = signs(directions)
    blocks = [sums[n * rank:(n + 1) * rank] * (1.0 / cells) for n in range(4)]
    table = [table[d * rank:(d + 1) * rank] for d in range(6)]
    upper, inverse = factor(blocks[0][:, :rank])
    d_sum = blocks[0][:, rank:]
    back = [d_sum - blocks[1 + d][:, rank:] for d in range(3)]
    fore = [blocks[1 + d][:, :rank].T - d_sum for d in range(3)]
    drift = jnp.zeros((rank, rank), jnp.float32)
    for d in range(3):
        drift = drift + mm(back[d], table[2 * d]) - mm(fore[d], table[2 * d + 1])
    spread = jnp.broadcast_to(mean, (rank, rank))
    mid = (1.0 + tumble) * upper - tumble * mm(upper, spread) * spread.T + courant * mm(inverse, drift)
    solved = mm(inverse, mid, (0, 0))
    inner = jnp.concatenate([m for d in range(3) for m in (-back[d], fore[d])], axis=0)
    inner = mm(inner, solved)
    rows = [(1.0 - tumble) * mid]
    for n in range(6):
        rows.append(courant * mm(inverse, inner[n * rank:(n + 1) * rank]))
    rows_high, rows_low = halves(jnp.concatenate(rows, axis=0))
    high, low = halves(orient)
    moved = dot(
        jnp.concatenate([rows_high, rows_high, rows_low], axis=1),
        jnp.concatenate([high, low, high], axis=0),
    )
    new = moved[:rank] + tumble * mm(mid, spread)[:, :1]
    for d in range(3):
        new = new + plus[d:d + 1] * moved[(1 + 2 * d) * rank:(2 + 2 * d) * rank]
        new = new + minus[d:d + 1] * moved[(2 + 2 * d) * rank:(3 + 2 * d) * rank]
    upper_v, inverse_v = factor(three(new, new, (1, 1)) * (1.0 / count))
    return inverse, upper_v, three(inverse_v, new, (1, 0))


def turn_kernel(cells, sums_ref, orient_ref, table_ref, mean_ref, e_ref, orient_out, table_out, mean_out, weight_ref, column_ref):
    directions = e_ref[...]
    inverse, upper_v, orient = orient_stage(cells, sums_ref[...], orient_ref[...], table_ref[...], mean_ref[...], directions)
    orient_out[...] = orient
    table, mean = tables(orient, directions)
    table_out[...] = table
    mean_out[...] = mean
    weights, column_ref[...] = stage_weights(table, mean, mm(upper_v, inverse))
    weight_ref[...] = flat_weights(weights)


def last_kernel(cells, sums_ref, orient_ref, table_ref, mean_ref, e_ref, field_ref, x_ref, s_ref, v_ref):
    inverse, upper_v, orient = orient_stage(cells, sums_ref[...], orient_ref[...], table_ref[...], mean_ref[...], e_ref[...])
    x_ref[...] = three(inverse, field_ref[...], (1, 0)).T
    s_ref[...] = upper_v.T
    v_ref[...] = orient.T


def shifted(axis, up):
    count = lax.axis_size(axis)
    step = 1 if up else count - 1
    return [(i, (i + step) % count) for i in range(count)]


def all_sum(part):
    count = lax.axis_size("gx") * lax.axis_size("gy")
    rows, width = part.shape
    padded = -(-rows // count) * count
    if padded != rows:
        part = jnp.pad(part, ((0, padded - rows), (0, 0)))
    split = part.reshape(count, padded // count, width)
    mine = lax.all_to_all(split, ("gx", "gy"), 0, 0).sum(axis=0)
    every = lax.all_to_all(jnp.broadcast_to(mine[None], split.shape), ("gx", "gy"), 0, 0)
    return every.reshape(padded, width)[:rows]


def ahead(layers):
    return (
        lax.ppermute(layers[0], "gx", shifted("gx", False)),
        lax.ppermute(layers[2], "gy", shifted("gy", False)),
    )


def behind(layers):
    return (
        lax.ppermute(layers[1], "gx", shifted("gx", True)),
        lax.ppermute(layers[3], "gy", shifted("gy", True)),
    )


def shards(spatial_factor, coupling, orient_factor, directions):
    dims = spatial_factor.shape[:3]
    rank = spatial_factor.shape[-1]
    sites = dims[0] * dims[1] * dims[2]
    count = orient_factor.shape[0]
    cells = sites * lax.axis_size("gx") * lax.axis_size("gy")
    layers = layer_shapes(rank, dims)
    stage = [(rank, count), (6 * rank, rank), (rank, 1), (rank, 8 * rank), (rank, 1)]
    field, *edges = call(
        functools.partial(enter_kernel, dims), [(rank, sites)] + layers, spatial_factor.reshape(sites, rank)
    )
    x_after, y_after = ahead(edges)
    x_before, y_before = behind(edges)
    orient, table, mean, weights, column = call(table_kernel, stage, orient_factor, directions, coupling)
    for step in range(STEPS):
        field, *edges = call(
            functools.partial(k_kernel, dims), [(rank, sites)] + layers,
            field, x_before, x_after, y_before, y_after, weights, column,
        )
        x_after, y_after = ahead(edges)
        if step < STEPS - 1:
            x_before, y_before = behind(edges)
        (part,) = call(
            functools.partial(galerkin_kernel, dims), [(4 * rank, 2 * rank)], field, x_after, y_after, mean
        )
        sums = all_sum(part)
        if step < STEPS - 1:
            orient, table, mean, weights, column = call(
                functools.partial(turn_kernel, cells), stage, sums, orient, table, mean, directions
            )
    new_spatial, new_coupling, new_orient = call(
        functools.partial(last_kernel, cells), [(sites, rank), (rank, rank), (count, rank)],
        sums, orient, table, mean, directions, field,
    )
    return new_spatial.reshape(spatial_factor.shape), new_coupling, new_orient


def solution(mesh):
    return jax.shard_map(
        shards,
        mesh=mesh,
        in_specs=(P("gx", "gy", None, None), P(), P(), P()),
        out_specs=(P("gx", "gy", None, None), P(), P()),
        check_vma=False,
    )
```

profile of v0, /device:TPU:0, one launch (start us, length us, event | category | flops | bytes accessed | tf_op | source)
XLA Modules:
  0.0 107.5 jit_solution(12513523913175566109)
XLA Ops:
  0.6 1.2 %copy-done = f32[4,16,32,64]{3,2,1,0:T(8,128)S(1)} copy-done((f32[4,16,32,64]{3,2,1,0:T(8,128)S(1)}, f32[4,16,32,64]{3,2,1,0:T(8,128)}, u32[]{:S(2)}) %copy-start) | copy-done | bytes 524312
  2.3 3.0 %collective-permute-start = (f32[64,512]{1,0:T(8,128)S(1)}, f32[64,512]{1,0:T(8,128)S(1)}, u32[]{:S(2)}, u32[]{:S(2)}) collective-permute-start(f32[64,512]{1,0:T(8,128)S(1)} %get-tuple-element.30), channel_id=1, source_target_pairs={{0,8},{8,16},{16,24},{24,0},{1,9},{9,17},{17,25},{25,1},{2,10},{10... | collective-permute-start | bytes 393224 | tf_op jit(solution)/shard_map/ppermute | solution.py:345
  5.3 1.0 collective-permute-start.1
  6.3 3.5 %collective-permute-start.3 = (f32[64,128]{1,0:T(8,128)S(1)}, f32[64,128]{1,0:T(8,128)S(1)}, u32[]{:S(2)}, u32[]{:S(2)}) collective-permute-start(f32[64,128]{1,0:T(8,128)S(1)} %get-tuple-element.33), channel_id=1, source_target_pairs={{0,7},{1,0},{2,1},{3,2},{4,3},{5,4},{6,5},{7,6},{8,15},{9,8},{10,9... | collective-permute-start | bytes 98312 | tf_op jit(solution)/shard_map/ppermute | solution.py:339
  10.2 1.8 %shard_map.68 = (f32[64,2048]{1,0:T(8,128)S(1)}, f32[384,64]{1,0:T(8,128)S(1)}, f32[64,1]{1,0:T(8,128)S(1)}, f32[64,512]{1,0:T(8,128)S(1)}, f32[64,1]{1,0:T(8,128)S(1)}) custom-call(f32[2048,64]{1,0:T(8,128)S(1)} %copy.7.v_ref, f32[3,2048]{1,0:T(4,128)S(1)} %copy-done.1, f32[64,64]{1,0:T(8,128)S(1)} %copy-done.2), custom_call_target="tpu_custom_call" | custom-call | tf_op jit(solution)/shard_map/pallas_call | solution.py:172
  12.8 1.4 %shard_map.69 = (f32[64,2048]{1,0:T(8,128)S(1)}, f32[64,512]{1,0:T(8,128)S(1)}, f32[64,512]{1,0:T(8,128)S(1)}, f32[64,128]{1,0:T(8,128)S(1)}, f32[64,128]{1,0:T(8,128)S(1)}) custom-call(f32[64,2048]{1,0:T(8,128)S(1)} %get-tuple-element.29.field_ref, f32[64,512]{1,0:T(8,128)S(1)} %collective-permute-done.xb_ref, f32[64,512]{1,0:T(8,128)S(1)} %collective-permute-done.1.xa_ref, ...), custom_call_target="tpu_custom_call" | custom-call | tf_op jit(solution)/shard_map/pallas_call | solution.py:172
  14.2 1.5 %collective-permute-start.5 = (f32[64,512]{1,0:T(8,128)S(1)}, f32[64,512]{1,0:T(8,128)S(1)}, u32[]{:S(2)}, u32[]{:S(2)}) collective-permute-start(f32[64,512]{1,0:T(8,128)S(1)} %get-tuple-element.38), channel_id=1, source_target_pairs={{0,24},{8,0},{16,8},{24,16},{1,25},{9,1},{17,9},{25,17},{2,26},{10... | collective-permute-start | bytes 393224 | tf_op jit(solution)/shard_map/ppermute | solution.py:338
  15.6 2.5 %collective-permute-start.7 = (f32[64,128]{1,0:T(8,128)S(1)}, f32[64,128]{1,0:T(8,128)S(1)}, u32[]{:S(2)}, u32[]{:S(2)}) collective-permute-start(f32[64,128]{1,0:T(8,128)S(1)} %get-tuple-element.40), channel_id=1, source_target_pairs={{0,7},{1,0},{2,1},{3,2},{4,3},{5,4},{6,5},{7,6},{8,15},{9,8},{10,9... | collective-permute-start | bytes 98312 | tf_op jit(solution)/shard_map/ppermute | solution.py:339
  18.1 1.6 %collective-permute-done.7.ya_ref = f32[64,128]{1,0:T(8,128)S(1)} collective-permute-done((f32[64,128]{1,0:T(8,128)S(1)}, f32[64,128]{1,0:T(8,128)S(1)}, u32[]{:S(2)}, u32[]{:S(2)}) %collective-permute-start.7) | collective-permute-done | bytes 32800 | tf_op jit(solution)/shard_map/ppermute | solution.py:339
  19.7 1.4 %shard_map.70 = f32[256,128]{1,0:T(8,128)S(1)} custom-call(f32[64,2048]{1,0:T(8,128)S(1)} %get-tuple-element.36.k_ref.field_ref, f32[64,512]{1,0:T(8,128)S(1)} %collective-permute-done.5.xa_ref, f32[64,128]{1,0:T(8,128)S(1)} %collective-permute-done.7.ya_ref, f32[64,1]{1,0:T(8,128)S(1)} %get-tuple-element.41.mean_ref), custom_call_target="tpu_custom_call" | custom-call | tf_op jit(solution)/shard_map/pallas_call | solution.py:172
  21.1 13.3 %all_to_all.20 = f32[32,8,128]{2,1,0:T(8,128)S(1)} all-to-all(f32[32,8,128]{2,1,0:T(8,128)S(1)} %bitcast.9), channel_id=1, replica_groups=mesh['gx'=4,'gy'=8] {'gx','gy'}, dimensions={0} | all-to-all | bytes 262144 | tf_op jit(solution)/shard_map/all_to_all | solution.py:331
  35.0 2.6 %all-to-all-start.1 = ((f32[32,8,128]{2,1,0:T(8,128)}), f32[32,8,128]{2,1,0:T(8,128)S(1)}, u32[]{:S(2)}, u32[]{:S(2)}) async-start(f32[32,8,128]{2,1,0:T(8,128)} %broadcast_in_dim.4), calls=%async_computation.1 | async-start | bytes 262144 | tf_op jit(solution)/shard_map/all_to_all | solution.py:332
  37.6 1.7 %collective-permute-start.4 = (f32[64,512]{1,0:T(8,128)S(1)}, f32[64,512]{1,0:T(8,128)S(1)}, u32[]{:S(2)}, u32[]{:S(2)}) collective-permute-start(f32[64,512]{1,0:T(8,128)S(1)} %get-tuple-element.37), channel_id=1, source_target_pairs={{0,8},{8,16},{16,24},{24,0},{1,9},{9,17},{17,25},{25,1},{2,10},{10... | collective-permute-start | bytes 393224 | tf_op jit(solution)/shard_map/ppermute | solution.py:345
  39.3 6.5 %all-to-all-done.1 = f32[32,8,128]{2,1,0:T(8,128)S(1)} async-done(((f32[32,8,128]{2,1,0:T(8,128)}), f32[32,8,128]{2,1,0:T(8,128)S(1)}, u32[]{:S(2)}, u32[]{:S(2)}) %all-to-all-start.1) | async-done | bytes 131104 | tf_op jit(solution)/shard_map/all_to_all | solution.py:332
  45.8 15.7 %shard_map.71 = (f32[64,2048]{1,0:T(8,128)S(1)}, f32[384,64]{1,0:T(8,128)S(1)}, f32[64,1]{1,0:T(8,128)S(1)}, f32[64,512]{1,0:T(8,128)S(1)}, f32[64,1]{1,0:T(8,128)S(1)}) custom-call(f32[256,128]{1,0:T(8,128)S(1)} %bitcast.7, f32[64,2048]{1,0:T(8,128)S(1)} %get-tuple-element.42.orient_ref, f32[384,64]{1,0:T(8,128)S(1)} %get-tuple-element.43.table_ref, ...), custom_call_target="tpu_custom_call" | custom-call | tf_op jit(solution)/shard_map/pallas_call | solution.py:172
  61.6 2.0 %shard_map.72 = (f32[64,2048]{1,0:T(8,128)S(1)}, f32[64,512]{1,0:T(8,128)S(1)}, f32[64,512]{1,0:T(8,128)}, f32[64,128]{1,0:T(8,128)S(1)}, f32[64,128]{1,0:T(8,128)}) custom-call(f32[64,2048]{1,0:T(8,128)S(1)} %get-tuple-element.36.k_ref.field_ref, f32[64,512]{1,0:T(8,128)S(1)} %collective-permute-done.4.xb_ref, f32[64,512]{1,0:T(8,128)S(1)} %collective-permute-done.5.xa_ref, ...), custom_call_target="tpu_custom_call" | custom-call | tf_op jit(solution)/shard_map/pallas_call | solution.py:172
  63.6 1.3 %collective-permute-start.8 = (f32[64,512]{1,0:T(8,128)S(1)}, f32[64,512]{1,0:T(8,128)S(1)}, u32[]{:S(2)}, u32[]{:S(2)}) collective-permute-start(f32[64,512]{1,0:T(8,128)S(1)} %get-tuple-element.47), channel_id=1, source_target_pairs={{0,24},{8,0},{16,8},{24,16},{1,25},{9,1},{17,9},{25,17},{2,26},{10... | collective-permute-start | bytes 393224 | tf_op jit(solution)/shard_map/ppermute | solution.py:338
  64.9 1.6 %collective-permute-done.9.ya_ref = f32[64,128]{1,0:T(8,128)S(1)} collective-permute-done((f32[64,128]{1,0:T(8,128)S(1)}, f32[64,128]{1,0:T(8,128)S(1)}, u32[]{:S(2)}, u32[]{:S(2)}) %collective-permute-start.9) | collective-permute-done | bytes 32800 | tf_op jit(solution)/shard_map/ppermute | solution.py:339
  66.5 3.2 %collective-permute-done.8.xa_ref = f32[64,512]{1,0:T(8,128)S(1)} collective-permute-done((f32[64,512]{1,0:T(8,128)S(1)}, f32[64,512]{1,0:T(8,128)S(1)}, u32[]{:S(2)}, u32[]{:S(2)}) %collective-permute-start.8) | collective-permute-done | bytes 131104 | tf_op jit(solution)/shard_map/ppermute | solution.py:338
  69.7 1.4 %shard_map.73 = f32[256,128]{1,0:T(8,128)S(1)} custom-call(f32[64,2048]{1,0:T(8,128)S(1)} %get-tuple-element.46.k_ref.field_ref, f32[64,512]{1,0:T(8,128)S(1)} %collective-permute-done.8.xa_ref, f32[64,128]{1,0:T(8,128)S(1)} %collective-permute-done.9.ya_ref, f32[64,1]{1,0:T(8,128)S(1)} %get-tuple-element.49.mean_ref), custom_call_target="tpu_custom_call" | custom-call | tf_op jit(solution)/shard_map/pallas_call | solution.py:172
  71.1 10.0 %all_to_all.21 = f32[32,8,128]{2,1,0:T(8,128)S(1)} all-to-all(f32[32,8,128]{2,1,0:T(8,128)S(1)} %bitcast.8), channel_id=1, replica_groups=mesh['gx'=4,'gy'=8] {'gx','gy'}, dimensions={0} | all-to-all | bytes 262144 | tf_op jit(solution)/shard_map/all_to_all | solution.py:331
  81.1 9.9 %all_to_all.22 = f32[32,8,128]{2,1,0:T(8,128)S(1)} all-to-all(f32[32,8,128]{2,1,0:T(8,128)S(1)} %broadcast_in_dim.5), channel_id=1, replica_groups=mesh['gx'=4,'gy'=8] {'gx','gy'}, dimensions={0} | all-to-all | bytes 262144 | tf_op jit(solution)/shard_map/all_to_all | solution.py:332
  91.0 15.3 %shard_map.74 = (f32[2048,64]{1,0:T(8,128)}, f32[64,64]{1,0:T(8,128)}, f32[2048,64]{1,0:T(8,128)S(1)}) custom-call(f32[256,128]{1,0:T(8,128)S(1)} %bitcast.10, f32[64,2048]{1,0:T(8,128)S(1)} %get-tuple-element.50.orient_ref, f32[384,64]{1,0:T(8,128)S(1)} %get-tuple-element.51.table_ref, f32[64,1]{1,0:T(8,128)S(1)} %get-tuple-element.49.mean_ref, ...), custom_call_target="tpu_custom_call" | custom-call | tf_op jit(solution)/shard_map/pallas_call | solution.py:172
  106.3 1.1 %copy.8 = f32[2048,64]{0,1:T(8,128)} copy(f32[2048,64]{1,0:T(8,128)S(1)} %get-tuple-element.57) | data formatting | bytes 1048576
  (23 shorter events, 2.2 us)
Async XLA Ops:
  0.6 1.2 %copy-start = (f32[4,16,32,64]{3,2,1,0:T(8,128)S(1)}, f32[4,16,32,64]{3,2,1,0:T(8,128)}, u32[]{:S(2)}) copy-start(f32[4,16,32,64]{3,2,1,0:T(8,128)} %param.4) | copy-start | bytes 1572868
  1.9 8.0 %copy-start.3 = (f32[2048,64]{0,1:T(8,128)S(1)}, f32[2048,64]{0,1:T(8,128)}, u32[]{:S(2)}) copy-start(f32[2048,64]{0,1:T(8,128)} %param.6) | copy-start | bytes 1572868
  2.3 9.8 %collective-permute-start = (f32[64,512]{1,0:T(8,128)S(1)}, f32[64,512]{1,0:T(8,128)S(1)}, u32[]{:S(2)}, u32[]{:S(2)}) collective-permute-start(f32[64,512]{1,0:T(8,128)S(1)} %get-tuple-element.30), channel_id=1, source_target_pairs={{0,8},{8,16},{16,24},{24,0},{1,9},{9,17},{17,25},{25,1},{2,10},{10... | collective-permute-start | bytes 393224 | tf_op jit(solution)/shard_map/ppermute | solution.py:345
  5.3 7.5 %collective-permute-start.1 = (f32[64,512]{1,0:T(8,128)S(1)}, f32[64,512]{1,0:T(8,128)S(1)}, u32[]{:S(2)}, u32[]{:S(2)}) collective-permute-start(f32[64,512]{1,0:T(8,128)S(1)} %get-tuple-element.31), channel_id=1, source_target_pairs={{0,24},{8,0},{16,8},{24,16},{1,25},{9,1},{17,9},{25,17},{2,26},{10... | collective-permute-start | bytes 393224 | tf_op jit(solution)/shard_map/ppermute | solution.py:338
  6.3 5.7 %collective-permute-start.2 = (f32[64,128]{1,0:T(8,128)S(1)}, f32[64,128]{1,0:T(8,128)S(1)}, u32[]{:S(2)}, u32[]{:S(2)}) collective-permute-start(f32[64,128]{1,0:T(8,128)S(1)} %get-tuple-element.32), channel_id=1, source_target_pairs={{0,1},{1,2},{2,3},{3,4},{4,5},{5,6},{6,7},{7,0},{8,9},{9,10},{10,1... | collective-permute-start | bytes 98312 | tf_op jit(solution)/shard_map/ppermute | solution.py:346
  6.3 3.9 %copy-start.1 = (f32[3,2048]{1,0:T(4,128)S(1)}, f32[3,2048]{1,0:T(4,128)}, u32[]{:S(2)}) copy-start(f32[3,2048]{1,0:T(4,128)} %e_ref.5) | copy-start | bytes 73732
  6.3 3.9 %copy-start.2 = (f32[64,64]{1,0:T(8,128)S(1)}, f32[64,64]{1,0:T(8,128)}, u32[]{:S(2)}) copy-start(f32[64,64]{1,0:T(8,128)} %s_ref.1) | copy-start | bytes 49156
  6.3 5.7 %collective-permute-start.3 = (f32[64,128]{1,0:T(8,128)S(1)}, f32[64,128]{1,0:T(8,128)S(1)}, u32[]{:S(2)}, u32[]{:S(2)}) collective-permute-start(f32[64,128]{1,0:T(8,128)S(1)} %get-tuple-element.33), channel_id=1, source_target_pairs={{0,7},{1,0},{2,1},{3,2},{4,3},{5,4},{6,5},{7,6},{8,15},{9,8},{10,9... | collective-permute-start | bytes 98312 | tf_op jit(solution)/shard_map/ppermute | solution.py:339
  14.2 5.5 %collective-permute-start.5 = (f32[64,512]{1,0:T(8,128)S(1)}, f32[64,512]{1,0:T(8,128)S(1)}, u32[]{:S(2)}, u32[]{:S(2)}) collective-permute-start(f32[64,512]{1,0:T(8,128)S(1)} %get-tuple-element.38), channel_id=1, source_target_pairs={{0,24},{8,0},{16,8},{24,16},{1,25},{9,1},{17,9},{25,17},{2,26},{10... | collective-permute-start | bytes 393224 | tf_op jit(solution)/shard_map/ppermute | solution.py:338
  15.6 4.1 %collective-permute-start.7 = (f32[64,128]{1,0:T(8,128)S(1)}, f32[64,128]{1,0:T(8,128)S(1)}, u32[]{:S(2)}, u32[]{:S(2)}) collective-permute-start(f32[64,128]{1,0:T(8,128)S(1)} %get-tuple-element.40), channel_id=1, source_target_pairs={{0,7},{1,0},{2,1},{3,2},{4,3},{5,4},{6,5},{7,6},{8,15},{9,8},{10,9... | collective-permute-start | bytes 98312 | tf_op jit(solution)/shard_map/ppermute | solution.py:339
  35.0 10.8 %all-to-all-start.1 = ((f32[32,8,128]{2,1,0:T(8,128)}), f32[32,8,128]{2,1,0:T(8,128)S(1)}, u32[]{:S(2)}, u32[]{:S(2)}) async-start(f32[32,8,128]{2,1,0:T(8,128)} %broadcast_in_dim.4), calls=%async_computation.1 | async-start | bytes 262144 | tf_op jit(solution)/shard_map/all_to_all | solution.py:332
  37.6 23.9 %collective-permute-start.4 = (f32[64,512]{1,0:T(8,128)S(1)}, f32[64,512]{1,0:T(8,128)S(1)}, u32[]{:S(2)}, u32[]{:S(2)}) collective-permute-start(f32[64,512]{1,0:T(8,128)S(1)} %get-tuple-element.37), channel_id=1, source_target_pairs={{0,8},{8,16},{16,24},{24,0},{1,9},{9,17},{17,25},{25,1},{2,10},{10... | collective-permute-start | bytes 393224 | tf_op jit(solution)/shard_map/ppermute | solution.py:345
  39.3 22.2 %collective-permute-start.6 = (f32[64,128]{1,0:T(8,128)S(1)}, f32[64,128]{1,0:T(8,128)S(1)}, u32[]{:S(2)}, u32[]{:S(2)}) collective-permute-start(f32[64,128]{1,0:T(8,128)S(1)} %get-tuple-element.39), channel_id=1, source_target_pairs={{0,1},{1,2},{2,3},{3,4},{4,5},{5,6},{6,7},{7,0},{8,9},{9,10},{10,1... | collective-permute-start | bytes 98312 | tf_op jit(solution)/shard_map/ppermute | solution.py:346
  63.6 6.1 %collective-permute-start.8 = (f32[64,512]{1,0:T(8,128)S(1)}, f32[64,512]{1,0:T(8,128)S(1)}, u32[]{:S(2)}, u32[]{:S(2)}) collective-permute-start(f32[64,512]{1,0:T(8,128)S(1)} %get-tuple-element.47), channel_id=1, source_target_pairs={{0,24},{8,0},{16,8},{24,16},{1,25},{9,1},{17,9},{25,17},{2,26},{10... | collective-permute-start | bytes 393224 | tf_op jit(solution)/shard_map/ppermute | solution.py:338
  64.9 1.6 %collective-permute-start.9 = (f32[64,128]{1,0:T(8,128)S(1)}, f32[64,128]{1,0:T(8,128)S(1)}, u32[]{:S(2)}, u32[]{:S(2)}) collective-permute-start(f32[64,128]{1,0:T(8,128)S(1)} %get-tuple-element.48), channel_id=1, source_target_pairs={{0,7},{1,0},{2,1},{3,2},{4,3},{5,4},{6,5},{7,6},{8,15},{9,8},{10,9... | collective-permute-start | bytes 98312 | tf_op jit(solution)/shard_map/ppermute | solution.py:339
where the time goes:
time: 108 us; the launch traced here: 107 us
  Pallas kernels  39.5 us (37%)
  blocking collectives  33.2 us (31%)
  starting transfers between devices  17.1 us (16%)
  waiting for transfers between devices  13.6 us (13%)
  local copies, waits for them, and re-layouts  3.35 us (3%)
    pallas_call x8, Pallas kernels, call(): pl.pallas_call(body, out_shape=[jax.ShapeDtypeStruct(shape, jnp.float32)...  39.5 us
    all_to_all x2, blocking collectives, all_sum(): mine = lax.all_to_all(split, ('gx', 'gy'), 0, 0).sum(axis=0)  23.3 us
    all_to_all x1, blocking collectives, all_sum(): lax.all_to_all(jnp.broadcast_to(mine[None], split.shape), ('gx', 'gy'), 0...  9.88 us
    all_to_all x1, waiting for transfers between devices, all_sum(): lax.all_to_all(jnp.broadcast_to(mine[None], split.shape), ('gx', 'gy'), 0...  6.48 us
    ppermute x3, starting transfers between devices, ahead(): lax.ppermute(layers[2], 'gy', shifted('gy', False))  6 us
    ppermute x2, starting transfers between devices, behind(): lax.ppermute(layers[1], 'gx', shifted('gx', True))  4.68 us
    ppermute x3, waiting for transfers between devices, ahead(): lax.ppermute(layers[0], 'gx', shifted('gx', False))  3.88 us
    ppermute x3, starting transfers between devices, ahead(): lax.ppermute(layers[0], 'gx', shifted('gx', False))  3.82 us
  transfers between devices with their start and end apart: 11, of which 5 were waited for; matrix products, arithmetic and copies ran while one was open for 0% of the time, Pallas kernels for 16%

commit v1 on v0

--- a/solution.py
+++ b/solution.py
@@ -7,8 +7,6 @@
 from jax.experimental.pallas import tpu as pltpu
 from jax.sharding import PartitionSpec as P
 
-STEPS = 2
-
 courant = 0.3
 tumble = 0.2
 highest = lax.Precision.HIGHEST
@@ -59,31 +57,30 @@
     return [value[:, x * slab:(x + 1) * slab] for x in range(dims[0])]
 
 
-def y_layers(slabs, dims):
+def y_layer(slabs, dims, index):
     lx, ly, lz = dims
     width = lx * lz
+    start = index * lz // width * width
     owner = lane_index(width) // lz
-    first = last = None
+    layer = None
     for x in range(lx):
-        head = roll(slabs[x][:, :width], lz * x)
-        tail = roll(slabs[x][:, -width:], lz * (x + 1))
-        first = head if first is None else jnp.where(owner == x, head, first)
-        last = tail if last is None else jnp.where(owner == x, tail, last)
-    return first, last
-
-
-def y_ahead(slab, layer, x, dims):
-    lz, width = dims[2], layer.shape[1]
+        line = roll(slabs[x][:, start:start + width], lz * x - (index * lz - start))
+        layer = line if layer is None else jnp.where(owner == x, line, layer)
+    return layer
+
+
+def y_ahead(slab, edge, dims):
+    lz, width = dims[2], edge.shape[1]
     moved = roll(slab, -lz)
-    edge = jnp.where(lane_index(width) >= width - lz, roll(layer, -lz * (x + 1)), moved[:, -width:])
-    return jnp.concatenate([moved[:, :-width], edge], axis=1)
-
-
-def y_behind(slab, layer, x, dims):
-    lz, width = dims[2], layer.shape[1]
+    last = jnp.where(lane_index(width) >= width - lz, edge, moved[:, -width:])
+    return jnp.concatenate([moved[:, :-width], last], axis=1)
+
+
+def y_behind(slab, edge, dims):
+    lz, width = dims[2], edge.shape[1]
     moved = roll(slab, lz)
-    edge = jnp.where(lane_index(width) < lz, roll(layer, -lz * x), moved[:, :width])
-    return jnp.concatenate([edge, moved[:, width:]], axis=1)
+    first = jnp.where(lane_index(width) < lz, edge, moved[:, :width])
+    return jnp.concatenate([first, moved[:, width:]], axis=1)
 
 
 def z_ahead(slab, dims):
@@ -141,25 +138,58 @@
 
 def factor(gram):
     rank = gram.shape[0]
-    wide = jnp.concatenate([gram, unit(rank)], axis=1)
     group = 8
-    rows = [wide[b * group:(b + 1) * group] for b in range(rank // group)]
-    place = lax.broadcasted_iota(jnp.int32, (group, 1), 0)
-    lane = lax.broadcasted_iota(jnp.int32, (group, 2 * rank), 1)
-    for k in range(rank):
-        b, i = divmod(k, group)
-        row = rows[b][i:i + 1]
-        scaled = row * (1.0 / row[:, k:k + 1])
-        for c in range(b, rank // group):
-            col = rows[c][:, k:k + 1]
-            if c == b:
-                col = jnp.where(place > i, col, 0.0)
-            rows[c] = rows[c] - col * scaled
+    shape = (group, 2 * rank)
+    eye = unit(rank)
+    diag_row = jnp.sum(eye * gram, axis=0, keepdims=True)
+    diag_column = jnp.sum(eye * gram, axis=1, keepdims=True)
+    scale = lax.rsqrt(diag_row)
+    wide = jnp.concatenate([gram * lax.rsqrt(diag_column) * scale, eye], axis=1)
+    blocks = rank // group
+    rows = [wide[b * group:(b + 1) * group] for b in range(blocks)]
+    place = lax.broadcasted_iota(jnp.int32, shape, 0)
+    lane = lax.broadcasted_iota(jnp.int32, shape, 1)
+
+    def spread(value, i):
+        return jnp.broadcast_to(value[i:i + 1], shape)
+
+    for b in range(blocks):
+        start = b * group
+        cols = {
+            c: [jnp.broadcast_to(rows[c][:, start + j:start + j + 1], shape) for j in range(group)]
+            for c in range(b, blocks)
+        }
+        for j in range(0, group, 2):
+            first, second = cols[b][j], cols[b][j + 1]
+            p, o, q = spread(first, j), spread(second, j), spread(second, j + 1)
+            over = 1.0 / (p * q - o * o)
+            p, o, q = p * over, o * over, q * over
+
+            def solve(value):
+                upper, lower = spread(value, j), spread(value, j + 1)
+                return q * upper - o * lower, p * lower - o * upper
+
+            later = [solve(cols[b][n]) for n in range(j + 2, group)]
+            row_first, row_second = solve(rows[b])
+            for c in range(b, blocks):
+                left, right = cols[c][j], cols[c][j + 1]
+                if c == b:
+                    if j == group - 2:
+                        continue
+                    left, right = jnp.where(place > j + 1, left, 0.0), jnp.where(place > j + 1, right, 0.0)
+                for n, (up, low) in enumerate(later):
+                    cols[c][j + 2 + n] = cols[c][j + 2 + n] - left * up - right * low
+                rows[c] = rows[c] - left * row_first - right * row_second
     done = []
     for b, block in enumerate(rows):
-        pivot = jnp.sum(jnp.where(lane == place + b * group, block, 0.0), axis=1, keepdims=True)
-        done.append(block * lax.rsqrt(pivot))
-    done = jnp.concatenate(done, axis=0)
+        at = place + b * group
+        pivot = jnp.sum(jnp.where(lane == at, block, 0.0), axis=1, keepdims=True)
+        beside = jnp.sum(jnp.where((lane == at - 1) & (place % 2 == 1), block, 0.0), axis=1, keepdims=True)
+        pivot = jnp.broadcast_to(pivot, shape)
+        part = beside / pltpu.roll(pivot, 1, axis=0)
+        block = block - part * pltpu.roll(block, 1, axis=0)
+        done.append(block * lax.rsqrt(pivot - part * beside))
+    done = jnp.concatenate(done, axis=0) * jnp.concatenate([diag_row * scale, scale], axis=1)
     return done[:, :rank], done[:, rank:]
 
 
@@ -178,21 +208,12 @@
     )(*args)
 
 
-def layer_shapes(rank, dims):
-    lx, ly, lz = dims
-    return [(rank, ly * lz)] * 2 + [(rank, lx * lz)] * 2
-
-
-def write_layers(slabs, dims, refs):
-    refs[0][...] = slabs[0]
-    refs[1][...] = slabs[-1]
-    refs[2][...], refs[3][...] = y_layers(slabs, dims)
-
-
-def enter_kernel(dims, x_ref, field_ref, *layer_refs):
+def enter_kernel(dims, x_ref, field_ref, first_ref, last_ref, y_first_ref, y_last_ref):
     field = x_ref[...].T
     field_ref[...] = field
-    write_layers(slabs_of(field, dims), dims, layer_refs)
+    slabs = slabs_of(field, dims)
+    first_ref[...], last_ref[...] = slabs[0], slabs[-1]
+    y_first_ref[...], y_last_ref[...] = y_layer(slabs, dims, 0), y_layer(slabs, dims, dims[1] - 1)
 
 
 def table_kernel(v_ref, e_ref, s_ref, orient_ref, table_ref, mean_ref, weight_ref, column_ref):
@@ -205,62 +226,100 @@
     weight_ref[...] = flat_weights(weights)
 
 
-def k_kernel(dims, field_ref, xb_ref, xa_ref, yb_ref, ya_ref, weight_ref, column_ref, out_ref, *layer_refs):
+def weighted(weights, rank):
+    w_high, w_low = halves(weights)
+    w_both = jnp.concatenate([w_high, w_low], axis=0)
+
+    def product(stack):
+        high, low = halves(jnp.concatenate(stack, axis=0))
+        wide = dot(w_both, high)
+        return wide[:rank] + wide[rank:] + dot(w_high, low)
+
+    return product
+
+
+def k_stage(dims, field, weights, column, xb, xa, yb, ya, further=None):
     lx, ly, lz = dims
-    slab = ly * lz
-    column = column_ref[...]
-    rank = column.shape[0]
+    slab, width = ly * lz, lx * lz
 
     def flux_of(value):
         return speed_of(column, value) * value
 
-    fields = slabs_of(field_ref[...], dims)
+    product = weighted(weights, column.shape[0])
+    fields = slabs_of(field, dims) + [xa]
     flux = [flux_of(f) for f in fields]
-    before, after = flux_of(xb_ref[...]), flux_of(xa_ref[...])
-    layer_before, layer_after = flux_of(yb_ref[...]), flux_of(ya_ref[...])
-    w_high, w_low = halves(weight_ref[...])
-    w_both = jnp.concatenate([w_high, w_low], axis=0)
+    before, layer, layer_before = flux_of(xb), flux_of(ya), flux_of(yb)
+    if further is not None:
+        second, corner_before, layer_next = [flux_of(f) for f in further]
+        corners = second[:, slab:]
+        corner_after = roll(corners, -2 * lz)
+        flux.append(second[:, :slab])
+    flux.append(before)
     results = []
-    for x in range(lx):
+    for x in range(lx if further is None else lx + 1):
         g = flux[x]
-        stack = [
-            fields[x],
-            g,
-            flux[x - 1] if x > 0 else before,
-            flux[x + 1] if x < lx - 1 else after,
-            y_behind(g, layer_before, x, dims),
-            y_ahead(g, layer_after, x, dims),
-            z_behind(g, dims),
-            z_ahead(g, dims),
-        ]
-        high, low = halves(jnp.concatenate(stack, axis=0))
-        wide = dot(w_both, high)
-        result = wide[:rank] + wide[rank:] + dot(w_high, low)
-        out_ref[:, x * slab:(x + 1) * slab] = result
-        results.append(result)
-    write_layers(results, dims, layer_refs)
-
-
-def galerkin_kernel(dims, k_ref, xa_ref, ya_ref, mean_ref, out_ref):
+        line_before = roll(layer_before, -lz * x) if x < lx else corners
+        line_after = roll(layer, -lz * (x + 1)) if x < lx else corner_after
+        results.append(product([
+            fields[x], g, flux[x - 1], flux[x + 1],
+            y_behind(g, line_before, dims), y_ahead(g, line_after, dims), z_behind(g, dims), z_ahead(g, dims),
+        ]))
+    if further is None:
+        return results
+    lane = lane_index(width)
+    side = product([
+        ya, layer,
+        jnp.where(lane < lz, roll(corner_before, lz), roll(layer, lz)),
+        jnp.where(lane >= width - lz, corner_after, roll(layer, -lz)),
+        y_layer(flux[:lx], dims, ly - 1), layer_next, z_behind(layer, dims), z_ahead(layer, dims),
+    ])
+    return results, side
+
+
+def galerkin(dims, fields, layer, mean):
     lx, ly, lz = dims
-    mean = mean_ref[...]
     rank = mean.shape[0]
-    fields = slabs_of(k_ref[...], dims)
-    after, layer = xa_ref[...], ya_ref[...]
-    speeds = [speed_of(mean, f) for f in fields] + [speed_of(mean, after)]
+    speeds = [speed_of(mean, f) for f in fields]
     sums = [jnp.zeros((rank, 2 * rank), jnp.float32) for _ in range(4)]
     for x in range(lx):
         k = fields[x]
         q = speeds[x] * k
-        pairs = [(k, k)]
-        moved = fields[x + 1] if x < lx - 1 else after
-        pairs.append((moved, speeds[x + 1] * k))
-        for moved in (y_ahead(k, layer, x, dims), z_ahead(k, dims)):
+        pairs = [(k, k), (fields[x + 1], speeds[x + 1] * k)]
+        for moved in (y_ahead(k, roll(layer, -lz * (x + 1)), dims), z_ahead(k, dims)):
             pairs.append((moved, speed_of(mean, moved) * k))
         for n, (left, right) in enumerate(pairs):
             sums[n] = sums[n] + three(left, jnp.concatenate([right, q], axis=0), (1, 1))
-    for n in range(4):
-        out_ref[n * rank:(n + 1) * rank] = sums[n]
+    return jnp.concatenate(sums, axis=0)
+
+
+def write_slabs(ref, slabs):
+    slab = slabs[0].shape[1]
+    for x, value in enumerate(slabs):
+        ref[:, x * slab:(x + 1) * slab] = value
+
+
+def first_kernel(
+    dims, field_ref, xb, xa, yb, ya, weight_ref, column_ref, out_ref, first_ref, y_first_ref, y_last_ref
+):
+    slabs = k_stage(
+        dims, field_ref[...], weight_ref[...], column_ref[...], xb[...], xa[...], yb[...], ya[...]
+    )
+    write_slabs(out_ref, slabs)
+    first_ref[...] = slabs[0]
+    y_first_ref[...], y_last_ref[...] = y_layer(slabs, dims, 0), y_layer(slabs, dims, dims[1] - 1)
+
+
+def galerkin_kernel(dims, field_ref, xa, ya, yb, mean_ref, sums_ref, down_ref, up_ref, next_ref):
+    lx, ly, lz = dims
+    slab, width = ly * lz, lx * lz
+    slabs = slabs_of(field_ref[...], dims)
+    layer = ya[...]
+    sums_ref[...] = galerkin(dims, slabs + [xa[...]], layer, mean_ref[...])
+    down_ref[:, :slab] = slabs[1]
+    down_ref[:, slab:] = jnp.where(lane_index(width) < lz, yb[...], roll(layer, lz))
+    up_ref[:, :slab] = slabs[-1]
+    up_ref[:, slab:] = layer
+    next_ref[...] = y_layer(slabs, dims, 1)
 
 
 def orient_stage(cells, sums, orient, table, mean, directions):
@@ -297,7 +356,9 @@
     return inverse, upper_v, three(inverse_v, new, (1, 0))
 
 
-def turn_kernel(cells, sums_ref, orient_ref, table_ref, mean_ref, e_ref, orient_out, table_out, mean_out, weight_ref, column_ref):
+def turn_kernel(
+    cells, sums_ref, orient_ref, table_ref, mean_ref, e_ref, orient_out, table_out, mean_out, weight_ref, column_ref
+):
     directions = e_ref[...]
     inverse, upper_v, orient = orient_stage(cells, sums_ref[...], orient_ref[...], table_ref[...], mean_ref[...], directions)
     orient_out[...] = orient
@@ -306,6 +367,18 @@
     mean_out[...] = mean
     weights, column_ref[...] = stage_weights(table, mean, mm(upper_v, inverse))
     weight_ref[...] = flat_weights(weights)
+
+
+def second_kernel(
+    dims, field_ref, xa, ya, yb, second, behind, after, weight_ref, column_ref, mean_ref, field_out, sums_out
+):
+    slab = dims[1] * dims[2]
+    slabs, side = k_stage(
+        dims, field_ref[...], weight_ref[...], column_ref[...], behind[:, :slab], xa[...], yb[...], ya[...],
+        (second[...], behind[:, slab:], after[...]),
+    )
+    write_slabs(field_out, slabs[:-1])
+    sums_out[...] = galerkin(dims, slabs, side, mean_ref[...])
 
 
 def last_kernel(cells, sums_ref, orient_ref, table_ref, mean_ref, e_ref, field_ref, x_ref, s_ref, v_ref):
@@ -333,53 +406,49 @@
     return every.reshape(padded, width)[:rows]
 
 
-def ahead(layers):
-    return (
-        lax.ppermute(layers[0], "gx", shifted("gx", False)),
-        lax.ppermute(layers[2], "gy", shifted("gy", False)),
-    )
-
-
-def behind(layers):
-    return (
-        lax.ppermute(layers[1], "gx", shifted("gx", True)),
-        lax.ppermute(layers[3], "gy", shifted("gy", True)),
-    )
+def up(value, axis):
+    return lax.ppermute(value, axis, shifted(axis, True))
+
+
+def down(value, axis):
+    return lax.ppermute(value, axis, shifted(axis, False))
 
 
 def shards(spatial_factor, coupling, orient_factor, directions):
     dims = spatial_factor.shape[:3]
+    lx, ly, lz = dims
     rank = spatial_factor.shape[-1]
-    sites = dims[0] * dims[1] * dims[2]
+    sites = lx * ly * lz
     count = orient_factor.shape[0]
     cells = sites * lax.axis_size("gx") * lax.axis_size("gy")
-    layers = layer_shapes(rank, dims)
-    stage = [(rank, count), (6 * rank, rank), (rank, 1), (rank, 8 * rank), (rank, 1)]
-    field, *edges = call(
-        functools.partial(enter_kernel, dims), [(rank, sites)] + layers, spatial_factor.reshape(sites, rank)
-    )
-    x_after, y_after = ahead(edges)
-    x_before, y_before = behind(edges)
+    whole, slab, layer = (rank, sites), (rank, ly * lz), (rank, lx * lz)
+    more = (rank, ly * lz + lx * lz)
+    summed = (4 * rank, 2 * rank)
+    basis = [(rank, count), (6 * rank, rank), (rank, 1)]
+    field, first, last, y_first, y_last = call(
+        functools.partial(enter_kernel, dims), [whole, slab, slab, layer, layer], spatial_factor.reshape(sites, rank)
+    )
+    xb, xa, yb, ya = up(last, "gx"), down(first, "gx"), up(y_last, "gy"), down(y_first, "gy")
+    stage = basis + [(rank, 8 * rank), (rank, 1)]
     orient, table, mean, weights, column = call(table_kernel, stage, orient_factor, directions, coupling)
-    for step in range(STEPS):
-        field, *edges = call(
-            functools.partial(k_kernel, dims), [(rank, sites)] + layers,
-            field, x_before, x_after, y_before, y_after, weights, column,
-        )
-        x_after, y_after = ahead(edges)
-        if step < STEPS - 1:
-            x_before, y_before = behind(edges)
-        (part,) = call(
-            functools.partial(galerkin_kernel, dims), [(4 * rank, 2 * rank)], field, x_after, y_after, mean
-        )
-        sums = all_sum(part)
-        if step < STEPS - 1:
-            orient, table, mean, weights, column = call(
-                functools.partial(turn_kernel, cells), stage, sums, orient, table, mean, directions
-            )
+    field, first, y_first, y_last = call(
+        functools.partial(first_kernel, dims), [whole, slab, layer, layer], field, xb, xa, yb, ya, weights, column
+    )
+    xa, ya, yb = down(first, "gx"), down(y_first, "gy"), up(y_last, "gy")
+    part, second, behind, after = call(
+        functools.partial(galerkin_kernel, dims), [summed, more, more, layer], field, xa, ya, yb, mean
+    )
+    second, behind, after = down(second, "gx"), up(behind, "gx"), down(after, "gy")
+    orient, table, mean, weights, column = call(
+        functools.partial(turn_kernel, cells), stage, all_sum(part), orient, table, mean, directions
+    )
+    field, part = call(
+        functools.partial(second_kernel, dims), [whole, summed],
+        field, xa, ya, yb, second, behind, after, weights, column, mean,
+    )
     new_spatial, new_coupling, new_orient = call(
         functools.partial(last_kernel, cells), [(sites, rank), (rank, rank), (count, rank)],
-        sums, orient, table, mean, directions, field,
+        all_sum(part), orient, table, mean, directions, field,
     )
     return new_spatial.reshape(spatial_factor.shape), new_coupling, new_orient
 

time: 108 us -> 88.2 us (0.82)
  Pallas kernels: 39.5 us -> 26 us
  waiting for transfers between devices: 13.6 us -> 8.5 us
  blocking collectives: 33.2 us -> 29.6 us
  starting transfers between devices: 17.1 us -> 19.6 us
    pallas_call x8 -> x7, Pallas kernels: 39.5 us -> 26 us  [call(): pl.pallas_call(body, out_shape=[jax.ShapeDtypeStruct(shape, jnp.float32)...]
    all_to_all x1, waiting for transfers between devices: 6.48 us -> 2.62 us  [all_sum(): lax.all_to_all(jnp.broadcast_to(mine[None], split.shape), ('gx', 'gy'), 0...]
    all_to_all x2, blocking collectives: 23.3 us -> 19.8 us  [all_sum(): mine = lax.all_to_all(split, ('gx', 'gy'), 0, 0).sum(axis=0)]
    ppermute x10, starting transfers between devices: 14.5 us -> 17.1 us  [the longest x6 14.1 us: down(): return lax.ppermute(value, axis, shifted(axis, False))]
    ppermute x10, waiting for transfers between devices: 7.09 us -> 5.88 us  [the longest x4 3.55 us: up(): return lax.ppermute(value, axis, shifted(axis, True))]
  transfers between devices with their start and end apart: 11 -> 11, of which waited for: 5 -> 4; matrix products, arithmetic and copies ran while one was open for 0% -> 0% of each run, Pallas kernels for 16% -> 12%
where the time goes in v1:
time: 88.2 us; the launch traced here: 87.9 us
  blocking collectives  29.6 us (34%)
  Pallas kernels  26 us (29%)
  starting transfers between devices  19.6 us (22%)
  waiting for transfers between devices  8.5 us (10%)
  local copies, waits for them, and re-layouts  3.35 us (4%)
    pallas_call x7, Pallas kernels, call(): pl.pallas_call(body, out_shape=[jax.ShapeDtypeStruct(shape, jnp.float32)...  26 us
    all_to_all x2, blocking collectives, all_sum(): mine = lax.all_to_all(split, ('gx', 'gy'), 0, 0).sum(axis=0)  19.8 us
    ppermute x6, starting transfers between devices, down(): return lax.ppermute(value, axis, shifted(axis, False))  14.1 us
    all_to_all x1, blocking collectives, all_sum(): lax.all_to_all(jnp.broadcast_to(mine[None], split.shape), ('gx', 'gy'), 0...  9.88 us
    ppermute x4, waiting for transfers between devices, up(): return lax.ppermute(value, axis, shifted(axis, True))  3.55 us
    ppermute x4, starting transfers between devices, up(): return lax.ppermute(value, axis, shifted(axis, True))  3 us
    unnamed x10, local copies, waits for them, and re-layouts  2.67 us
    all_to_all x1, waiting for transfers between devices, all_sum(): lax.all_to_all(jnp.broadcast_to(mine[None], split.shape), ('gx', 'gy'), 0...  2.62 us
  transfers between devices with their start and end apart: 11, of which 4 were waited for; matrix products, arithmetic and copies ran while one was open for 0% of the time, Pallas kernels for 12%

profile of v1, /device:TPU:0, one launch (start us, length us, event | category | flops | bytes accessed | tf_op | source)
XLA Modules:
  0.0 87.9 jit_solution(6252698560520575956)
XLA Ops:
  0.6 1.2 %copy-done = f32[4,16,32,64]{3,2,1,0:T(8,128)S(1)} copy-done((f32[4,16,32,64]{3,2,1,0:T(8,128)S(1)}, f32[4,16,32,64]{3,2,1,0:T(8,128)}, u32[]{:S(2)}) %copy-start) | copy-done | bytes 524312
  2.3 3.0 %collective-permute-start = (f32[64,512]{1,0:T(8,128)S(1)}, f32[64,512]{1,0:T(8,128)S(1)}, u32[]{:S(2)}, u32[]{:S(2)}) collective-permute-start(f32[64,512]{1,0:T(8,128)S(1)} %get-tuple-element.32), channel_id=1, source_target_pairs={{0,8},{8,16},{16,24},{24,0},{1,9},{9,17},{17,25},{25,1},{2,10},{10... | collective-permute-start | bytes 393224 | tf_op jit(solution)/shard_map/ppermute | solution.py:410
  5.3 1.0 %collective-permute-start.1 = (f32[64,512]{1,0:T(8,128)S(1)}, f32[64,512]{1,0:T(8,128)S(1)}, u32[]{:S(2)}, u32[]{:S(2)}) collective-permute-start(f32[64,512]{1,0:T(8,128)S(1)} %get-tuple-element.33), channel_id=1, source_target_pairs={{0,24},{8,0},{16,8},{24,16},{1,25},{9,1},{17,9},{25,17},{2,26},{10... | collective-permute-start | bytes 393224 | tf_op jit(solution)/shard_map/ppermute | solution.py:414
  6.3 3.5 %collective-permute-start.3 = (f32[64,128]{1,0:T(8,128)S(1)}, f32[64,128]{1,0:T(8,128)S(1)}, u32[]{:S(2)}, u32[]{:S(2)}) collective-permute-start(f32[64,128]{1,0:T(8,128)S(1)} %get-tuple-element.35), channel_id=1, source_target_pairs={{0,7},{1,0},{2,1},{3,2},{4,3},{5,4},{6,5},{7,6},{8,15},{9,8},{10,9... | collective-permute-start | bytes 98312 | tf_op jit(solution)/shard_map/ppermute | solution.py:414
  10.2 1.8 %shard_map.68 = (f32[64,2048]{1,0:T(8,128)S(1)}, f32[384,64]{1,0:T(8,128)S(1)}, f32[64,1]{1,0:T(8,128)S(1)}, f32[64,512]{1,0:T(8,128)S(1)}, f32[64,1]{1,0:T(8,128)S(1)}) custom-call(f32[2048,64]{1,0:T(8,128)S(1)} %copy.7.v_ref, f32[3,2048]{1,0:T(4,128)S(1)} %copy-done.1, f32[64,64]{1,0:T(8,128)S(1)} %copy-done.2), custom_call_target="tpu_custom_call" | custom-call | tf_op jit(solution)/shard_map/pallas_call | solution.py:202
  12.0 0.7 collective-permute-done.1.xa
  12.8 1.4 %shard_map.69 = (f32[64,2048]{1,0:T(8,128)S(1)}, f32[64,512]{1,0:T(8,128)S(1)}, f32[64,128]{1,0:T(8,128)S(1)}, f32[64,128]{1,0:T(8,128)S(1)}) custom-call(f32[64,2048]{1,0:T(8,128)S(1)} %get-tuple-element.31.field_ref, f32[64,512]{1,0:T(8,128)S(1)} %collective-permute-done.xb, f32[64,512]{1,0:T(8,128)S(1)} %collective-permute-done.1.xa, ...), custom_call_target="tpu_custom_call" | custom-call | tf_op jit(solution)/shard_map/pallas_call | solution.py:202
  14.2 1.5 %collective-permute-start.4 = (f32[64,512]{1,0:T(8,128)S(1)}, f32[64,512]{1,0:T(8,128)S(1)}, u32[]{:S(2)}, u32[]{:S(2)}) collective-permute-start(f32[64,512]{1,0:T(8,128)S(1)} %get-tuple-element.39), channel_id=1, source_target_pairs={{0,24},{8,0},{16,8},{24,16},{1,25},{9,1},{17,9},{25,17},{2,26},{10... | collective-permute-start | bytes 393224 | tf_op jit(solution)/shard_map/ppermute | solution.py:414
  15.7 2.4 %collective-permute-start.5 = (f32[64,128]{1,0:T(8,128)S(1)}, f32[64,128]{1,0:T(8,128)S(1)}, u32[]{:S(2)}, u32[]{:S(2)}) collective-permute-start(f32[64,128]{1,0:T(8,128)S(1)} %get-tuple-element.40), channel_id=1, source_target_pairs={{0,7},{1,0},{2,1},{3,2},{4,3},{5,4},{6,5},{7,6},{8,15},{9,8},{10,9... | collective-permute-start | bytes 98312 | tf_op jit(solution)/shard_map/ppermute | solution.py:414
  18.1 1.6 %collective-permute-done.5.ya = f32[64,128]{1,0:T(8,128)S(1)} collective-permute-done((f32[64,128]{1,0:T(8,128)S(1)}, f32[64,128]{1,0:T(8,128)S(1)}, u32[]{:S(2)}, u32[]{:S(2)}) %collective-permute-start.5) | collective-permute-done | bytes 32800 | tf_op jit(solution)/shard_map/ppermute | solution.py:414
  19.7 3.5 %collective-permute-done.6.yb = f32[64,128]{1,0:T(8,128)S(1)} collective-permute-done((f32[64,128]{1,0:T(8,128)S(1)}, f32[64,128]{1,0:T(8,128)S(1)}, u32[]{:S(2)}, u32[]{:S(2)}) %collective-permute-start.6) | collective-permute-done | bytes 32800 | tf_op jit(solution)/shard_map/ppermute | solution.py:410
  23.2 1.4 %shard_map.70 = (f32[256,128]{1,0:T(8,128)S(1)}, f32[64,640]{1,0:T(8,128)S(1)}, f32[64,640]{1,0:T(8,128)S(1)}, f32[64,128]{1,0:T(8,128)S(1)}) custom-call(f32[64,2048]{1,0:T(8,128)S(1)} %get-tuple-element.38.field_ref, f32[64,512]{1,0:T(8,128)S(1)} %collective-permute-done.4.xa, f32[64,128]{1,0:T(8,128)S(1)} %collective-permute-done.5.ya, ...), custom_call_target="tpu_custom_call" | custom-call | tf_op jit(solution)/shard_map/pallas_call | solution.py:202
  24.7 9.9 %all_to_all.20 = f32[32,8,128]{2,1,0:T(8,128)S(1)} all-to-all(f32[32,8,128]{2,1,0:T(8,128)S(1)} %bitcast.10), channel_id=1, replica_groups=mesh['gx'=4,'gy'=8] {'gx','gy'}, dimensions={0} | all-to-all | bytes 262144 | tf_op jit(solution)/shard_map/all_to_all | solution.py:404
  34.6 0.7 broadcast_in_dim.4
  35.2 2.6 %all-to-all-start.1 = ((f32[32,8,128]{2,1,0:T(8,128)}), f32[32,8,128]{2,1,0:T(8,128)S(1)}, u32[]{:S(2)}, u32[]{:S(2)}) async-start(f32[32,8,128]{2,1,0:T(8,128)} %broadcast_in_dim.4), calls=%async_computation.1 | async-start | bytes 262144 | tf_op jit(solution)/shard_map/all_to_all | solution.py:405
  37.8 2.6 %collective-permute-start.7 = (f32[64,640]{1,0:T(8,128)S(1)}, f32[64,640]{1,0:T(8,128)S(1)}, u32[]{:S(2)}, u32[]{:S(2)}) collective-permute-start(f32[64,640]{1,0:T(8,128)S(1)} %get-tuple-element.43), channel_id=1, source_target_pairs={{0,24},{8,0},{16,8},{24,16},{1,25},{9,1},{17,9},{25,17},{2,26},{10... | collective-permute-start | bytes 491528 | tf_op jit(solution)/shard_map/ppermute | solution.py:414
  40.4 2.9 %collective-permute-start.9 = (f32[64,128]{1,0:T(8,128)S(1)}, f32[64,128]{1,0:T(8,128)S(1)}, u32[]{:S(2)}, u32[]{:S(2)}) collective-permute-start(f32[64,128]{1,0:T(8,128)S(1)} %get-tuple-element.45), channel_id=1, source_target_pairs={{0,7},{1,0},{2,1},{3,2},{4,3},{5,4},{6,5},{7,6},{8,15},{9,8},{10,9... | collective-permute-start | bytes 98312 | tf_op jit(solution)/shard_map/ppermute | solution.py:414
  43.4 2.6 %all-to-all-done.1 = f32[32,8,128]{2,1,0:T(8,128)S(1)} async-done(((f32[32,8,128]{2,1,0:T(8,128)}), f32[32,8,128]{2,1,0:T(8,128)S(1)}, u32[]{:S(2)}, u32[]{:S(2)}) %all-to-all-start.1) | async-done | bytes 131104 | tf_op jit(solution)/shard_map/all_to_all | solution.py:405
  46.0 9.0 %shard_map.71 = (f32[64,2048]{1,0:T(8,128)S(1)}, f32[384,64]{1,0:T(8,128)S(1)}, f32[64,1]{1,0:T(8,128)S(1)}, f32[64,512]{1,0:T(8,128)S(1)}, f32[64,1]{1,0:T(8,128)S(1)}) custom-call(f32[256,128]{1,0:T(8,128)S(1)} %bitcast.7, f32[64,2048]{1,0:T(8,128)S(1)} %get-tuple-element.47.orient_ref, f32[384,64]{1,0:T(8,128)S(1)} %get-tuple-element.48.table_ref, ...), custom_call_target="tpu_custom_call" | custom-call | tf_op jit(solution)/shard_map/pallas_call | solution.py:202
  55.1 3.3 %shard_map.72 = (f32[64,2048]{1,0:T(8,128)S(1)}, f32[256,128]{1,0:T(8,128)S(1)}) custom-call(f32[64,2048]{1,0:T(8,128)S(1)} %get-tuple-element.38.field_ref, f32[64,512]{1,0:T(8,128)S(1)} %collective-permute-done.4.xa, f32[64,128]{1,0:T(8,128)S(1)} %collective-permute-done.5.ya, f32[64,128]{1,0:T(8,128)S(1)} %collective-permute-done.6.yb, ...), custom_call_target="tpu_custom_call" | custom-call | tf_op jit(solution)/shard_map/pallas_call | solution.py:202
  58.4 9.9 %all_to_all.21 = f32[32,8,128]{2,1,0:T(8,128)S(1)} all-to-all(f32[32,8,128]{2,1,0:T(8,128)S(1)} %bitcast.9), channel_id=1, replica_groups=mesh['gx'=4,'gy'=8] {'gx','gy'}, dimensions={0} | all-to-all | bytes 262144 | tf_op jit(solution)/shard_map/all_to_all | solution.py:404
  68.3 9.9 %all_to_all.22 = f32[32,8,128]{2,1,0:T(8,128)S(1)} all-to-all(f32[32,8,128]{2,1,0:T(8,128)S(1)} %broadcast_in_dim.5), channel_id=1, replica_groups=mesh['gx'=4,'gy'=8] {'gx','gy'}, dimensions={0} | all-to-all | bytes 262144 | tf_op jit(solution)/shard_map/all_to_all | solution.py:405
  78.2 8.6 %shard_map.73 = (f32[2048,64]{1,0:T(8,128)}, f32[64,64]{1,0:T(8,128)}, f32[2048,64]{1,0:T(8,128)S(1)}) custom-call(f32[256,128]{1,0:T(8,128)S(1)} %bitcast.8, f32[64,2048]{1,0:T(8,128)S(1)} %get-tuple-element.53.orient_ref, f32[384,64]{1,0:T(8,128)S(1)} %get-tuple-element.54.table_ref, f32[64,1]{1,0:T(8,128)S(1)} %get-tuple-element.51.mean_ref, ...), custom_call_target="tpu_custom_call" | custom-call | tf_op jit(solution)/shard_map/pallas_call | solution.py:202
  86.8 1.1 %copy.8 = f32[2048,64]{0,1:T(8,128)} copy(f32[2048,64]{1,0:T(8,128)S(1)} %get-tuple-element.61) | data formatting | bytes 1048576
  (22 shorter events, 0.9 us)
Async XLA Ops:
  0.6 1.2 %copy-start = (f32[4,16,32,64]{3,2,1,0:T(8,128)S(1)}, f32[4,16,32,64]{3,2,1,0:T(8,128)}, u32[]{:S(2)}) copy-start(f32[4,16,32,64]{3,2,1,0:T(8,128)} %param.4) | copy-start | bytes 1572868
  1.9 8.0 %copy-start.3 = (f32[2048,64]{0,1:T(8,128)S(1)}, f32[2048,64]{0,1:T(8,128)}, u32[]{:S(2)}) copy-start(f32[2048,64]{0,1:T(8,128)} %param.6) | copy-start | bytes 1572868
  2.3 9.8 %collective-permute-start = (f32[64,512]{1,0:T(8,128)S(1)}, f32[64,512]{1,0:T(8,128)S(1)}, u32[]{:S(2)}, u32[]{:S(2)}) collective-permute-start(f32[64,512]{1,0:T(8,128)S(1)} %get-tuple-element.32), channel_id=1, source_target_pairs={{0,8},{8,16},{16,24},{24,0},{1,9},{9,17},{17,25},{25,1},{2,10},{10... | collective-permute-start | bytes 393224 | tf_op jit(solution)/shard_map/ppermute | solution.py:410
  5.3 7.5 %collective-permute-start.1 = (f32[64,512]{1,0:T(8,128)S(1)}, f32[64,512]{1,0:T(8,128)S(1)}, u32[]{:S(2)}, u32[]{:S(2)}) collective-permute-start(f32[64,512]{1,0:T(8,128)S(1)} %get-tuple-element.33), channel_id=1, source_target_pairs={{0,24},{8,0},{16,8},{24,16},{1,25},{9,1},{17,9},{25,17},{2,26},{10... | collective-permute-start | bytes 393224 | tf_op jit(solution)/shard_map/ppermute | solution.py:414
  6.3 5.7 %collective-permute-start.2 = (f32[64,128]{1,0:T(8,128)S(1)}, f32[64,128]{1,0:T(8,128)S(1)}, u32[]{:S(2)}, u32[]{:S(2)}) collective-permute-start(f32[64,128]{1,0:T(8,128)S(1)} %get-tuple-element.34), channel_id=1, source_target_pairs={{0,1},{1,2},{2,3},{3,4},{4,5},{5,6},{6,7},{7,0},{8,9},{9,10},{10,1... | collective-permute-start | bytes 98312 | tf_op jit(solution)/shard_map/ppermute | solution.py:410
  6.3 3.9 %copy-start.1 = (f32[3,2048]{1,0:T(4,128)S(1)}, f32[3,2048]{1,0:T(4,128)}, u32[]{:S(2)}) copy-start(f32[3,2048]{1,0:T(4,128)} %e_ref.5) | copy-start | bytes 73732
  6.3 3.9 %copy-start.2 = (f32[64,64]{1,0:T(8,128)S(1)}, f32[64,64]{1,0:T(8,128)}, u32[]{:S(2)}) copy-start(f32[64,64]{1,0:T(8,128)} %s_ref.1) | copy-start | bytes 49156
  6.3 5.7 %collective-permute-start.3 = (f32[64,128]{1,0:T(8,128)S(1)}, f32[64,128]{1,0:T(8,128)S(1)}, u32[]{:S(2)}, u32[]{:S(2)}) collective-permute-start(f32[64,128]{1,0:T(8,128)S(1)} %get-tuple-element.35), channel_id=1, source_target_pairs={{0,7},{1,0},{2,1},{3,2},{4,3},{5,4},{6,5},{7,6},{8,15},{9,8},{10,9... | collective-permute-start | bytes 98312 | tf_op jit(solution)/shard_map/ppermute | solution.py:414
  14.2 9.1 %collective-permute-start.4 = (f32[64,512]{1,0:T(8,128)S(1)}, f32[64,512]{1,0:T(8,128)S(1)}, u32[]{:S(2)}, u32[]{:S(2)}) collective-permute-start(f32[64,512]{1,0:T(8,128)S(1)} %get-tuple-element.39), channel_id=1, source_target_pairs={{0,24},{8,0},{16,8},{24,16},{1,25},{9,1},{17,9},{25,17},{2,26},{10... | collective-permute-start | bytes 393224 | tf_op jit(solution)/shard_map/ppermute | solution.py:414
  15.7 4.0 %collective-permute-start.5 = (f32[64,128]{1,0:T(8,128)S(1)}, f32[64,128]{1,0:T(8,128)S(1)}, u32[]{:S(2)}, u32[]{:S(2)}) collective-permute-start(f32[64,128]{1,0:T(8,128)S(1)} %get-tuple-element.40), channel_id=1, source_target_pairs={{0,7},{1,0},{2,1},{3,2},{4,3},{5,4},{6,5},{7,6},{8,15},{9,8},{10,9... | collective-permute-start | bytes 98312 | tf_op jit(solution)/shard_map/ppermute | solution.py:414
  18.1 5.1 %collective-permute-start.6 = (f32[64,128]{1,0:T(8,128)S(1)}, f32[64,128]{1,0:T(8,128)S(1)}, u32[]{:S(2)}, u32[]{:S(2)}) collective-permute-start(f32[64,128]{1,0:T(8,128)S(1)} %get-tuple-element.41), channel_id=1, source_target_pairs={{0,1},{1,2},{2,3},{3,4},{4,5},{5,6},{6,7},{7,0},{8,9},{9,10},{10,1... | collective-permute-start | bytes 98312 | tf_op jit(solution)/shard_map/ppermute | solution.py:410
  35.2 10.8 %all-to-all-start.1 = ((f32[32,8,128]{2,1,0:T(8,128)}), f32[32,8,128]{2,1,0:T(8,128)S(1)}, u32[]{:S(2)}, u32[]{:S(2)}) async-start(f32[32,8,128]{2,1,0:T(8,128)} %broadcast_in_dim.4), calls=%async_computation.1 | async-start | bytes 262144 | tf_op jit(solution)/shard_map/all_to_all | solution.py:405
  37.8 17.2 %collective-permute-start.7 = (f32[64,640]{1,0:T(8,128)S(1)}, f32[64,640]{1,0:T(8,128)S(1)}, u32[]{:S(2)}, u32[]{:S(2)}) collective-permute-start(f32[64,640]{1,0:T(8,128)S(1)} %get-tuple-element.43), channel_id=1, source_target_pairs={{0,24},{8,0},{16,8},{24,16},{1,25},{9,1},{17,9},{25,17},{2,26},{10... | collective-permute-start | bytes 491528 | tf_op jit(solution)/shard_map/ppermute | solution.py:414
  40.4 14.6 %collective-permute-start.8 = (f32[64,640]{1,0:T(8,128)S(1)}, f32[64,640]{1,0:T(8,128)S(1)}, u32[]{:S(2)}, u32[]{:S(2)}) collective-permute-start(f32[64,640]{1,0:T(8,128)S(1)} %get-tuple-element.44), channel_id=1, source_target_pairs={{0,8},{8,16},{16,24},{24,0},{1,9},{9,17},{17,25},{25,1},{2,10},{10... | collective-permute-start | bytes 491528 | tf_op jit(solution)/shard_map/ppermute | solution.py:410
  40.4 14.6 %collective-permute-start.9 = (f32[64,128]{1,0:T(8,128)S(1)}, f32[64,128]{1,0:T(8,128)S(1)}, u32[]{:S(2)}, u32[]{:S(2)}) collective-permute-start(f32[64,128]{1,0:T(8,128)S(1)} %get-tuple-element.45), channel_id=1, source_target_pairs={{0,7},{1,0},{2,1},{3,2},{4,3},{5,4},{6,5},{7,6},{8,15},{9,8},{10,9... | collective-permute-start | bytes 98312 | tf_op jit(solution)/shard_map/ppermute | solution.py:414

commit v2 on v1

--- a/solution.py
+++ b/solution.py
@@ -114,9 +114,13 @@
     both = jnp.concatenate([high, low], axis=0)
     stack = [orient * part[d:d + 1] for d in range(3) for part in (plus, minus)]
     stack_high, stack_low = halves(jnp.concatenate(stack, axis=0))
-    wide = dot(stack_high, both, (1, 1))
-    summed = (wide[:, :rank] + wide[:, rank:] + dot(stack_low, high, (1, 1))) * (1.0 / count)
-    return summed, jnp.sum(orient, axis=1, keepdims=True) * (1.0 / count)
+    scale = 1.0 / count
+
+    def product(left_high, left_low):
+        wide = dot(left_high, both, (1, 1))
+        return (wide[:, :rank] + wide[:, rank:] + dot(left_low, high, (1, 1))) * scale
+
+    return product(high, low), product(stack_high, stack_low), jnp.sum(orient, axis=1, keepdims=True) * scale
 
 
 def unit(rank):
@@ -125,18 +129,18 @@
     return jnp.where(row == col, 1.0, 0.0).astype(jnp.float32)
 
 
-def stage_weights(table, mean, into):
+def stage_weights(gram, table, mean, into):
     rank = mean.shape[0]
     blocks = [table[d * rank:(d + 1) * rank] for d in range(6)]
     total = blocks[0] + blocks[1] + blocks[2] + blocks[3] + blocks[4] + blocks[5]
     spread = jnp.broadcast_to(mean, (rank, rank))
-    first = (1.0 - tumble) * unit(rank) + tumble * spread * spread.T
-    stack = jnp.concatenate([first, -courant * total, courant * table], axis=0)
-    column = mm(into, spread, (0, 0))[:, :1]
-    return mm(stack, into), column
-
-
-def factor(gram):
+    first = (1.0 - tumble) * gram + tumble * spread * spread.T
+    weights = mm(jnp.concatenate([first, -courant * total, courant * table], axis=0), into)
+    weights = jnp.concatenate([weights[b * rank:(b + 1) * rank] for b in range(8)], axis=1)
+    return weights, mm(into, spread, (0, 0))[:, :1]
+
+
+def factor(gram, beside=None, meanwhile=()):
     rank = gram.shape[0]
     group = 8
     shape = (group, 2 * rank)
@@ -144,14 +148,17 @@
     diag_row = jnp.sum(eye * gram, axis=0, keepdims=True)
     diag_column = jnp.sum(eye * gram, axis=1, keepdims=True)
     scale = lax.rsqrt(diag_row)
-    wide = jnp.concatenate([gram * lax.rsqrt(diag_column) * scale, eye], axis=1)
+    scale_column = lax.rsqrt(diag_column)
+    wide = jnp.concatenate([gram * scale_column * scale, eye], axis=1)
     blocks = rank // group
-    rows = [wide[b * group:(b + 1) * group] for b in range(blocks)]
+    fields = [wide] if beside is None else [wide, beside * scale_column]
+    fields = [[f[b * group:(b + 1) * group] for b in range(blocks)] for f in fields]
+    rows = fields[0]
     place = lax.broadcasted_iota(jnp.int32, shape, 0)
     lane = lax.broadcasted_iota(jnp.int32, shape, 1)
 
     def spread(value, i):
-        return jnp.broadcast_to(value[i:i + 1], shape)
+        return jnp.broadcast_to(value[i:i + 1], value.shape)
 
     for b in range(blocks):
         start = b * group
@@ -166,11 +173,15 @@
             p, o, q = p * over, o * over, q * over
 
             def solve(value):
+                width = value.shape[1]
                 upper, lower = spread(value, j), spread(value, j + 1)
-                return q * upper - o * lower, p * lower - o * upper
+                return (
+                    q[:, :width] * upper - o[:, :width] * lower,
+                    p[:, :width] * lower - o[:, :width] * upper,
+                )
 
             later = [solve(cols[b][n]) for n in range(j + 2, group)]
-            row_first, row_second = solve(rows[b])
+            pivots = [solve(f[b]) for f in fields]
             for c in range(b, blocks):
                 left, right = cols[c][j], cols[c][j + 1]
                 if c == b:
@@ -179,31 +190,37 @@
                     left, right = jnp.where(place > j + 1, left, 0.0), jnp.where(place > j + 1, right, 0.0)
                 for n, (up, low) in enumerate(later):
                     cols[c][j + 2 + n] = cols[c][j + 2 + n] - left * up - right * low
-                rows[c] = rows[c] - left * row_first - right * row_second
-    done = []
+                for f, (up, low) in zip(fields, pivots):
+                    width = up.shape[1]
+                    f[c] = f[c] - left[:, :width] * up - right[:, :width] * low
+        if b < len(meanwhile):
+            meanwhile[b]()
+    done = [[] for _ in fields]
     for b, block in enumerate(rows):
         at = place + b * group
         pivot = jnp.sum(jnp.where(lane == at, block, 0.0), axis=1, keepdims=True)
-        beside = jnp.sum(jnp.where((lane == at - 1) & (place % 2 == 1), block, 0.0), axis=1, keepdims=True)
+        under = jnp.sum(jnp.where((lane == at - 1) & (place % 2 == 1), block, 0.0), axis=1, keepdims=True)
         pivot = jnp.broadcast_to(pivot, shape)
-        part = beside / pltpu.roll(pivot, 1, axis=0)
-        block = block - part * pltpu.roll(block, 1, axis=0)
-        done.append(block * lax.rsqrt(pivot - part * beside))
-    done = jnp.concatenate(done, axis=0) * jnp.concatenate([diag_row * scale, scale], axis=1)
-    return done[:, :rank], done[:, rank:]
-
-
-def flat_weights(weights):
-    rank = weights.shape[1]
-    return jnp.concatenate([weights[b * rank:(b + 1) * rank] for b in range(weights.shape[0] // rank)], axis=1)
-
-
-def call(body, outs, *args):
+        part = under / pltpu.roll(pivot, 1, axis=0)
+        root = lax.rsqrt(pivot - part * under)
+        for f, out in zip(fields, done):
+            width = f[b].shape[1]
+            out.append((f[b] - part[:, :width] * pltpu.roll(f[b], 1, axis=0)) * root[:, :width])
+    done = [jnp.concatenate(d, axis=0) for d in done]
+    both = done[0] * jnp.concatenate([diag_row * scale, scale], axis=1)
+    return (both[:, :rank], both[:, rank:], *done[1:])
+
+
+def call(body, outs, *args, far_out=(), scratch=()):
+    def space(n, far):
+        return pl.BlockSpec(memory_space=pltpu.HBM if n in far else pltpu.VMEM)
+
     return pl.pallas_call(
         body,
         out_shape=[jax.ShapeDtypeStruct(shape, jnp.float32) for shape in outs],
         in_specs=[pl.BlockSpec(memory_space=pltpu.VMEM)] * len(args),
-        out_specs=[pl.BlockSpec(memory_space=pltpu.VMEM)] * len(outs),
+        out_specs=[space(n, far_out) for n in range(len(outs))],
+        scratch_shapes=list(scratch),
         compiler_params=pltpu.CompilerParams(vmem_limit_bytes=VMEM_BYTES),
     )(*args)
 
@@ -216,14 +233,11 @@
     y_first_ref[...], y_last_ref[...] = y_layer(slabs, dims, 0), y_layer(slabs, dims, dims[1] - 1)
 
 
-def table_kernel(v_ref, e_ref, s_ref, orient_ref, table_ref, mean_ref, weight_ref, column_ref):
-    orient = v_ref[...].T
-    orient_ref[...] = orient
-    table, mean = tables(orient, e_ref[...])
+def table_kernel(orient_ref, e_ref, s_ref, table_ref, mean_ref, weight_ref, column_ref):
+    _, table, mean = tables(orient_ref[...], e_ref[...])
     table_ref[...] = table
     mean_ref[...] = mean
-    weights, column_ref[...] = stage_weights(table, mean, s_ref[...].T)
-    weight_ref[...] = flat_weights(weights)
+    weight_ref[...], column_ref[...] = stage_weights(unit(mean.shape[0]), table, mean, s_ref[...].T)
 
 
 def weighted(weights, rank):
@@ -322,51 +336,54 @@
     next_ref[...] = y_layer(slabs, dims, 1)
 
 
-def orient_stage(cells, sums, orient, table, mean, directions):
-    rank, count = orient.shape
+def apply(left, right):
+    left_high, left_low = halves(left)
+    high, low = halves(right)
+    return dot(
+        jnp.concatenate([left_high, left_high, left_low], axis=1), jnp.concatenate([high, low, high], axis=0)
+    )
+
+
+def orient_stage(cells, sums, orient, table, mean, directions, basis=None):
+    rank = orient.shape[0]
     plus, minus = signs(directions)
     blocks = [sums[n * rank:(n + 1) * rank] * (1.0 / cells) for n in range(4)]
-    table = [table[d * rank:(d + 1) * rank] for d in range(6)]
-    upper, inverse = factor(blocks[0][:, :rank])
-    d_sum = blocks[0][:, rank:]
-    back = [d_sum - blocks[1 + d][:, rank:] for d in range(3)]
-    fore = [blocks[1 + d][:, :rank].T - d_sum for d in range(3)]
-    drift = jnp.zeros((rank, rank), jnp.float32)
+    gram, d_sum = blocks[0][:, :rank], blocks[0][:, rank:]
+    inner = []
     for d in range(3):
-        drift = drift + mm(back[d], table[2 * d]) - mm(fore[d], table[2 * d + 1])
+        inner += [blocks[1 + d][:, rank:] - d_sum, blocks[1 + d][:, :rank].T - d_sum]
+    drift = -mm(jnp.concatenate(inner, axis=1), table)
+    upper, inverse, drift = factor(gram, drift)
     spread = jnp.broadcast_to(mean, (rank, rank))
-    mid = (1.0 + tumble) * upper - tumble * mm(upper, spread) * spread.T + courant * mm(inverse, drift)
-    solved = mm(inverse, mid, (0, 0))
-    inner = jnp.concatenate([m for d in range(3) for m in (-back[d], fore[d])], axis=0)
-    inner = mm(inner, solved)
-    rows = [(1.0 - tumble) * mid]
-    for n in range(6):
-        rows.append(courant * mm(inverse, inner[n * rank:(n + 1) * rank]))
-    rows_high, rows_low = halves(jnp.concatenate(rows, axis=0))
-    high, low = halves(orient)
-    moved = dot(
-        jnp.concatenate([rows_high, rows_high, rows_low], axis=1),
-        jnp.concatenate([high, low, high], axis=0),
-    )
-    new = moved[:rank] + tumble * mm(mid, spread)[:, :1]
+    solved = (1.0 + tumble) * unit(rank) - tumble * spread * spread.T + courant * mm(inverse, drift, (0, 0))
+    rows = [(1.0 - tumble) * upper] + [courant * mm(inverse, part) for part in inner]
+    rows = mm(jnp.concatenate(rows, axis=0), solved)
+    mid_mean = mm(rows[:rank], spread)[:, :1]
+    moved = apply(rows if basis is None else mm(rows, basis), orient)
+    new = moved[:rank] + mid_mean * (tumble / (1.0 - tumble))
     for d in range(3):
         new = new + plus[d:d + 1] * moved[(1 + 2 * d) * rank:(2 + 2 * d) * rank]
         new = new + minus[d:d + 1] * moved[(2 + 2 * d) * rank:(3 + 2 * d) * rank]
-    upper_v, inverse_v = factor(three(new, new, (1, 1)) * (1.0 / count))
-    return inverse, upper_v, three(inverse_v, new, (1, 0))
+    return inverse, new
 
 
 def turn_kernel(
-    cells, sums_ref, orient_ref, table_ref, mean_ref, e_ref, orient_out, table_out, mean_out, weight_ref, column_ref
+    cells, sums_ref, orient_ref, table_ref, mean_ref, e_ref,
+    weight_ref, column_ref, mean_out, new_ref, inverse_ref, table_out,
 ):
     directions = e_ref[...]
-    inverse, upper_v, orient = orient_stage(cells, sums_ref[...], orient_ref[...], table_ref[...], mean_ref[...], directions)
-    orient_out[...] = orient
-    table, mean = tables(orient, directions)
-    table_out[...] = table
-    mean_out[...] = mean
-    weights, column_ref[...] = stage_weights(table, mean, mm(upper_v, inverse))
-    weight_ref[...] = flat_weights(weights)
+    rank = orient_ref.shape[0]
+    inverse, new = orient_stage(cells, sums_ref[...], orient_ref[...], table_ref[...], mean_ref[...], directions)
+    new_ref[...] = new
+    gram, table, mean = tables(new, directions)
+    weights, column_ref[...] = stage_weights(gram, table, mean, inverse)
+    _, inverse_v = factor(gram)
+    inverse_ref[...] = inverse_v
+    weight_ref[...] = mm(inverse_v, weights)
+    mean_out[...] = mm(inverse_v, jnp.broadcast_to(mean, (rank, rank)))[:, :1]
+    right = mm(table, inverse_v, (1, 1))
+    for n in range(6):
+        table_out[n * rank:(n + 1) * rank] = mm(inverse_v, right[n * rank:(n + 1) * rank])
 
 
 def second_kernel(
@@ -381,11 +398,36 @@
     sums_out[...] = galerkin(dims, slabs, side, mean_ref[...])
 
 
-def last_kernel(cells, sums_ref, orient_ref, table_ref, mean_ref, e_ref, field_ref, x_ref, s_ref, v_ref):
-    inverse, upper_v, orient = orient_stage(cells, sums_ref[...], orient_ref[...], table_ref[...], mean_ref[...], e_ref[...])
-    x_ref[...] = three(inverse, field_ref[...], (1, 0)).T
+def last_kernel(
+    cells, sums_ref, orient_ref, basis_ref, table_ref, mean_ref, e_ref, field_ref, x_ref, s_ref, v_ref, x_buffer, sems
+):
+    inverse, new = orient_stage(
+        cells, sums_ref[...], orient_ref[...], table_ref[...], mean_ref[...], e_ref[...], basis_ref[...]
+    )
+    count = new.shape[1]
+    parts = sems.shape[0]
+    chunk = field_ref.shape[1] // parts
+
+    copies = [
+        pltpu.make_async_copy(
+            x_buffer.at[pl.ds(n * chunk, chunk)], x_ref.at[pl.ds(n * chunk, chunk)], sems.at[n]
+        )
+        for n in range(parts)
+    ]
+
+    def x_part(n):
+        def work():
+            x_buffer[n * chunk:(n + 1) * chunk] = apply(inverse, field_ref[:, n * chunk:(n + 1) * chunk]).T
+            copies[n].start()
+        return work
+
+    upper_v, inverse_v = factor(
+        three(new, new, (1, 1)) * (1.0 / count), meanwhile=[x_part(n) for n in range(parts)]
+    )
     s_ref[...] = upper_v.T
-    v_ref[...] = orient.T
+    v_ref[...] = apply(inverse_v, new)
+    for copy in copies:
+        copy.wait()
 
 
 def shifted(axis, up):
@@ -424,13 +466,16 @@
     whole, slab, layer = (rank, sites), (rank, ly * lz), (rank, lx * lz)
     more = (rank, ly * lz + lx * lz)
     summed = (4 * rank, 2 * rank)
-    basis = [(rank, count), (6 * rank, rank), (rank, 1)]
     field, first, last, y_first, y_last = call(
         functools.partial(enter_kernel, dims), [whole, slab, slab, layer, layer], spatial_factor.reshape(sites, rank)
     )
     xb, xa, yb, ya = up(last, "gx"), down(first, "gx"), up(y_last, "gy"), down(y_first, "gy")
-    stage = basis + [(rank, 8 * rank), (rank, 1)]
-    orient, table, mean, weights, column = call(table_kernel, stage, orient_factor, directions, coupling)
+    basis = [(rank, count), (6 * rank, rank)]
+    column_shape, weight_shape = (rank, 1), (rank, 8 * rank)
+    orient = orient_factor.T
+    table, mean, weights, column = call(
+        table_kernel, [basis[1], column_shape, weight_shape, column_shape], orient, directions, coupling
+    )
     field, first, y_first, y_last = call(
         functools.partial(first_kernel, dims), [whole, slab, layer, layer], field, xb, xa, yb, ya, weights, column
     )
@@ -439,18 +484,21 @@
         functools.partial(galerkin_kernel, dims), [summed, more, more, layer], field, xa, ya, yb, mean
     )
     second, behind, after = down(second, "gx"), up(behind, "gx"), down(after, "gy")
-    orient, table, mean, weights, column = call(
-        functools.partial(turn_kernel, cells), stage, all_sum(part), orient, table, mean, directions
+    weights, column, mean, new, inverse, table = call(
+        functools.partial(turn_kernel, cells),
+        [weight_shape, column_shape, column_shape, basis[0], (rank, rank), basis[1]],
+        all_sum(part), orient, table, mean, directions,
     )
     field, part = call(
         functools.partial(second_kernel, dims), [whole, summed],
         field, xa, ya, yb, second, behind, after, weights, column, mean,
     )
     new_spatial, new_coupling, new_orient = call(
-        functools.partial(last_kernel, cells), [(sites, rank), (rank, rank), (count, rank)],
-        all_sum(part), orient, table, mean, directions, field,
-    )
-    return new_spatial.reshape(spatial_factor.shape), new_coupling, new_orient
+        functools.partial(last_kernel, cells), [(sites, rank), (rank, rank), (rank, count)],
+        all_sum(part), new, inverse, table, mean, directions, field, far_out=(0,),
+        scratch=(pltpu.VMEM((sites, rank), jnp.float32), pltpu.SemaphoreType.DMA((4,))),
+    )
+    return new_spatial.reshape(spatial_factor.shape), new_coupling, new_orient.T
 
 
 def solution(mesh):

time: 88.2 us -> 85.8 us (0.973)
  Pallas kernels: 26 us -> 24.4 us
  local copies, waits for them, and re-layouts: 3.35 us -> 1.91 us
    pallas_call x7, Pallas kernels: 26 us -> 24.4 us  [call(): pl.pallas_call(body, out_shape=[jax.ShapeDtypeStruct(shape, jnp.float32)...]
    unnamed x10 -> x8, local copies, waits for them, and re-layouts: 2.67 us -> 1.23 us
  transfers between devices with their start and end apart: 11 -> 11, of which waited for: 4 -> 4; matrix products, arithmetic and copies ran while one was open for 0% -> 0% of each run, Pallas kernels for 12% -> 11%
where the time goes in v2:
time: 85.8 us; the launch traced here: 85.6 us
  blocking collectives  29.6 us (34%)
  Pallas kernels  24.4 us (28%)
  starting transfers between devices  19.6 us (23%)
  waiting for transfers between devices  8.95 us (10%)
  local copies, waits for them, and re-layouts  1.91 us (2%)
  between operations  0.92 us (1%)
    pallas_call x7, Pallas kernels, call(): pl.pallas_call(body, out_shape=[jax.ShapeDtypeStruct(shape, jnp.float32)...  24.4 us
    all_to_all x2, blocking collectives, all_sum(): mine = lax.all_to_all(split, ('gx', 'gy'), 0, 0).sum(axis=0)  19.8 us
    ppermute x6, starting transfers between devices, down(): return lax.ppermute(value, axis, shifted(axis, False))  14.1 us
    all_to_all x1, blocking collectives, all_sum(): lax.all_to_all(jnp.broadcast_to(mine[None], split.shape), ('gx', 'gy'), 0...  9.88 us
    ppermute x4, waiting for transfers between devices, up(): return lax.ppermute(value, axis, shifted(axis, True))  3.55 us
    ppermute x4, starting transfers between devices, up(): return lax.ppermute(value, axis, shifted(axis, True))  3 us
    ppermute x6, waiting for transfers between devices, down(): return lax.ppermute(value, axis, shifted(axis, False))  2.78 us
    all_to_all x1, waiting for transfers between devices, all_sum(): lax.all_to_all(jnp.broadcast_to(mine[None], split.shape), ('gx', 'gy'), 0...  2.62 us
  transfers between devices with their start and end apart: 11, of which 4 were waited for; matrix products, arithmetic and copies ran while one was open for 0% of the time, Pallas kernels for 11%

profile of v2, /device:TPU:0, one launch (start us, length us, event | category | flops | bytes accessed | tf_op | source)
XLA Modules:
  0.0 85.6 jit_solution(12743995357185678771)
XLA Ops:
  0.6 1.2 %copy-done.1 = f32[4,16,32,64]{3,2,1,0:T(8,128)S(1)} copy-done((f32[4,16,32,64]{3,2,1,0:T(8,128)S(1)}, f32[4,16,32,64]{3,2,1,0:T(8,128)}, u32[]{:S(2)}) %copy-start.1) | copy-done | bytes 524312
  1.9 0.4 shard_map.67
  2.3 3.0 %collective-permute-start = (f32[64,512]{1,0:T(8,128)S(1)}, f32[64,512]{1,0:T(8,128)S(1)}, u32[]{:S(2)}, u32[]{:S(2)}) collective-permute-start(f32[64,512]{1,0:T(8,128)S(1)} %get-tuple-element.32), channel_id=1, source_target_pairs={{0,8},{8,16},{16,24},{24,0},{1,9},{9,17},{17,25},{25,1},{2,10},{10... | collective-permute-start | bytes 393224 | tf_op jit(solution)/shard_map/ppermute | solution.py:452
  5.3 1.0 %collective-permute-start.1 = (f32[64,512]{1,0:T(8,128)S(1)}, f32[64,512]{1,0:T(8,128)S(1)}, u32[]{:S(2)}, u32[]{:S(2)}) collective-permute-start(f32[64,512]{1,0:T(8,128)S(1)} %get-tuple-element.33), channel_id=1, source_target_pairs={{0,24},{8,0},{16,8},{24,16},{1,25},{9,1},{17,9},{25,17},{2,26},{10... | collective-permute-start | bytes 393224 | tf_op jit(solution)/shard_map/ppermute | solution.py:456
  6.3 3.5 %collective-permute-start.3 = (f32[64,128]{1,0:T(8,128)S(1)}, f32[64,128]{1,0:T(8,128)S(1)}, u32[]{:S(2)}, u32[]{:S(2)}) collective-permute-start(f32[64,128]{1,0:T(8,128)S(1)} %get-tuple-element.35), channel_id=1, source_target_pairs={{0,7},{1,0},{2,1},{3,2},{4,3},{5,4},{6,5},{7,6},{8,15},{9,8},{10,9... | collective-permute-start | bytes 98312 | tf_op jit(solution)/shard_map/ppermute | solution.py:456
  9.8 1.7 %shard_map.68 = (f32[384,64]{1,0:T(8,128)S(1)}, f32[64,1]{1,0:T(8,128)S(1)}, f32[64,512]{1,0:T(8,128)S(1)}, f32[64,1]{1,0:T(8,128)S(1)}) custom-call(f32[64,2048]{1,0:T(8,128)S(1)} %bitcast.8, f32[3,2048]{1,0:T(4,128)S(1)} %copy-done.2, f32[64,64]{1,0:T(8,128)S(1)} %copy-done.3), custom_call_target="tpu_custom_call" | custom-call | tf_op jit(solution)/shard_map/pallas_call | solution.py:218
  11.6 1.2 %collective-permute-done.1.xa = f32[64,512]{1,0:T(8,128)S(1)} collective-permute-done((f32[64,512]{1,0:T(8,128)S(1)}, f32[64,512]{1,0:T(8,128)S(1)}, u32[]{:S(2)}, u32[]{:S(2)}) %collective-permute-start.1) | collective-permute-done | bytes 131104 | tf_op jit(solution)/shard_map/ppermute | solution.py:456
  12.8 1.4 %shard_map.69 = (f32[64,2048]{1,0:T(8,128)S(1)}, f32[64,512]{1,0:T(8,128)S(1)}, f32[64,128]{1,0:T(8,128)S(1)}, f32[64,128]{1,0:T(8,128)S(1)}) custom-call(f32[64,2048]{1,0:T(8,128)S(1)} %get-tuple-element.31.field_ref, f32[64,512]{1,0:T(8,128)S(1)} %collective-permute-done.xb, f32[64,512]{1,0:T(8,128)S(1)} %collective-permute-done.1.xa, ...), custom_call_target="tpu_custom_call" | custom-call | tf_op jit(solution)/shard_map/pallas_call | solution.py:218
  14.2 1.5 %collective-permute-start.4 = (f32[64,512]{1,0:T(8,128)S(1)}, f32[64,512]{1,0:T(8,128)S(1)}, u32[]{:S(2)}, u32[]{:S(2)}) collective-permute-start(f32[64,512]{1,0:T(8,128)S(1)} %get-tuple-element.39), channel_id=1, source_target_pairs={{0,24},{8,0},{16,8},{24,16},{1,25},{9,1},{17,9},{25,17},{2,26},{10... | collective-permute-start | bytes 393224 | tf_op jit(solution)/shard_map/ppermute | solution.py:456
  15.7 2.4 %collective-permute-start.5 = (f32[64,128]{1,0:T(8,128)S(1)}, f32[64,128]{1,0:T(8,128)S(1)}, u32[]{:S(2)}, u32[]{:S(2)}) collective-permute-start(f32[64,128]{1,0:T(8,128)S(1)} %get-tuple-element.40), channel_id=1, source_target_pairs={{0,7},{1,0},{2,1},{3,2},{4,3},{5,4},{6,5},{7,6},{8,15},{9,8},{10,9... | collective-permute-start | bytes 98312 | tf_op jit(solution)/shard_map/ppermute | solution.py:456
  18.1 1.6 %collective-permute-done.5.ya = f32[64,128]{1,0:T(8,128)S(1)} collective-permute-done((f32[64,128]{1,0:T(8,128)S(1)}, f32[64,128]{1,0:T(8,128)S(1)}, u32[]{:S(2)}, u32[]{:S(2)}) %collective-permute-start.5) | collective-permute-done | bytes 32800 | tf_op jit(solution)/shard_map/ppermute | solution.py:456
  19.7 3.5 %collective-permute-done.6.yb = f32[64,128]{1,0:T(8,128)S(1)} collective-permute-done((f32[64,128]{1,0:T(8,128)S(1)}, f32[64,128]{1,0:T(8,128)S(1)}, u32[]{:S(2)}, u32[]{:S(2)}) %collective-permute-start.6) | collective-permute-done | bytes 32800 | tf_op jit(solution)/shard_map/ppermute | solution.py:452
  23.2 1.4 %shard_map.70 = (f32[256,128]{1,0:T(8,128)S(1)}, f32[64,640]{1,0:T(8,128)S(1)}, f32[64,640]{1,0:T(8,128)S(1)}, f32[64,128]{1,0:T(8,128)S(1)}) custom-call(f32[64,2048]{1,0:T(8,128)S(1)} %get-tuple-element.38.field_ref, f32[64,512]{1,0:T(8,128)S(1)} %collective-permute-done.4.xa, f32[64,128]{1,0:T(8,128)S(1)} %collective-permute-done.5.ya, ...), custom_call_target="tpu_custom_call" | custom-call | tf_op jit(solution)/shard_map/pallas_call | solution.py:218
  24.7 9.9 %all_to_all.20 = f32[32,8,128]{2,1,0:T(8,128)S(1)} all-to-all(f32[32,8,128]{2,1,0:T(8,128)S(1)} %bitcast.14), channel_id=1, replica_groups=mesh['gx'=4,'gy'=8] {'gx','gy'}, dimensions={0} | all-to-all | bytes 262144 | tf_op jit(solution)/shard_map/all_to_all | solution.py:446
  34.6 0.7 broadcast_in_dim.4
  35.2 2.6 %all-to-all-start.1 = ((f32[32,8,128]{2,1,0:T(8,128)}), f32[32,8,128]{2,1,0:T(8,128)S(1)}, u32[]{:S(2)}, u32[]{:S(2)}) async-start(f32[32,8,128]{2,1,0:T(8,128)} %broadcast_in_dim.4), calls=%async_computation.1 | async-start | bytes 262144 | tf_op jit(solution)/shard_map/all_to_all | solution.py:447
  37.8 2.6 %collective-permute-start.7 = (f32[64,640]{1,0:T(8,128)S(1)}, f32[64,640]{1,0:T(8,128)S(1)}, u32[]{:S(2)}, u32[]{:S(2)}) collective-permute-start(f32[64,640]{1,0:T(8,128)S(1)} %get-tuple-element.43), channel_id=1, source_target_pairs={{0,24},{8,0},{16,8},{24,16},{1,25},{9,1},{17,9},{25,17},{2,26},{10... | collective-permute-start | bytes 491528 | tf_op jit(solution)/shard_map/ppermute | solution.py:456
  40.4 2.9 %collective-permute-start.9 = (f32[64,128]{1,0:T(8,128)S(1)}, f32[64,128]{1,0:T(8,128)S(1)}, u32[]{:S(2)}, u32[]{:S(2)}) collective-permute-start(f32[64,128]{1,0:T(8,128)S(1)} %get-tuple-element.45), channel_id=1, source_target_pairs={{0,7},{1,0},{2,1},{3,2},{4,3},{5,4},{6,5},{7,6},{8,15},{9,8},{10,9... | collective-permute-start | bytes 98312 | tf_op jit(solution)/shard_map/ppermute | solution.py:456
  43.4 2.6 %all-to-all-done.1 = f32[32,8,128]{2,1,0:T(8,128)S(1)} async-done(((f32[32,8,128]{2,1,0:T(8,128)}), f32[32,8,128]{2,1,0:T(8,128)S(1)}, u32[]{:S(2)}, u32[]{:S(2)}) %all-to-all-start.1) | async-done | bytes 131104 | tf_op jit(solution)/shard_map/all_to_all | solution.py:447
  46.0 7.6 %shard_map.71 = (f32[64,512]{1,0:T(8,128)S(1)}, f32[64,1]{1,0:T(8,128)S(1)}, f32[64,1]{1,0:T(8,128)S(1)}, f32[64,2048]{1,0:T(8,128)S(1)}, f32[64,64]{1,0:T(8,128)S(1)}, /*index=5*/f32[384,64]{1,0:T(8,128)S(1)}) custom-call(f32[256,128]{1,0:T(8,128)S(1)} %bitcast.11, f32[64,2048]{1,0:T(8,128)S(1)} %bitcast.9, f32[384,64]{1,0:T(8,128)S(1)} %get-tuple-element.47.table_ref, ...), custom_call_target="tpu_custom_call" | custom-call | tf_op jit(solution)/shard_map/pallas_call | solution.py:218
  53.7 3.3 %shard_map.72 = (f32[64,2048]{1,0:T(8,128)S(1)}, f32[256,128]{1,0:T(8,128)S(1)}) custom-call(f32[64,2048]{1,0:T(8,128)S(1)} %get-tuple-element.38.field_ref, f32[64,512]{1,0:T(8,128)S(1)} %collective-permute-done.4.xa, f32[64,128]{1,0:T(8,128)S(1)} %collective-permute-done.5.ya, f32[64,128]{1,0:T(8,128)S(1)} %collective-permute-done.6.yb, ...), custom_call_target="tpu_custom_call" | custom-call | tf_op jit(solution)/shard_map/pallas_call | solution.py:218
  57.0 9.9 %all_to_all.21 = f32[32,8,128]{2,1,0:T(8,128)S(1)} all-to-all(f32[32,8,128]{2,1,0:T(8,128)S(1)} %bitcast.13), channel_id=1, replica_groups=mesh['gx'=4,'gy'=8] {'gx','gy'}, dimensions={0} | all-to-all | bytes 262144 | tf_op jit(solution)/shard_map/all_to_all | solution.py:446
  66.9 9.9 %all_to_all.22 = f32[32,8,128]{2,1,0:T(8,128)S(1)} all-to-all(f32[32,8,128]{2,1,0:T(8,128)S(1)} %broadcast_in_dim.5), channel_id=1, replica_groups=mesh['gx'=4,'gy'=8] {'gx','gy'}, dimensions={0} | all-to-all | bytes 262144 | tf_op jit(solution)/shard_map/all_to_all | solution.py:447
  76.8 8.5 %shard_map.73 = (f32[2048,64]{1,0:T(8,128)}, f32[64,64]{1,0:T(8,128)}, f32[64,2048]{1,0:T(8,128)}) custom-call(f32[256,128]{1,0:T(8,128)S(1)} %bitcast.12, f32[64,2048]{1,0:T(8,128)S(1)} %get-tuple-element.52.orient_ref, f32[64,64]{1,0:T(8,128)S(1)} %get-tuple-element.53.basis_ref, f32[384,64]{1,0:T(8,128)S(1)} %get-tuple-element.54.table_ref, ...), custom_call_target="tpu_custom_call" | custom-call | tf_op jit(solution)/shard_map/pallas_call | solution.py:218
  (20 shorter events, 0.1 us)
Async XLA Ops:
  0.6 1.2 %copy-start.1 = (f32[4,16,32,64]{3,2,1,0:T(8,128)S(1)}, f32[4,16,32,64]{3,2,1,0:T(8,128)}, u32[]{:S(2)}) copy-start(f32[4,16,32,64]{3,2,1,0:T(8,128)} %param.4) | copy-start | bytes 1572868
  1.9 8.0 %copy-start = (f32[2048,64]{0,1:T(8,128)S(1)}, f32[2048,64]{0,1:T(8,128)}, u32[]{:S(2)}) copy-start(f32[2048,64]{0,1:T(8,128)} %param.6) | copy-start | bytes 1572868
  1.9 8.0 %copy-start.2 = (f32[3,2048]{1,0:T(4,128)S(1)}, f32[3,2048]{1,0:T(4,128)}, u32[]{:S(2)}) copy-start(f32[3,2048]{1,0:T(4,128)} %e_ref.5) | copy-start | bytes 73732
  1.9 8.0 %copy-start.3 = (f32[64,64]{1,0:T(8,128)S(1)}, f32[64,64]{1,0:T(8,128)}, u32[]{:S(2)}) copy-start(f32[64,64]{1,0:T(8,128)} %s_ref.1) | copy-start | bytes 49156
  2.3 9.3 %collective-permute-start = (f32[64,512]{1,0:T(8,128)S(1)}, f32[64,512]{1,0:T(8,128)S(1)}, u32[]{:S(2)}, u32[]{:S(2)}) collective-permute-start(f32[64,512]{1,0:T(8,128)S(1)} %get-tuple-element.32), channel_id=1, source_target_pairs={{0,8},{8,16},{16,24},{24,0},{1,9},{9,17},{17,25},{25,1},{2,10},{10... | collective-permute-start | bytes 393224 | tf_op jit(solution)/shard_map/ppermute | solution.py:452
  5.3 7.5 %collective-permute-start.1 = (f32[64,512]{1,0:T(8,128)S(1)}, f32[64,512]{1,0:T(8,128)S(1)}, u32[]{:S(2)}, u32[]{:S(2)}) collective-permute-start(f32[64,512]{1,0:T(8,128)S(1)} %get-tuple-element.33), channel_id=1, source_target_pairs={{0,24},{8,0},{16,8},{24,16},{1,25},{9,1},{17,9},{25,17},{2,26},{10... | collective-permute-start | bytes 393224 | tf_op jit(solution)/shard_map/ppermute | solution.py:456
  6.3 5.3 %collective-permute-start.2 = (f32[64,128]{1,0:T(8,128)S(1)}, f32[64,128]{1,0:T(8,128)S(1)}, u32[]{:S(2)}, u32[]{:S(2)}) collective-permute-start(f32[64,128]{1,0:T(8,128)S(1)} %get-tuple-element.34), channel_id=1, source_target_pairs={{0,1},{1,2},{2,3},{3,4},{4,5},{5,6},{6,7},{7,0},{8,9},{9,10},{10,1... | collective-permute-start | bytes 98312 | tf_op jit(solution)/shard_map/ppermute | solution.py:452
  6.3 5.3 %collective-permute-start.3 = (f32[64,128]{1,0:T(8,128)S(1)}, f32[64,128]{1,0:T(8,128)S(1)}, u32[]{:S(2)}, u32[]{:S(2)}) collective-permute-start(f32[64,128]{1,0:T(8,128)S(1)} %get-tuple-element.35), channel_id=1, source_target_pairs={{0,7},{1,0},{2,1},{3,2},{4,3},{5,4},{6,5},{7,6},{8,15},{9,8},{10,9... | collective-permute-start | bytes 98312 | tf_op jit(solution)/shard_map/ppermute | solution.py:456
  14.2 9.1 %collective-permute-start.4 = (f32[64,512]{1,0:T(8,128)S(1)}, f32[64,512]{1,0:T(8,128)S(1)}, u32[]{:S(2)}, u32[]{:S(2)}) collective-permute-start(f32[64,512]{1,0:T(8,128)S(1)} %get-tuple-element.39), channel_id=1, source_target_pairs={{0,24},{8,0},{16,8},{24,16},{1,25},{9,1},{17,9},{25,17},{2,26},{10... | collective-permute-start | bytes 393224 | tf_op jit(solution)/shard_map/ppermute | solution.py:456
  15.7 4.0 %collective-permute-start.5 = (f32[64,128]{1,0:T(8,128)S(1)}, f32[64,128]{1,0:T(8,128)S(1)}, u32[]{:S(2)}, u32[]{:S(2)}) collective-permute-start(f32[64,128]{1,0:T(8,128)S(1)} %get-tuple-element.40), channel_id=1, source_target_pairs={{0,7},{1,0},{2,1},{3,2},{4,3},{5,4},{6,5},{7,6},{8,15},{9,8},{10,9... | collective-permute-start | bytes 98312 | tf_op jit(solution)/shard_map/ppermute | solution.py:456
  18.1 5.1 %collective-permute-start.6 = (f32[64,128]{1,0:T(8,128)S(1)}, f32[64,128]{1,0:T(8,128)S(1)}, u32[]{:S(2)}, u32[]{:S(2)}) collective-permute-start(f32[64,128]{1,0:T(8,128)S(1)} %get-tuple-element.41), channel_id=1, source_target_pairs={{0,1},{1,2},{2,3},{3,4},{4,5},{5,6},{6,7},{7,0},{8,9},{9,10},{10,1... | collective-permute-start | bytes 98312 | tf_op jit(solution)/shard_map/ppermute | solution.py:452
  35.2 10.8 %all-to-all-start.1 = ((f32[32,8,128]{2,1,0:T(8,128)}), f32[32,8,128]{2,1,0:T(8,128)S(1)}, u32[]{:S(2)}, u32[]{:S(2)}) async-start(f32[32,8,128]{2,1,0:T(8,128)} %broadcast_in_dim.4), calls=%async_computation.1 | async-start | bytes 262144 | tf_op jit(solution)/shard_map/all_to_all | solution.py:447
  37.8 15.8 %collective-permute-start.7 = (f32[64,640]{1,0:T(8,128)S(1)}, f32[64,640]{1,0:T(8,128)S(1)}, u32[]{:S(2)}, u32[]{:S(2)}) collective-permute-start(f32[64,640]{1,0:T(8,128)S(1)} %get-tuple-element.43), channel_id=1, source_target_pairs={{0,24},{8,0},{16,8},{24,16},{1,25},{9,1},{17,9},{25,17},{2,26},{10... | collective-permute-start | bytes 491528 | tf_op jit(solution)/shard_map/ppermute | solution.py:456
  40.4 13.2 %collective-permute-start.8 = (f32[64,640]{1,0:T(8,128)S(1)}, f32[64,640]{1,0:T(8,128)S(1)}, u32[]{:S(2)}, u32[]{:S(2)}) collective-permute-start(f32[64,640]{1,0:T(8,128)S(1)} %get-tuple-element.44), channel_id=1, source_target_pairs={{0,8},{8,16},{16,24},{24,0},{1,9},{9,17},{17,25},{25,1},{2,10},{10... | collective-permute-start | bytes 491528 | tf_op jit(solution)/shard_map/ppermute | solution.py:452
  40.4 13.2 %collective-permute-start.9 = (f32[64,128]{1,0:T(8,128)S(1)}, f32[64,128]{1,0:T(8,128)S(1)}, u32[]{:S(2)}, u32[]{:S(2)}) collective-permute-start(f32[64,128]{1,0:T(8,128)S(1)} %get-tuple-element.45), channel_id=1, source_target_pairs={{0,7},{1,0},{2,1},{3,2},{4,3},{5,4},{6,5},{7,6},{8,15},{9,8},{10,9... | collective-permute-start | bytes 98312 | tf_op jit(solution)/shard_map/ppermute | solution.py:456

commit v3 on v2

--- a/solution.py
+++ b/solution.py
@@ -211,7 +211,7 @@
     return (both[:, :rank], both[:, rank:], *done[1:])
 
 
-def call(body, outs, *args, far_out=(), scratch=()):
+def call(body, outs, *args, far_out=(), scratch=(), cost=None):
     def space(n, far):
         return pl.BlockSpec(memory_space=pltpu.HBM if n in far else pltpu.VMEM)
 
@@ -221,6 +221,7 @@
         in_specs=[pl.BlockSpec(memory_space=pltpu.VMEM)] * len(args),
         out_specs=[space(n, far_out) for n in range(len(outs))],
         scratch_shapes=list(scratch),
+        cost_estimate=cost,
         compiler_params=pltpu.CompilerParams(vmem_limit_bytes=VMEM_BYTES),
     )(*args)
 
@@ -303,7 +304,13 @@
             pairs.append((moved, speed_of(mean, moved) * k))
         for n, (left, right) in enumerate(pairs):
             sums[n] = sums[n] + three(left, jnp.concatenate([right, q], axis=0), (1, 1))
-    return jnp.concatenate(sums, axis=0)
+    low = lane_index(2 * rank) < rank
+    centre = jnp.where(low, -roll(sums[0], rank), sums[0])
+    gram = sums[0][:, :rank]
+    rows = [jnp.concatenate([gram[:rank // 2], gram[rank // 2:]], axis=1)]
+    for part in sums[1:]:
+        rows.append(centre + jnp.where(low, part, -part))
+    return jnp.concatenate(rows, axis=0)
 
 
 def write_slabs(ref, slabs):
@@ -312,28 +319,32 @@
         ref[:, x * slab:(x + 1) * slab] = value
 
 
-def first_kernel(
-    dims, field_ref, xb, xa, yb, ya, weight_ref, column_ref, out_ref, first_ref, y_first_ref, y_last_ref
-):
+def first_kernel(dims, field_ref, xb, xa, yb, ya, weight_ref, column_ref, out_ref, first_ref, y_first_ref):
+    width = dims[0] * dims[2]
     slabs = k_stage(
         dims, field_ref[...], weight_ref[...], column_ref[...], xb[...], xa[...], yb[...], ya[...]
     )
     write_slabs(out_ref, slabs)
     first_ref[...] = slabs[0]
-    y_first_ref[...], y_last_ref[...] = y_layer(slabs, dims, 0), y_layer(slabs, dims, dims[1] - 1)
-
-
-def galerkin_kernel(dims, field_ref, xa, ya, yb, mean_ref, sums_ref, down_ref, up_ref, next_ref):
+    y_first_ref[:, :width], y_first_ref[:, width:] = y_layer(slabs, dims, 0), y_layer(slabs, dims, 1)
+
+
+def galerkin_kernel(dims, field_ref, xa, ya, mean_ref, sums_ref, up_ref, y_last_ref):
     lx, ly, lz = dims
     slab, width = ly * lz, lx * lz
     slabs = slabs_of(field_ref[...], dims)
-    layer = ya[...]
+    layer = ya[:, :width]
     sums_ref[...] = galerkin(dims, slabs + [xa[...]], layer, mean_ref[...])
-    down_ref[:, :slab] = slabs[1]
-    down_ref[:, slab:] = jnp.where(lane_index(width) < lz, yb[...], roll(layer, lz))
     up_ref[:, :slab] = slabs[-1]
     up_ref[:, slab:] = layer
-    next_ref[...] = y_layer(slabs, dims, 1)
+    y_last_ref[...] = y_layer(slabs, dims, ly - 1)
+
+
+def pack_kernel(dims, field_ref, ya, yb, down_ref):
+    lx, ly, lz = dims
+    slab, width = ly * lz, lx * lz
+    down_ref[:, :slab] = field_ref[:, slab:2 * slab]
+    down_ref[:, slab:] = jnp.where(lane_index(width) < lz, yb[...], roll(ya[:, :width], lz))
 
 
 def apply(left, right):
@@ -347,11 +358,12 @@
 def orient_stage(cells, sums, orient, table, mean, directions, basis=None):
     rank = orient.shape[0]
     plus, minus = signs(directions)
-    blocks = [sums[n * rank:(n + 1) * rank] * (1.0 / cells) for n in range(4)]
-    gram, d_sum = blocks[0][:, :rank], blocks[0][:, rank:]
+    sums = sums * (1.0 / cells)
+    gram = jnp.concatenate([sums[:rank // 2, :rank], sums[:rank // 2, rank:]], axis=0)
     inner = []
     for d in range(3):
-        inner += [blocks[1 + d][:, rank:] - d_sum, blocks[1 + d][:, :rank].T - d_sum]
+        block = sums[rank // 2 + d * rank:rank // 2 + (d + 1) * rank]
+        inner += [-block[:, rank:], block[:, :rank].T]
     drift = -mm(jnp.concatenate(inner, axis=1), table)
     upper, inverse, drift = factor(gram, drift)
     spread = jnp.broadcast_to(mean, (rank, rank))
@@ -387,12 +399,12 @@
 
 
 def second_kernel(
-    dims, field_ref, xa, ya, yb, second, behind, after, weight_ref, column_ref, mean_ref, field_out, sums_out
+    dims, field_ref, xa, ya, yb, second, behind, weight_ref, column_ref, mean_ref, field_out, sums_out
 ):
-    slab = dims[1] * dims[2]
+    slab, width = dims[1] * dims[2], dims[0] * dims[2]
     slabs, side = k_stage(
-        dims, field_ref[...], weight_ref[...], column_ref[...], behind[:, :slab], xa[...], yb[...], ya[...],
-        (second[...], behind[:, slab:], after[...]),
+        dims, field_ref[...], weight_ref[...], column_ref[...], behind[:, :slab], xa[...], yb[...], ya[:, :width],
+        (second[...], behind[:, slab:], ya[:, width:]),
     )
     write_slabs(field_out, slabs[:-1])
     sums_out[...] = galerkin(dims, slabs, side, mean_ref[...])
@@ -436,7 +448,7 @@
     return [(i, (i + step) % count) for i in range(count)]
 
 
-def all_sum(part):
+def scatter_gather_sum(part):
     count = lax.axis_size("gx") * lax.axis_size("gy")
     rows, width = part.shape
     padded = -(-rows // count) * count
@@ -448,6 +460,32 @@
     return every.reshape(padded, width)[:rows]
 
 
+def swapped(value, bits):
+    count = lax.axis_size("gx") * lax.axis_size("gy")
+    return lax.ppermute(value, ("gx", "gy"), [(i, i ^ bits) for i in range(count)])
+
+
+def sum_of_four(value, step):
+    near, far, cross = [swapped(value, n * step) for n in (1, 2, 3)]
+    return (value + near) + (far + cross)
+
+
+def all_sum(part, meanwhile=(lambda value: value,) * 2):
+    nx, ny = lax.axis_size("gx"), lax.axis_size("gy")
+    rows = part.shape[0] // 2
+    if nx != 4 or ny != 8 or rows % 8:
+        for work in meanwhile:
+            part = work(part)
+        return scatter_gather_sum(part)
+    first = lax.axis_index("gy") % 2 == 0
+    total = part + swapped(part, 1)
+    mine = jnp.where(first, total[:rows], total[rows:])
+    for step, work in zip((ny, 2), meanwhile):
+        mine = work(sum_of_four(mine, step))
+    other = swapped(mine, 1)
+    return jnp.concatenate([jnp.where(first, mine, other), jnp.where(first, other, mine)], axis=0)
+
+
 def up(value, axis):
     return lax.ppermute(value, axis, shifted(axis, True))
 
@@ -464,8 +502,8 @@
     count = orient_factor.shape[0]
     cells = sites * lax.axis_size("gx") * lax.axis_size("gy")
     whole, slab, layer = (rank, sites), (rank, ly * lz), (rank, lx * lz)
-    more = (rank, ly * lz + lx * lz)
-    summed = (4 * rank, 2 * rank)
+    two_layers, more = (rank, 2 * lx * lz), (rank, ly * lz + lx * lz)
+    summed = (7 * rank // 2, 2 * rank)
     field, first, last, y_first, y_last = call(
         functools.partial(enter_kernel, dims), [whole, slab, slab, layer, layer], spatial_factor.reshape(sites, rank)
     )
@@ -476,22 +514,31 @@
     table, mean, weights, column = call(
         table_kernel, [basis[1], column_shape, weight_shape, column_shape], orient, directions, coupling
     )
-    field, first, y_first, y_last = call(
-        functools.partial(first_kernel, dims), [whole, slab, layer, layer], field, xb, xa, yb, ya, weights, column
-    )
-    xa, ya, yb = down(first, "gx"), down(y_first, "gy"), up(y_last, "gy")
-    part, second, behind, after = call(
-        functools.partial(galerkin_kernel, dims), [summed, more, more, layer], field, xa, ya, yb, mean
-    )
-    second, behind, after = down(second, "gx"), up(behind, "gx"), down(after, "gy")
+    field, first, y_first = call(
+        functools.partial(first_kernel, dims), [whole, slab, two_layers], field, xb, xa, yb, ya, weights, column
+    )
+    xa, ya = down(first, "gx"), down(y_first, "gy")
+    part, behind, y_last = call(
+        functools.partial(galerkin_kernel, dims), [summed, more, layer], field, xa, ya, mean
+    )
+    yb, behind = up(y_last, "gy"), up(behind, "gx")
+    halo = {"yb": yb, "behind": behind}
+
+    def with_layer(value):
+        value, halo["yb"] = lax.optimization_barrier((value, halo["yb"]))
+        (packed,) = call(functools.partial(pack_kernel, dims), [more], field, ya, halo["yb"])
+        halo["second"] = down(packed, "gx")
+        return value
+
+    sums = all_sum(part, (with_layer, lambda value: value))
     weights, column, mean, new, inverse, table = call(
         functools.partial(turn_kernel, cells),
         [weight_shape, column_shape, column_shape, basis[0], (rank, rank), basis[1]],
-        all_sum(part), orient, table, mean, directions,
+        sums, orient, table, mean, directions, cost=pl.CostEstimate(flops=1, bytes_accessed=1, transcendentals=0),
     )
     field, part = call(
         functools.partial(second_kernel, dims), [whole, summed],
-        field, xa, ya, yb, second, behind, after, weights, column, mean,
+        field, xa, ya, halo["yb"], halo["second"], halo["behind"], weights, column, mean,
     )
     new_spatial, new_coupling, new_orient = call(
         functools.partial(last_kernel, cells), [(sites, rank), (rank, rank), (rank, count)],

time: 85.8 us -> 79.3 us (0.924)
  blocking collectives: 29.6 us -> 0 us
  waiting for transfers between devices: 8.95 us -> 21.3 us
  starting transfers between devices: 19.6 us -> 30.9 us
    all_to_all x3 -> x0, blocking collectives: 29.6 us -> none  [the longest x2 19.8 us: all_sum(): mine = lax.all_to_all(split, ('gx', 'gy'), 0, 0).sum(axis=0)]
    ppermute x0 -> x16, waiting for transfers between devices: none -> 16.8 us  [swapped(): lax.ppermute(value, ('gx', 'gy'), [(i, i ^ bits) for i in range(count)])]
    ppermute x0 -> x16, starting transfers between devices: none -> 16.2 us  [swapped(): lax.ppermute(value, ('gx', 'gy'), [(i, i ^ bits) for i in range(count)])]
    ppermute x6 -> x5, starting transfers between devices: 14.1 us -> 10.4 us  [down(): return lax.ppermute(value, axis, shifted(axis, False))]
    all_to_all x1 -> x0, waiting for transfers between devices: 2.62 us -> none  [all_sum(): lax.all_to_all(jnp.broadcast_to(mine[None], split.shape), ('gx', 'gy'), 0...]
    all_to_all x1 -> x0, starting transfers between devices: 2.58 us -> none  [all_sum(): lax.all_to_all(jnp.broadcast_to(mine[None], split.shape), ('gx', 'gy'), 0...]
    ppermute x4, waiting for transfers between devices: 3.55 us -> 1.41 us  [up(): return lax.ppermute(value, axis, shifted(axis, True))]
    ppermute x4, starting transfers between devices: 3 us -> 4.25 us  [up(): return lax.ppermute(value, axis, shifted(axis, True))]
  transfers between devices with their start and end apart: 11 -> 25, of which waited for: 4 -> 15; matrix products, arithmetic and copies ran while one was open for 0% -> 0% of each run, Pallas kernels for 11% -> 12%
where the time goes in v3:
time: 79.3 us; the launch traced here: 79.1 us
  starting transfers between devices  30.9 us (39%)
  Pallas kernels  24.5 us (31%)
  waiting for transfers between devices  21.3 us (27%)
  local copies, waits for them, and re-layouts  1.23 us (2%)
  between operations  1 us (1%)
    pallas_call x8, Pallas kernels, call(): pl.pallas_call(body, out_shape=[jax.ShapeDtypeStruct(shape, jnp.float32)...  24.5 us
    ppermute x16, waiting for transfers between devices, swapped(): lax.ppermute(value, ('gx', 'gy'), [(i, i ^ bits) for i in range(count)])  16.8 us
    ppermute x16, starting transfers between devices, swapped(): lax.ppermute(value, ('gx', 'gy'), [(i, i ^ bits) for i in range(count)])  16.2 us
    ppermute x5, starting transfers between devices, down(): return lax.ppermute(value, axis, shifted(axis, False))  10.4 us
    ppermute x4, starting transfers between devices, up(): return lax.ppermute(value, axis, shifted(axis, True))  4.25 us
    ppermute x5, waiting for transfers between devices, down(): return lax.ppermute(value, axis, shifted(axis, False))  3.09 us
  transfers between devices with their start and end apart: 25, of which 15 were waited for; matrix products, arithmetic and copies ran while one was open for 0% of the time, Pallas kernels for 12%

profile of v3, /device:TPU:0, one launch (start us, length us, event | category | flops | bytes accessed | tf_op | source)
XLA Modules:
  0.0 79.1 jit_solution(16083817452523238633)
XLA Ops:
  2.3 3.0 %collective-permute-start = (f32[64,512]{1,0:T(8,128)S(1)}, f32[64,512]{1,0:T(8,128)S(1)}, u32[]{:S(2)}, u32[]{:S(2)}) collective-permute-start(f32[64,512]{1,0:T(8,128)S(1)} %get-tuple-element.32), channel_id=1, source_target_pairs={{0,8},{8,16},{16,24},{24,0},{1,9},{9,17},{17,25},{25,1},{2,10},{10... | collective-permute-start | bytes 393224 | tf_op jit(solution)/shard_map/ppermute | solution.py:490
  6.3 3.5 %collective-permute-start.3 = (f32[64,128]{1,0:T(8,128)S(1)}, f32[64,128]{1,0:T(8,128)S(1)}, u32[]{:S(2)}, u32[]{:S(2)}) collective-permute-start(f32[64,128]{1,0:T(8,128)S(1)} %get-tuple-element.35), channel_id=1, source_target_pairs={{0,7},{1,0},{2,1},{3,2},{4,3},{5,4},{6,5},{7,6},{8,15},{9,8},{10,9... | collective-permute-start | bytes 98312 | tf_op jit(solution)/shard_map/ppermute | solution.py:494
  9.8 1.7 %shard_map.68 = (f32[384,64]{1,0:T(8,128)S(1)}, f32[64,1]{1,0:T(8,128)S(1)}, f32[64,512]{1,0:T(8,128)S(1)}, f32[64,1]{1,0:T(8,128)S(1)}) custom-call(f32[64,2048]{1,0:T(8,128)S(1)} %bitcast.4, f32[3,2048]{1,0:T(4,128)S(1)} %copy-done.2, f32[64,64]{1,0:T(8,128)S(1)} %copy-done.3), custom_call_target="tpu_custom_call" | custom-call | tf_op jit(solution)/shard_map/pallas_call | solution.py:218
  12.8 1.4 %shard_map.69 = (f32[64,2048]{1,0:T(8,128)S(1)}, f32[64,512]{1,0:T(8,128)S(1)}, f32[64,256]{1,0:T(8,128)S(1)}) custom-call(f32[64,2048]{1,0:T(8,128)S(1)} %get-tuple-element.31.field_ref, f32[64,512]{1,0:T(8,128)S(1)} %collective-permute-done.xb, f32[64,512]{1,0:T(8,128)S(1)} %collective-permute-done.1.xa, f32[64,128]{1,0:T(8,128)S(1)} %collective-permute-done.2.yb, ...), custom_call_target="tpu_custom_call" | custom-call | tf_op jit(solution)/shard_map/pallas_call | solution.py:218
  14.2 1.5 %collective-permute-start.4 = (f32[64,512]{1,0:T(8,128)S(1)}, f32[64,512]{1,0:T(8,128)S(1)}, u32[]{:S(2)}, u32[]{:S(2)}) collective-permute-start(f32[64,512]{1,0:T(8,128)S(1)} %get-tuple-element.39), channel_id=1, source_target_pairs={{0,24},{8,0},{16,8},{24,16},{1,25},{9,1},{17,9},{25,17},{2,26},{10... | collective-permute-start | bytes 393224 | tf_op jit(solution)/shard_map/ppermute | solution.py:494
  15.7 2.4 %collective-permute-start.5 = (f32[64,256]{1,0:T(8,128)S(1)}, f32[64,256]{1,0:T(8,128)S(1)}, u32[]{:S(2)}, u32[]{:S(2)}) collective-permute-start(f32[64,256]{1,0:T(8,128)S(1)} %get-tuple-element.40), channel_id=1, source_target_pairs={{0,7},{1,0},{2,1},{3,2},{4,3},{5,4},{6,5},{7,6},{8,15},{9,8},{10,9... | collective-permute-start | bytes 196616 | tf_op jit(solution)/shard_map/ppermute | solution.py:494
  18.1 1.9 %collective-permute-done.5.ya = f32[64,256]{1,0:T(8,128)S(1)} collective-permute-done((f32[64,256]{1,0:T(8,128)S(1)}, f32[64,256]{1,0:T(8,128)S(1)}, u32[]{:S(2)}, u32[]{:S(2)}) %collective-permute-start.5) | collective-permute-done | bytes 65568 | tf_op jit(solution)/shard_map/ppermute | solution.py:494
  20.0 1.4 %shard_map.70 = (f32[224,128]{1,0:T(8,128)S(1)}, f32[64,640]{1,0:T(8,128)S(1)}, f32[64,128]{1,0:T(8,128)S(1)}) custom-call(f32[64,2048]{1,0:T(8,128)S(1)} %get-tuple-element.38.field_ref, f32[64,512]{1,0:T(8,128)S(1)} %collective-permute-done.4.xa, f32[64,256]{1,0:T(8,128)S(1)} %collective-permute-done.5.ya, f32[64,1]{1,0:T(8,128)S(1)} %get-tuple-element.41.mean_ref), custom_call_target="tpu_custom_call" | custom-call | tf_op jit(solution)/shard_map/pallas_call | solution.py:218
  23.9 2.1 %collective-permute-start.9 = (f32[112,128]{1,0:T(8,128)S(1)}, f32[112,128]{1,0:T(8,128)S(1)}, u32[]{:S(2)}, u32[]{:S(2)}) collective-permute-start(f32[112,128]{1,0:T(8,128)S(1)} %slice_select_fusion.1), channel_id=1, source_target_pairs={{0,24},{1,25},{2,26},{3,27},{4,28},{5,29},{6,30},{7,31},{8,16},{9,... | collective-permute-start | bytes 172040 | tf_op jit(solution)/shard_map/ppermute | solution.py:465
  27.1 2.3 %collective-permute-done.9 = f32[112,128]{1,0:T(8,128)S(1)} collective-permute-done((f32[112,128]{1,0:T(8,128)S(1)}, f32[112,128]{1,0:T(8,128)S(1)}, u32[]{:S(2)}, u32[]{:S(2)}) %collective-permute-start.9) | collective-permute-done | bytes 57376 | tf_op jit(solution)/shard_map/ppermute | solution.py:465
  30.2 1.4 %collective-permute-done.10.yb = f32[64,128]{1,0:T(8,128)S(1)} collective-permute-done((f32[64,128]{1,0:T(8,128)S(1)}, f32[64,128]{1,0:T(8,128)S(1)}, u32[]{:S(2)}, u32[]{:S(2)}) %collective-permute-start.10) | collective-permute-done | bytes 32800 | tf_op jit(solution)/shard_map/ppermute | solution.py:490
  31.5 2.3 %collective-permute-start.15 = (f32[112,128]{1,0:T(8,128)S(1)}, f32[112,128]{1,0:T(8,128)S(1)}, u32[]{:S(2)}, u32[]{:S(2)}) collective-permute-start(f32[112,128]{1,0:T(8,128)S(1)} %add_add_fusion.3), channel_id=1, source_target_pairs={{0,6},{1,7},{2,4},{3,5},{4,2},{5,3},{6,0},{7,1},{8,14},{9,15},{10,... | collective-permute-start | bytes 172040 | tf_op jit(solution)/shard_map/ppermute | solution.py:465
  33.8 2.1 %collective-permute-start.13 = (f32[112,128]{1,0:T(8,128)S(1)}, f32[112,128]{1,0:T(8,128)S(1)}, u32[]{:S(2)}, u32[]{:S(2)}) collective-permute-start(f32[112,128]{1,0:T(8,128)S(1)} %add_add_fusion.3), channel_id=1, source_target_pairs={{0,2},{1,3},{2,0},{3,1},{4,6},{5,7},{6,4},{7,5},{8,10},{9,11},{10,... | collective-permute-start | bytes 172040 | tf_op jit(solution)/shard_map/ppermute | solution.py:465
  35.9 1.8 %collective-permute-done.15 = f32[112,128]{1,0:T(8,128)S(1)} collective-permute-done((f32[112,128]{1,0:T(8,128)S(1)}, f32[112,128]{1,0:T(8,128)S(1)}, u32[]{:S(2)}, u32[]{:S(2)}) %collective-permute-start.15) | collective-permute-done | bytes 57376 | tf_op jit(solution)/shard_map/ppermute | solution.py:465
  37.7 1.5 %collective-permute-done.14 = f32[112,128]{1,0:T(8,128)S(1)} collective-permute-done((f32[112,128]{1,0:T(8,128)S(1)}, f32[112,128]{1,0:T(8,128)S(1)}, u32[]{:S(2)}, u32[]{:S(2)}) %collective-permute-start.14) | collective-permute-done | bytes 57376 | tf_op jit(solution)/shard_map/ppermute | solution.py:465
  40.7 1.9 %collective-permute-start.11 = (f32[64,640]{1,0:T(8,128)S(1)}, f32[64,640]{1,0:T(8,128)S(1)}, u32[]{:S(2)}, u32[]{:S(2)}) collective-permute-start(f32[64,640]{1,0:T(8,128)S(1)} %shard_map.71), channel_id=1, source_target_pairs={{0,24},{8,0},{16,8},{24,16},{1,25},{9,1},{17,9},{25,17},{2,26},{10... | collective-permute-start | bytes 491528 | tf_op jit(solution)/shard_map/ppermute | solution.py:494
  42.6 7.5 %shard_map.72 = (f32[64,512]{1,0:T(8,128)S(1)}, f32[64,1]{1,0:T(8,128)S(1)}, f32[64,1]{1,0:T(8,128)S(1)}, f32[64,2048]{1,0:T(8,128)S(1)}, f32[64,64]{1,0:T(8,128)S(1)}, /*index=5*/f32[384,64]{1,0:T(8,128)S(1)}) custom-call(f32[224,128]{1,0:T(8,128)S(1)} %pad_maximum_fusion.sums_ref, f32[64,2048]{1,0:T(8,128)S(1)} %bitcast.5, ...), custom_call_target="tpu_custom_call" | custom-call | flops 1 | bytes 1 | tf_op jit(solution)/shard_map/pallas_call | solution.py:218
  50.1 3.3 %shard_map.73 = (f32[64,2048]{1,0:T(8,128)S(1)}, f32[224,128]{1,0:T(8,128)S(1)}) custom-call(f32[64,2048]{1,0:T(8,128)S(1)} %get-tuple-element.38.field_ref, f32[64,512]{1,0:T(8,128)S(1)} %collective-permute-done.4.xa, f32[64,256]{1,0:T(8,128)S(1)} %collective-permute-done.5.ya, f32[64,128]{1,0:T(8,128)S(1)} %collective-permute-done.10.yb, ...), custom_call_target="tpu_custom_call" | custom-call | tf_op jit(solution)/shard_map/pallas_call | solution.py:218
  55.8 1.3 %collective-permute-start.20 = (f32[112,128]{1,0:T(8,128)S(1)}, f32[112,128]{1,0:T(8,128)S(1)}, u32[]{:S(2)}, u32[]{:S(2)}) collective-permute-start(f32[112,128]{1,0:T(8,128)S(1)} %slice_select_fusion), channel_id=1, source_target_pairs={{0,24},{1,25},{2,26},{3,27},{4,28},{5,29},{6,30},{7,31},{8,16},{9,... | collective-permute-start | bytes 172040 | tf_op jit(solution)/shard_map/ppermute | solution.py:465
  59.1 2.2 %collective-permute-done.20 = f32[112,128]{1,0:T(8,128)S(1)} collective-permute-done((f32[112,128]{1,0:T(8,128)S(1)}, f32[112,128]{1,0:T(8,128)S(1)}, u32[]{:S(2)}, u32[]{:S(2)}) %collective-permute-start.20) | collective-permute-done | bytes 57376 | tf_op jit(solution)/shard_map/ppermute | solution.py:465
  61.3 2.0 %collective-permute-start.23 = (f32[112,128]{1,0:T(8,128)S(1)}, f32[112,128]{1,0:T(8,128)S(1)}, u32[]{:S(2)}, u32[]{:S(2)}) collective-permute-start(f32[112,128]{1,0:T(8,128)S(1)} %add_add_fusion.1), channel_id=1, source_target_pairs={{0,6},{1,7},{2,4},{3,5},{4,2},{5,3},{6,0},{7,1},{8,14},{9,15},{10,... | collective-permute-start | bytes 172040 | tf_op jit(solution)/shard_map/ppermute | solution.py:465
  63.9 1.8 %collective-permute-start.21 = (f32[112,128]{1,0:T(8,128)S(1)}, f32[112,128]{1,0:T(8,128)S(1)}, u32[]{:S(2)}, u32[]{:S(2)}) collective-permute-start(f32[112,128]{1,0:T(8,128)S(1)} %add_add_fusion.1), channel_id=1, source_target_pairs={{0,2},{1,3},{2,0},{3,1},{4,6},{5,7},{6,4},{7,5},{8,10},{9,11},{10,... | collective-permute-start | bytes 172040 | tf_op jit(solution)/shard_map/ppermute | solution.py:465
  65.8 1.9 %collective-permute-done.23 = f32[112,128]{1,0:T(8,128)S(1)} collective-permute-done((f32[112,128]{1,0:T(8,128)S(1)}, f32[112,128]{1,0:T(8,128)S(1)}, u32[]{:S(2)}, u32[]{:S(2)}) %collective-permute-start.23) | collective-permute-done | bytes 57376 | tf_op jit(solution)/shard_map/ppermute | solution.py:465
  70.2 8.7 %shard_map.74 = (f32[2048,64]{1,0:T(8,128)}, f32[64,64]{1,0:T(8,128)}, f32[64,2048]{1,0:T(8,128)}) custom-call(f32[224,128]{1,0:T(8,128)S(1)} %pad_maximum_fusion.1.sums_ref, f32[64,2048]{1,0:T(8,128)S(1)} %get-tuple-element.52.orient_ref, f32[64,64]{1,0:T(8,128)S(1)} %get-tuple-element.53.basis_ref, f32[384,64]{1,0:T(8,128)S(1)} %get-tuple-element.54.table_ref, ...), custom_call_target="tpu_custom_call" | custom-call | tf_op jit(solution)/shard_map/pallas_call | solution.py:218
  (54 shorter events, 17.2 us)
Async XLA Ops:
  2.3 9.3 %collective-permute-start = (f32[64,512]{1,0:T(8,128)S(1)}, f32[64,512]{1,0:T(8,128)S(1)}, u32[]{:S(2)}, u32[]{:S(2)}) collective-permute-start(f32[64,512]{1,0:T(8,128)S(1)} %get-tuple-element.32), channel_id=1, source_target_pairs={{0,8},{8,16},{16,24},{24,0},{1,9},{9,17},{17,25},{25,1},{2,10},{10... | collective-permute-start | bytes 393224 | tf_op jit(solution)/shard_map/ppermute | solution.py:490
  5.3 7.5 %collective-permute-start.1 = (f32[64,512]{1,0:T(8,128)S(1)}, f32[64,512]{1,0:T(8,128)S(1)}, u32[]{:S(2)}, u32[]{:S(2)}) collective-permute-start(f32[64,512]{1,0:T(8,128)S(1)} %get-tuple-element.33), channel_id=1, source_target_pairs={{0,24},{8,0},{16,8},{24,16},{1,25},{9,1},{17,9},{25,17},{2,26},{10... | collective-permute-start | bytes 393224 | tf_op jit(solution)/shard_map/ppermute | solution.py:494
  6.3 5.3 %collective-permute-start.2 = (f32[64,128]{1,0:T(8,128)S(1)}, f32[64,128]{1,0:T(8,128)S(1)}, u32[]{:S(2)}, u32[]{:S(2)}) collective-permute-start(f32[64,128]{1,0:T(8,128)S(1)} %get-tuple-element.34), channel_id=1, source_target_pairs={{0,1},{1,2},{2,3},{3,4},{4,5},{5,6},{6,7},{7,0},{8,9},{9,10},{10,1... | collective-permute-start | bytes 98312 | tf_op jit(solution)/shard_map/ppermute | solution.py:490
  6.3 5.3 %collective-permute-start.3 = (f32[64,128]{1,0:T(8,128)S(1)}, f32[64,128]{1,0:T(8,128)S(1)}, u32[]{:S(2)}, u32[]{:S(2)}) collective-permute-start(f32[64,128]{1,0:T(8,128)S(1)} %get-tuple-element.35), channel_id=1, source_target_pairs={{0,7},{1,0},{2,1},{3,2},{4,3},{5,4},{6,5},{7,6},{8,15},{9,8},{10,9... | collective-permute-start | bytes 98312 | tf_op jit(solution)/shard_map/ppermute | solution.py:494
  14.2 5.8 %collective-permute-start.4 = (f32[64,512]{1,0:T(8,128)S(1)}, f32[64,512]{1,0:T(8,128)S(1)}, u32[]{:S(2)}, u32[]{:S(2)}) collective-permute-start(f32[64,512]{1,0:T(8,128)S(1)} %get-tuple-element.39), channel_id=1, source_target_pairs={{0,24},{8,0},{16,8},{24,16},{1,25},{9,1},{17,9},{25,17},{2,26},{10... | collective-permute-start | bytes 393224 | tf_op jit(solution)/shard_map/ppermute | solution.py:494
  15.7 4.4 %collective-permute-start.5 = (f32[64,256]{1,0:T(8,128)S(1)}, f32[64,256]{1,0:T(8,128)S(1)}, u32[]{:S(2)}, u32[]{:S(2)}) collective-permute-start(f32[64,256]{1,0:T(8,128)S(1)} %get-tuple-element.40), channel_id=1, source_target_pairs={{0,7},{1,0},{2,1},{3,2},{4,3},{5,4},{6,5},{7,6},{8,15},{9,8},{10,9... | collective-permute-start | bytes 196616 | tf_op jit(solution)/shard_map/ppermute | solution.py:494
  21.4 1.4 %collective-permute-start.6 = (f32[224,128]{1,0:T(8,128)S(1)}, f32[224,128]{1,0:T(8,128)S(1)}, u32[]{:S(2)}, u32[]{:S(2)}) collective-permute-start(f32[224,128]{1,0:T(8,128)S(1)} %get-tuple-element.42), channel_id=1, source_target_pairs={{0,1},{1,0},{2,3},{3,2},{4,5},{5,4},{6,7},{7,6},{8,9},{9,8},{10,11... | collective-permute-start | bytes 344072 | tf_op jit(solution)/shard_map/ppermute | solution.py:465
  22.9 4.2 %collective-permute-start.8 = (f32[112,128]{1,0:T(8,128)S(1)}, f32[112,128]{1,0:T(8,128)S(1)}, u32[]{:S(2)}, u32[]{:S(2)}) collective-permute-start(f32[112,128]{1,0:T(8,128)S(1)} %slice_select_fusion.1), channel_id=1, source_target_pairs={{0,16},{1,17},{2,18},{3,19},{4,20},{5,21},{6,22},{7,23},{8,24},{9,... | collective-permute-start | bytes 172040 | tf_op jit(solution)/shard_map/ppermute | solution.py:465
  23.9 5.5 %collective-permute-start.9 = (f32[112,128]{1,0:T(8,128)S(1)}, f32[112,128]{1,0:T(8,128)S(1)}, u32[]{:S(2)}, u32[]{:S(2)}) collective-permute-start(f32[112,128]{1,0:T(8,128)S(1)} %slice_select_fusion.1), channel_id=1, source_target_pairs={{0,24},{1,25},{2,26},{3,27},{4,28},{5,29},{6,30},{7,31},{8,16},{9,... | collective-permute-start | bytes 172040 | tf_op jit(solution)/shard_map/ppermute | solution.py:465
  25.9 4.2 %collective-permute-start.7 = (f32[112,128]{1,0:T(8,128)S(1)}, f32[112,128]{1,0:T(8,128)S(1)}, u32[]{:S(2)}, u32[]{:S(2)}) collective-permute-start(f32[112,128]{1,0:T(8,128)S(1)} %slice_select_fusion.1), channel_id=1, source_target_pairs={{0,8},{1,9},{2,10},{3,11},{4,12},{5,13},{6,14},{7,15},{8,0},{9,1},... | collective-permute-start | bytes 172040 | tf_op jit(solution)/shard_map/ppermute | solution.py:465
  26.4 5.1 %collective-permute-start.10 = (f32[64,128]{1,0:T(8,128)S(1)}, f32[64,128]{1,0:T(8,128)S(1)}, u32[]{:S(2)}, u32[]{:S(2)}) collective-permute-start(f32[64,128]{1,0:T(8,128)S(1)} %get-tuple-element.43), channel_id=1, source_target_pairs={{0,1},{1,2},{2,3},{3,4},{4,5},{5,6},{6,7},{7,0},{8,9},{9,10},{10,1... | collective-permute-start | bytes 98312 | tf_op jit(solution)/shard_map/ppermute | solution.py:490
  31.5 6.1 %collective-permute-start.15 = (f32[112,128]{1,0:T(8,128)S(1)}, f32[112,128]{1,0:T(8,128)S(1)}, u32[]{:S(2)}, u32[]{:S(2)}) collective-permute-start(f32[112,128]{1,0:T(8,128)S(1)} %add_add_fusion.3), channel_id=1, source_target_pairs={{0,6},{1,7},{2,4},{3,5},{4,2},{5,3},{6,0},{7,1},{8,14},{9,15},{10,... | collective-permute-start | bytes 172040 | tf_op jit(solution)/shard_map/ppermute | solution.py:465
  33.8 5.4 %collective-permute-start.14 = (f32[112,128]{1,0:T(8,128)S(1)}, f32[112,128]{1,0:T(8,128)S(1)}, u32[]{:S(2)}, u32[]{:S(2)}) collective-permute-start(f32[112,128]{1,0:T(8,128)S(1)} %add_add_fusion.3), channel_id=1, source_target_pairs={{0,4},{1,5},{2,6},{3,7},{4,0},{5,1},{6,2},{7,3},{8,12},{9,13},{10,... | collective-permute-start | bytes 172040 | tf_op jit(solution)/shard_map/ppermute | solution.py:465
  33.8 5.4 %collective-permute-start.13 = (f32[112,128]{1,0:T(8,128)S(1)}, f32[112,128]{1,0:T(8,128)S(1)}, u32[]{:S(2)}, u32[]{:S(2)}) collective-permute-start(f32[112,128]{1,0:T(8,128)S(1)} %add_add_fusion.3), channel_id=1, source_target_pairs={{0,2},{1,3},{2,0},{3,1},{4,6},{5,7},{6,4},{7,5},{8,10},{9,11},{10,... | collective-permute-start | bytes 172040 | tf_op jit(solution)/shard_map/ppermute | solution.py:465
  39.2 3.3 %collective-permute-start.16 = (f32[112,128]{1,0:T(8,128)S(1)}, f32[112,128]{1,0:T(8,128)S(1)}, u32[]{:S(2)}, u32[]{:S(2)}) collective-permute-start(f32[112,128]{1,0:T(8,128)S(1)} %add_add_fusion.2), channel_id=1, source_target_pairs={{0,1},{1,0},{2,3},{3,2},{4,5},{5,4},{6,7},{7,6},{8,9},{9,8},{10,11... | collective-permute-start | bytes 172040 | tf_op jit(solution)/shard_map/ppermute | solution.py:465
  39.3 10.7 %collective-permute-start.12 = (f32[64,640]{1,0:T(8,128)S(1)}, f32[64,640]{1,0:T(8,128)S(1)}, u32[]{:S(2)}, u32[]{:S(2)}) collective-permute-start(f32[64,640]{1,0:T(8,128)S(1)} %get-tuple-element.45), channel_id=1, source_target_pairs={{0,8},{8,16},{16,24},{24,0},{1,9},{9,17},{17,25},{25,1},{2,10},{10... | collective-permute-start | bytes 491528 | tf_op jit(solution)/shard_map/ppermute | solution.py:490
  40.7 9.4 %collective-permute-start.11 = (f32[64,640]{1,0:T(8,128)S(1)}, f32[64,640]{1,0:T(8,128)S(1)}, u32[]{:S(2)}, u32[]{:S(2)}) collective-permute-start(f32[64,640]{1,0:T(8,128)S(1)} %shard_map.71), channel_id=1, source_target_pairs={{0,24},{8,0},{16,8},{24,16},{1,25},{9,1},{17,9},{25,17},{2,26},{10... | collective-permute-start | bytes 491528 | tf_op jit(solution)/shard_map/ppermute | solution.py:494
  53.4 1.4 %collective-permute-start.17 = (f32[224,128]{1,0:T(8,128)S(1)}, f32[224,128]{1,0:T(8,128)S(1)}, u32[]{:S(2)}, u32[]{:S(2)}) collective-permute-start(f32[224,128]{1,0:T(8,128)S(1)} %get-tuple-element.51), channel_id=1, source_target_pairs={{0,1},{1,0},{2,3},{3,2},{4,5},{5,4},{6,7},{7,6},{8,9},{9,8},{10,11... | collective-permute-start | bytes 344072 | tf_op jit(solution)/shard_map/ppermute | solution.py:465
  54.8 4.2 %collective-permute-start.19 = (f32[112,128]{1,0:T(8,128)S(1)}, f32[112,128]{1,0:T(8,128)S(1)}, u32[]{:S(2)}, u32[]{:S(2)}) collective-permute-start(f32[112,128]{1,0:T(8,128)S(1)} %slice_select_fusion), channel_id=1, source_target_pairs={{0,16},{1,17},{2,18},{3,19},{4,20},{5,21},{6,22},{7,23},{8,24},{9,... | collective-permute-start | bytes 172040 | tf_op jit(solution)/shard_map/ppermute | solution.py:465
  55.8 5.5 %collective-permute-start.20 = (f32[112,128]{1,0:T(8,128)S(1)}, f32[112,128]{1,0:T(8,128)S(1)}, u32[]{:S(2)}, u32[]{:S(2)}) collective-permute-start(f32[112,128]{1,0:T(8,128)S(1)} %slice_select_fusion), channel_id=1, source_target_pairs={{0,24},{1,25},{2,26},{3,27},{4,28},{5,29},{6,30},{7,31},{8,16},{9,... | collective-permute-start | bytes 172040 | tf_op jit(solution)/shard_map/ppermute | solution.py:465
  57.1 4.2 %collective-permute-start.18 = (f32[112,128]{1,0:T(8,128)S(1)}, f32[112,128]{1,0:T(8,128)S(1)}, u32[]{:S(2)}, u32[]{:S(2)}) collective-permute-start(f32[112,128]{1,0:T(8,128)S(1)} %slice_select_fusion), channel_id=1, source_target_pairs={{0,8},{1,9},{2,10},{3,11},{4,12},{5,13},{6,14},{7,15},{8,0},{9,1},... | collective-permute-start | bytes 172040 | tf_op jit(solution)/shard_map/ppermute | solution.py:465
  61.3 6.3 %collective-permute-start.23 = (f32[112,128]{1,0:T(8,128)S(1)}, f32[112,128]{1,0:T(8,128)S(1)}, u32[]{:S(2)}, u32[]{:S(2)}) collective-permute-start(f32[112,128]{1,0:T(8,128)S(1)} %add_add_fusion.1), channel_id=1, source_target_pairs={{0,6},{1,7},{2,4},{3,5},{4,2},{5,3},{6,0},{7,1},{8,14},{9,15},{10,... | collective-permute-start | bytes 172040 | tf_op jit(solution)/shard_map/ppermute | solution.py:465
  63.3 5.6 %collective-permute-start.22 = (f32[112,128]{1,0:T(8,128)S(1)}, f32[112,128]{1,0:T(8,128)S(1)}, u32[]{:S(2)}, u32[]{:S(2)}) collective-permute-start(f32[112,128]{1,0:T(8,128)S(1)} %add_add_fusion.1), channel_id=1, source_target_pairs={{0,4},{1,5},{2,6},{3,7},{4,0},{5,1},{6,2},{7,3},{8,12},{9,13},{10,... | collective-permute-start | bytes 172040 | tf_op jit(solution)/shard_map/ppermute | solution.py:465
  63.9 4.9 %collective-permute-start.21 = (f32[112,128]{1,0:T(8,128)S(1)}, f32[112,128]{1,0:T(8,128)S(1)}, u32[]{:S(2)}, u32[]{:S(2)}) collective-permute-start(f32[112,128]{1,0:T(8,128)S(1)} %add_add_fusion.1), channel_id=1, source_target_pairs={{0,2},{1,3},{2,0},{3,1},{4,6},{5,7},{6,4},{7,5},{8,10},{9,11},{10,... | collective-permute-start | bytes 172040 | tf_op jit(solution)/shard_map/ppermute | solution.py:465
  (5 other events, 26.5 us)

commit v4 on v3

--- a/solution.py
+++ b/solution.py
@@ -34,11 +34,15 @@
     return high, (value - high.astype(jnp.float32)).astype(half)
 
 
+def stacked(pairs, axis=0):
+    return tuple(jnp.concatenate(part, axis=axis) for part in zip(*pairs))
+
+
 def three(left, right, contract):
-    left_high, left_low = halves(left)
-    right_high, right_low = halves(right)
-    rows = left.shape[0]
-    both = dot(jnp.concatenate([left_high, left_low], axis=0), right_high, contract)
+    left_high, left_low = left
+    right_high, right_low = right
+    rows = left_high.shape[0]
+    both = dot(jnp.concatenate(left, axis=0), right_high, contract)
     return both[:rows] + both[rows:] + dot(left_high, right_low, contract)
 
 
@@ -154,8 +158,8 @@
     fields = [wide] if beside is None else [wide, beside * scale_column]
     fields = [[f[b * group:(b + 1) * group] for b in range(blocks)] for f in fields]
     rows = fields[0]
+    done = [list(f) for f in fields]
     place = lax.broadcasted_iota(jnp.int32, shape, 0)
-    lane = lax.broadcasted_iota(jnp.int32, shape, 1)
 
     def spread(value, i):
         return jnp.broadcast_to(value[i:i + 1], value.shape)
@@ -169,6 +173,15 @@
         for j in range(0, group, 2):
             first, second = cols[b][j], cols[b][j + 1]
             p, o, q = spread(first, j), spread(second, j), spread(second, j + 1)
+            root = lax.rsqrt(p)
+            along = o * root
+            root_next = lax.rsqrt(q - along * along)
+            for f, out in zip(fields, done):
+                width = f[b].shape[1]
+                upper = spread(f[b], j) * root[:, :width]
+                lower = (spread(f[b], j + 1) - along[:, :width] * upper) * root_next[:, :width]
+                at = place[:, :width]
+                out[b] = jnp.where(at == j, upper, jnp.where(at == j + 1, lower, out[b]))
             over = 1.0 / (p * q - o * o)
             p, o, q = p * over, o * over, q * over
 
@@ -195,17 +208,6 @@
                     f[c] = f[c] - left[:, :width] * up - right[:, :width] * low
         if b < len(meanwhile):
             meanwhile[b]()
-    done = [[] for _ in fields]
-    for b, block in enumerate(rows):
-        at = place + b * group
-        pivot = jnp.sum(jnp.where(lane == at, block, 0.0), axis=1, keepdims=True)
-        under = jnp.sum(jnp.where((lane == at - 1) & (place % 2 == 1), block, 0.0), axis=1, keepdims=True)
-        pivot = jnp.broadcast_to(pivot, shape)
-        part = under / pltpu.roll(pivot, 1, axis=0)
-        root = lax.rsqrt(pivot - part * under)
-        for f, out in zip(fields, done):
-            width = f[b].shape[1]
-            out.append((f[b] - part[:, :width] * pltpu.roll(f[b], 1, axis=0)) * root[:, :width])
     done = [jnp.concatenate(d, axis=0) for d in done]
     both = done[0] * jnp.concatenate([diag_row * scale, scale], axis=1)
     return (both[:, :rank], both[:, rank:], *done[1:])
@@ -241,69 +243,134 @@
     weight_ref[...], column_ref[...] = stage_weights(unit(mean.shape[0]), table, mean, s_ref[...].T)
 
 
-def weighted(weights, rank):
-    w_high, w_low = halves(weights)
-    w_both = jnp.concatenate([w_high, w_low], axis=0)
-
-    def product(stack):
-        high, low = halves(jnp.concatenate(stack, axis=0))
-        wide = dot(w_both, high)
-        return wide[:rank] + wide[rank:] + dot(w_high, low)
-
-    return product
+CENTRE, X_BEHIND, X_AHEAD, Y_BEHIND, Y_AHEAD, Z_BEHIND, Z_AHEAD = range(7)
+
+
+def triple(value):
+    high, low = halves(value)
+    return jnp.concatenate([high, low, high], axis=0)
+
+
+class Weights:
+    def __init__(self, weights, column):
+        self.column = column
+        self.rank = rank = column.shape[0]
+        blocks = [weights[:, n * rank:(n + 1) * rank] for n in range(8)]
+        high, low = halves(jnp.concatenate(blocks, axis=0))
+        self.left = jnp.concatenate([high, high, low], axis=1)
+
+    def times(self, value, start=CENTRE, stop=Z_AHEAD + 1):
+        rank = self.rank
+        flux = triple(speed_of(self.column, value) * value)
+        wide = dot(self.left[(1 + start) * rank:(1 + stop) * rank], flux)
+        return {n: wide[(n - start) * rank:(n - start + 1) * rank] for n in range(start, stop)}
+
+    def one(self, value, n):
+        return self.times(value, n, n + 1)[n]
+
+    def whole(self, value, part, dims):
+        return (
+            dot(self.left[:self.rank], triple(value)) + part[CENTRE]
+            + z_behind(part[Z_BEHIND], dims) + z_ahead(part[Z_AHEAD], dims)
+        )
+
+
+def k_edges(dims, field, weights, column, xb, xa, yb, ya):
+    lx, ly, lz = dims
+    width = lx * lz
+    w = Weights(weights, column)
+    slabs = slabs_of(field, dims)
+    from_behind, from_ahead = w.one(xb, X_BEHIND), w.one(xa, X_AHEAD)
+    before = w.one(yb, Y_BEHIND)
+    part = w.times(slabs[0])
+    first = (
+        w.whole(slabs[0], part, dims) + from_behind + w.one(slabs[1], X_AHEAD)
+        + y_behind(part[Y_BEHIND], before, dims)
+        + y_ahead(part[Y_AHEAD], roll(w.one(ya, Y_AHEAD), -lz), dims)
+    )
+    layers = jnp.concatenate([y_layer(slabs, dims, 0), y_layer(slabs, dims, 1)], axis=1)
+    part = w.times(layers)
+    after = w.one(y_layer(slabs, dims, 2), Y_AHEAD)
+    lane = lane_index(width)
+    over_y = [before + part[Y_AHEAD][:, width:], part[Y_BEHIND][:, :width] + after]
+    over_x = []
+    for n in range(2):
+        here = slice(n * width, (n + 1) * width)
+        over_x.append(
+            jnp.where(lane < lz, roll(from_behind[:, :width], -n * lz), roll(part[X_BEHIND][:, here], lz))
+            + jnp.where(
+                lane >= width - lz, roll(from_ahead[:, :width], -(n + 1) * lz), roll(part[X_AHEAD][:, here], -lz)
+            )
+        )
+    return first, w.whole(layers, part, dims) + jnp.concatenate([x + y for x, y in zip(over_x, over_y)], axis=1)
 
 
 def k_stage(dims, field, weights, column, xb, xa, yb, ya, further=None):
     lx, ly, lz = dims
     slab, width = ly * lz, lx * lz
-
-    def flux_of(value):
-        return speed_of(column, value) * value
-
-    product = weighted(weights, column.shape[0])
-    fields = slabs_of(field, dims) + [xa]
-    flux = [flux_of(f) for f in fields]
-    before, layer, layer_before = flux_of(xb), flux_of(ya), flux_of(yb)
+    w = Weights(weights, column)
+    fields = slabs_of(field, dims)
     if further is not None:
-        second, corner_before, layer_next = [flux_of(f) for f in further]
-        corners = second[:, slab:]
-        corner_after = roll(corners, -2 * lz)
-        flux.append(second[:, :slab])
-    flux.append(before)
+        fields.append(xa)
+        second, corner_before, layer_next = further
+        last = w.one(second[:, :slab], X_AHEAD)
+    else:
+        last = w.one(xa, X_AHEAD)
+    parts = [w.times(f) for f in fields]
+    from_behind = [w.one(xb, X_BEHIND)] + [p[X_BEHIND] for p in parts[:-1]]
+    from_ahead = [p[X_AHEAD] for p in parts[1:]] + [last]
+    layer_before = w.one(yb, Y_BEHIND)
+    if further is None:
+        layer = {Y_AHEAD: w.one(ya, Y_AHEAD)}
+    else:
+        layer = w.times(ya)
+        corners = w.times(second[:, slab:], X_AHEAD, Y_AHEAD + 1)
+
     results = []
-    for x in range(lx if further is None else lx + 1):
-        g = flux[x]
-        line_before = roll(layer_before, -lz * x) if x < lx else corners
-        line_after = roll(layer, -lz * (x + 1)) if x < lx else corner_after
-        results.append(product([
-            fields[x], g, flux[x - 1], flux[x + 1],
-            y_behind(g, line_before, dims), y_ahead(g, line_after, dims), z_behind(g, dims), z_ahead(g, dims),
-        ]))
+    for x, value in enumerate(fields):
+        line_before = roll(layer_before, -lz * x) if x < lx else corners[Y_BEHIND]
+        line_after = roll(layer[Y_AHEAD], -lz * (x + 1)) if x < lx else roll(corners[Y_AHEAD], -2 * lz)
+        results.append(
+            w.whole(value, parts[x], dims) + from_behind[x] + from_ahead[x]
+            + y_behind(parts[x][Y_BEHIND], line_before, dims) + y_ahead(parts[x][Y_AHEAD], line_after, dims)
+        )
     if further is None:
         return results
     lane = lane_index(width)
-    side = product([
-        ya, layer,
-        jnp.where(lane < lz, roll(corner_before, lz), roll(layer, lz)),
-        jnp.where(lane >= width - lz, corner_after, roll(layer, -lz)),
-        y_layer(flux[:lx], dims, ly - 1), layer_next, z_behind(layer, dims), z_ahead(layer, dims),
-    ])
+    side = (
+        w.whole(ya, layer, dims)
+        + jnp.where(lane < lz, roll(w.one(corner_before, X_BEHIND), lz), roll(layer[X_BEHIND], lz))
+        + jnp.where(lane >= width - lz, roll(corners[X_AHEAD], -2 * lz), roll(layer[X_AHEAD], -lz))
+        + y_layer([p[Y_BEHIND] for p in parts[:lx]], dims, ly - 1) + w.one(layer_next, Y_AHEAD)
+    )
     return results, side
 
 
-def galerkin(dims, fields, layer, mean):
+def pair_sums(left, right, q):
+    return three(halves(left), stacked([halves(right), q]), (1, 1))
+
+
+def inner_sums(dims, fields, layer, mean):
     lx, ly, lz = dims
     rank = mean.shape[0]
     speeds = [speed_of(mean, f) for f in fields]
+    split = [halves(f) for f in fields]
     sums = [jnp.zeros((rank, 2 * rank), jnp.float32) for _ in range(4)]
     for x in range(lx):
         k = fields[x]
-        q = speeds[x] * k
-        pairs = [(k, k), (fields[x + 1], speeds[x + 1] * k)]
-        for moved in (y_ahead(k, roll(layer, -lz * (x + 1)), dims), z_ahead(k, dims)):
-            pairs.append((moved, speed_of(mean, moved) * k))
-        for n, (left, right) in enumerate(pairs):
-            sums[n] = sums[n] + three(left, jnp.concatenate([right, q], axis=0), (1, 1))
+        q = halves(speeds[x] * k)
+        pairs = [(0, split[x], split[x])]
+        if x + 1 < len(fields):
+            pairs.append((1, split[x + 1], halves(speeds[x + 1] * k)))
+        for n, moved in ((2, y_ahead(k, roll(layer, -lz * (x + 1)), dims)), (3, z_ahead(k, dims))):
+            pairs.append((n, halves(moved), halves(speed_of(mean, moved) * k)))
+        for n, left, right in pairs:
+            sums[n] = sums[n] + three(left, stacked([right, q]), (1, 1))
+    return sums
+
+
+def packed_sums(sums):
+    rank = sums[0].shape[0]
     low = lane_index(2 * rank) < rank
     centre = jnp.where(low, -roll(sums[0], rank), sums[0])
     gram = sums[0][:, :rank]
@@ -319,25 +386,35 @@
         ref[:, x * slab:(x + 1) * slab] = value
 
 
-def first_kernel(dims, field_ref, xb, xa, yb, ya, weight_ref, column_ref, out_ref, first_ref, y_first_ref):
-    width = dims[0] * dims[2]
+def edge_kernel(dims, field_ref, xb, xa, yb, ya, weight_ref, column_ref, first_ref, y_first_ref):
+    first_ref[...], y_first_ref[...] = k_edges(
+        dims, field_ref[...], weight_ref[...], column_ref[...], xb[...], xa[...], yb[...], ya[...]
+    )
+
+
+def first_kernel(
+    dims, field_ref, xb, xa, yb, ya, weight_ref, column_ref, mean_ref, out_ref, sums_ref, last_ref, y_last_ref
+):
     slabs = k_stage(
         dims, field_ref[...], weight_ref[...], column_ref[...], xb[...], xa[...], yb[...], ya[...]
     )
     write_slabs(out_ref, slabs)
-    first_ref[...] = slabs[0]
-    y_first_ref[:, :width], y_first_ref[:, width:] = y_layer(slabs, dims, 0), y_layer(slabs, dims, 1)
-
-
-def galerkin_kernel(dims, field_ref, xa, ya, mean_ref, sums_ref, up_ref, y_last_ref):
-    lx, ly, lz = dims
-    slab, width = ly * lz, lx * lz
-    slabs = slabs_of(field_ref[...], dims)
+    last_ref[...], y_last_ref[...] = slabs[-1], y_layer(slabs, dims, dims[1] - 1)
+    none = jnp.zeros(y_last_ref.shape, jnp.float32)
+    sums_ref[...] = jnp.concatenate(inner_sums(dims, slabs, none, mean_ref[...]), axis=0)
+
+
+def face_kernel(dims, sums_ref, last_ref, y_last_ref, xa, ya, mean_ref, part_ref, up_ref):
+    slab, width = dims[1] * dims[2], dims[0] * dims[2]
+    mean = mean_ref[...]
+    rank = mean.shape[0]
     layer = ya[:, :width]
-    sums_ref[...] = galerkin(dims, slabs + [xa[...]], layer, mean_ref[...])
-    up_ref[:, :slab] = slabs[-1]
+    sums = [sums_ref[n * rank:(n + 1) * rank] for n in range(4)]
+    for n, moved, k in ((1, xa[...], last_ref[...]), (2, layer, y_last_ref[...])):
+        sums[n] = sums[n] + pair_sums(moved, speed_of(mean, moved) * k, halves(speed_of(mean, k) * k))
+    part_ref[...] = packed_sums(sums)
+    up_ref[:, :slab] = last_ref[...]
     up_ref[:, slab:] = layer
-    y_last_ref[...] = y_layer(slabs, dims, ly - 1)
 
 
 def pack_kernel(dims, field_ref, ya, yb, down_ref):
@@ -407,7 +484,7 @@
         (second[...], behind[:, slab:], ya[:, width:]),
     )
     write_slabs(field_out, slabs[:-1])
-    sums_out[...] = galerkin(dims, slabs, side, mean_ref[...])
+    sums_out[...] = packed_sums(inner_sums(dims, slabs, side, mean_ref[...]))
 
 
 def last_kernel(
@@ -433,8 +510,9 @@
             copies[n].start()
         return work
 
+    new_halves = halves(new)
     upper_v, inverse_v = factor(
-        three(new, new, (1, 1)) * (1.0 / count), meanwhile=[x_part(n) for n in range(parts)]
+        three(new_halves, new_halves, (1, 1)) * (1.0 / count), meanwhile=[x_part(n) for n in range(parts)]
     )
     s_ref[...] = upper_v.T
     v_ref[...] = apply(inverse_v, new)
@@ -514,12 +592,15 @@
     table, mean, weights, column = call(
         table_kernel, [basis[1], column_shape, weight_shape, column_shape], orient, directions, coupling
     )
-    field, first, y_first = call(
-        functools.partial(first_kernel, dims), [whole, slab, two_layers], field, xb, xa, yb, ya, weights, column
-    )
+    near = (field, xb, xa, yb, ya, weights, column)
+    first, y_first = call(functools.partial(edge_kernel, dims), [slab, two_layers], *near)
     xa, ya = down(first, "gx"), down(y_first, "gy")
-    part, behind, y_last = call(
-        functools.partial(galerkin_kernel, dims), [summed, more, layer], field, xa, ya, mean
+    field, part, last, y_last = call(
+        functools.partial(first_kernel, dims), [whole, (4 * rank, 2 * rank), slab, layer], *near, mean,
+        cost=pl.CostEstimate(flops=10**9, bytes_accessed=8 * 10**6, transcendentals=0),
+    )
+    part, behind = call(
+        functools.partial(face_kernel, dims), [summed, more], part, last, y_last, xa, ya, mean
     )
     yb, behind = up(y_last, "gy"), up(behind, "gx")
     halo = {"yb": yb, "behind": behind}

time: 79.3 us -> 77.4 us (0.976)
  waiting for transfers between devices: 21.3 us -> 19.2 us
    ppermute x5, waiting for transfers between devices: 3.09 us -> 1.19 us  [down(): return lax.ppermute(value, axis, shifted(axis, False))]
    ppermute x16, waiting for transfers between devices: 16.8 us -> 16 us  [swapped(): lax.ppermute(value, ('gx', 'gy'), [(i, i ^ bits) for i in range(count)])]
    pallas_call x8 -> x9, Pallas kernels: 24.5 us -> 24.7 us  [call(): pl.pallas_call(body, out_shape=[jax.ShapeDtypeStruct(shape, jnp.float32)...]
  transfers between devices with their start and end apart: 25 -> 25, of which waited for: 15 -> 15; matrix products, arithmetic and copies ran while one was open for 0% -> 0% of each run, Pallas kernels for 12% -> 15%
where the time goes in v4:
time: 77.4 us; the launch traced here: 77.2 us
  starting transfers between devices  30.9 us (40%)
  Pallas kernels  24.7 us (32%)
  waiting for transfers between devices  19.2 us (25%)
  local copies, waits for them, and re-layouts  1.23 us (2%)
  between operations  1.02 us (1%)
    pallas_call x9, Pallas kernels, call(): pl.pallas_call(body, out_shape=[jax.ShapeDtypeStruct(shape, jnp.float32)...  24.7 us
    ppermute x16, starting transfers between devices, swapped(): lax.ppermute(value, ('gx', 'gy'), [(i, i ^ bits) for i in range(count)])  16.2 us
    ppermute x16, waiting for transfers between devices, swapped(): lax.ppermute(value, ('gx', 'gy'), [(i, i ^ bits) for i in range(count)])  16 us
    ppermute x5, starting transfers between devices, down(): return lax.ppermute(value, axis, shifted(axis, False))  11 us
    ppermute x4, starting transfers between devices, up(): return lax.ppermute(value, axis, shifted(axis, True))  3.69 us
    ppermute x4, waiting for transfers between devices, up(): return lax.ppermute(value, axis, shifted(axis, True))  2.08 us
  transfers between devices with their start and end apart: 25, of which 15 were waited for; matrix products, arithmetic and copies ran while one was open for 0% of the time, Pallas kernels for 15%

profile of v4, /device:TPU:0, one launch (start us, length us, event | category | flops | bytes accessed | tf_op | source)
XLA Modules:
  0.0 77.2 jit_solution(15820148768249347048)
XLA Ops:
  2.3 3.0 %collective-permute-start = (f32[64,512]{1,0:T(8,128)S(1)}, f32[64,512]{1,0:T(8,128)S(1)}, u32[]{:S(2)}, u32[]{:S(2)}) collective-permute-start(f32[64,512]{1,0:T(8,128)S(1)} %get-tuple-element.34), channel_id=1, source_target_pairs={{0,8},{8,16},{16,24},{24,0},{1,9},{9,17},{17,25},{25,1},{2,10},{10... | collective-permute-start | bytes 393224 | tf_op jit(solution)/shard_map/ppermute | solution.py:568
  6.3 3.5 %collective-permute-start.3 = (f32[64,128]{1,0:T(8,128)S(1)}, f32[64,128]{1,0:T(8,128)S(1)}, u32[]{:S(2)}, u32[]{:S(2)}) collective-permute-start(f32[64,128]{1,0:T(8,128)S(1)} %get-tuple-element.37), channel_id=1, source_target_pairs={{0,7},{1,0},{2,1},{3,2},{4,3},{5,4},{6,5},{7,6},{8,15},{9,8},{10,9... | collective-permute-start | bytes 98312 | tf_op jit(solution)/shard_map/ppermute | solution.py:572
  9.8 1.7 %shard_map.68 = (f32[384,64]{1,0:T(8,128)S(1)}, f32[64,1]{1,0:T(8,128)S(1)}, f32[64,512]{1,0:T(8,128)S(1)}, f32[64,1]{1,0:T(8,128)S(1)}) custom-call(f32[64,2048]{1,0:T(8,128)S(1)} %bitcast.4, f32[3,2048]{1,0:T(4,128)S(1)} %copy-done.2, f32[64,64]{1,0:T(8,128)S(1)} %copy-done.3), custom_call_target="tpu_custom_call" | custom-call | tf_op jit(solution)/shard_map/pallas_call | solution.py:220
  13.5 1.5 %collective-permute-start.4 = (f32[64,512]{1,0:T(8,128)S(1)}, f32[64,512]{1,0:T(8,128)S(1)}, u32[]{:S(2)}, u32[]{:S(2)}) collective-permute-start(f32[64,512]{1,0:T(8,128)S(1)} %get-tuple-element.42), channel_id=1, source_target_pairs={{0,24},{8,0},{16,8},{24,16},{1,25},{9,1},{17,9},{25,17},{2,26},{10... | collective-permute-start | bytes 393224 | tf_op jit(solution)/shard_map/ppermute | solution.py:572
  15.0 2.4 %collective-permute-start.5 = (f32[64,256]{1,0:T(8,128)S(1)}, f32[64,256]{1,0:T(8,128)S(1)}, u32[]{:S(2)}, u32[]{:S(2)}) collective-permute-start(f32[64,256]{1,0:T(8,128)S(1)} %get-tuple-element.43), channel_id=1, source_target_pairs={{0,7},{1,0},{2,1},{3,2},{4,3},{5,4},{6,5},{7,6},{8,15},{9,8},{10,9... | collective-permute-start | bytes 196616 | tf_op jit(solution)/shard_map/ppermute | solution.py:572
  17.5 2.6 %shard_map.69 = (f32[64,2048]{1,0:T(8,128)S(1)}, f32[256,128]{1,0:T(8,128)S(1)}, f32[64,512]{1,0:T(8,128)S(1)}, f32[64,128]{1,0:T(8,128)S(1)}) custom-call(f32[64,2048]{1,0:T(8,128)S(1)} %get-tuple-element.33.field_ref, f32[64,512]{1,0:T(8,128)S(1)} %collective-permute-done.xb, f32[64,512]{1,0:T(8,128)S(1)} %collective-permute-done.1.xa, ...), custom_call_target="tpu_custom_call" | custom-call | flops 1000000000 | bytes 8000000 | tf_op jit(solution)/shard_map/pallas_call | solution.py:220
  20.5 1.3 %collective-permute-done.6 = f32[224,128]{1,0:T(8,128)S(1)} collective-permute-done((f32[224,128]{1,0:T(8,128)S(1)}, f32[224,128]{1,0:T(8,128)S(1)}, u32[]{:S(2)}, u32[]{:S(2)}) %collective-permute-start.6) | collective-permute-done | bytes 114720 | tf_op jit(solution)/shard_map/ppermute | solution.py:543
  22.9 1.4 %collective-permute-start.9 = (f32[112,128]{1,0:T(8,128)S(1)}, f32[112,128]{1,0:T(8,128)S(1)}, u32[]{:S(2)}, u32[]{:S(2)}) collective-permute-start(f32[112,128]{1,0:T(8,128)S(1)} %slice_select_fusion.1), channel_id=1, source_target_pairs={{0,24},{1,25},{2,26},{3,27},{4,28},{5,29},{6,30},{7,31},{8,16},{9,... | collective-permute-start | bytes 172040 | tf_op jit(solution)/shard_map/ppermute | solution.py:543
  26.1 2.1 %collective-permute-done.9 = f32[112,128]{1,0:T(8,128)S(1)} collective-permute-done((f32[112,128]{1,0:T(8,128)S(1)}, f32[112,128]{1,0:T(8,128)S(1)}, u32[]{:S(2)}, u32[]{:S(2)}) %collective-permute-start.9) | collective-permute-done | bytes 57376 | tf_op jit(solution)/shard_map/ppermute | solution.py:543
  28.5 2.1 %collective-permute-done.10.yb = f32[64,128]{1,0:T(8,128)S(1)} collective-permute-done((f32[64,128]{1,0:T(8,128)S(1)}, f32[64,128]{1,0:T(8,128)S(1)}, u32[]{:S(2)}, u32[]{:S(2)}) %collective-permute-start.10) | collective-permute-done | bytes 32800 | tf_op jit(solution)/shard_map/ppermute | solution.py:568
  30.5 1.6 %collective-permute-start.15 = (f32[112,128]{1,0:T(8,128)S(1)}, f32[112,128]{1,0:T(8,128)S(1)}, u32[]{:S(2)}, u32[]{:S(2)}) collective-permute-start(f32[112,128]{1,0:T(8,128)S(1)} %add_add_fusion.3), channel_id=1, source_target_pairs={{0,6},{1,7},{2,4},{3,5},{4,2},{5,3},{6,0},{7,1},{8,14},{9,15},{10,... | collective-permute-start | bytes 172040 | tf_op jit(solution)/shard_map/ppermute | solution.py:543
  32.1 2.8 %collective-permute-start.13 = (f32[112,128]{1,0:T(8,128)S(1)}, f32[112,128]{1,0:T(8,128)S(1)}, u32[]{:S(2)}, u32[]{:S(2)}) collective-permute-start(f32[112,128]{1,0:T(8,128)S(1)} %add_add_fusion.3), channel_id=1, source_target_pairs={{0,2},{1,3},{2,0},{3,1},{4,6},{5,7},{6,4},{7,5},{8,10},{9,11},{10,... | collective-permute-start | bytes 172040 | tf_op jit(solution)/shard_map/ppermute | solution.py:543
  34.9 2.2 %collective-permute-done.15 = f32[112,128]{1,0:T(8,128)S(1)} collective-permute-done((f32[112,128]{1,0:T(8,128)S(1)}, f32[112,128]{1,0:T(8,128)S(1)}, u32[]{:S(2)}, u32[]{:S(2)}) %collective-permute-start.15) | collective-permute-done | bytes 57376 | tf_op jit(solution)/shard_map/ppermute | solution.py:543
  39.0 2.5 %collective-permute-start.11 = (f32[64,640]{1,0:T(8,128)S(1)}, f32[64,640]{1,0:T(8,128)S(1)}, u32[]{:S(2)}, u32[]{:S(2)}) collective-permute-start(f32[64,640]{1,0:T(8,128)S(1)} %shard_map.72), channel_id=1, source_target_pairs={{0,24},{8,0},{16,8},{24,16},{1,25},{9,1},{17,9},{25,17},{2,26},{10... | collective-permute-start | bytes 491528 | tf_op jit(solution)/shard_map/ppermute | solution.py:572
  41.5 7.4 %shard_map.73 = (f32[64,512]{1,0:T(8,128)S(1)}, f32[64,1]{1,0:T(8,128)S(1)}, f32[64,1]{1,0:T(8,128)S(1)}, f32[64,2048]{1,0:T(8,128)S(1)}, f32[64,64]{1,0:T(8,128)S(1)}, /*index=5*/f32[384,64]{1,0:T(8,128)S(1)}) custom-call(f32[224,128]{1,0:T(8,128)S(1)} %pad_maximum_fusion.sums_ref, f32[64,2048]{1,0:T(8,128)S(1)} %bitcast.5, ...), custom_call_target="tpu_custom_call" | custom-call | flops 1 | bytes 1 | tf_op jit(solution)/shard_map/pallas_call | solution.py:220
  48.9 2.9 %shard_map.74 = (f32[64,2048]{1,0:T(8,128)S(1)}, f32[224,128]{1,0:T(8,128)S(1)}) custom-call(f32[64,2048]{1,0:T(8,128)S(1)} %get-tuple-element.41.field_ref, f32[64,512]{1,0:T(8,128)S(1)} %collective-permute-done.4.xa, f32[64,256]{1,0:T(8,128)S(1)} %collective-permute-done.5.ya, f32[64,128]{1,0:T(8,128)S(1)} %collective-permute-done.10.yb, ...), custom_call_target="tpu_custom_call" | custom-call | tf_op jit(solution)/shard_map/pallas_call | solution.py:220
  51.9 1.3 %collective-permute-done.17 = f32[224,128]{1,0:T(8,128)S(1)} collective-permute-done((f32[224,128]{1,0:T(8,128)S(1)}, f32[224,128]{1,0:T(8,128)S(1)}, u32[]{:S(2)}, u32[]{:S(2)}) %collective-permute-start.17) | collective-permute-done | bytes 114720 | tf_op jit(solution)/shard_map/ppermute | solution.py:543
  55.3 1.5 %collective-permute-start.18 = (f32[112,128]{1,0:T(8,128)S(1)}, f32[112,128]{1,0:T(8,128)S(1)}, u32[]{:S(2)}, u32[]{:S(2)}) collective-permute-start(f32[112,128]{1,0:T(8,128)S(1)} %slice_select_fusion), channel_id=1, source_target_pairs={{0,8},{1,9},{2,10},{3,11},{4,12},{5,13},{6,14},{7,15},{8,0},{9,1},... | collective-permute-start | bytes 172040 | tf_op jit(solution)/shard_map/ppermute | solution.py:543
  57.5 1.9 %collective-permute-done.20 = f32[112,128]{1,0:T(8,128)S(1)} collective-permute-done((f32[112,128]{1,0:T(8,128)S(1)}, f32[112,128]{1,0:T(8,128)S(1)}, u32[]{:S(2)}, u32[]{:S(2)}) %collective-permute-start.20) | collective-permute-done | bytes 57376 | tf_op jit(solution)/shard_map/ppermute | solution.py:543
  59.7 1.5 %collective-permute-start.23 = (f32[112,128]{1,0:T(8,128)S(1)}, f32[112,128]{1,0:T(8,128)S(1)}, u32[]{:S(2)}, u32[]{:S(2)}) collective-permute-start(f32[112,128]{1,0:T(8,128)S(1)} %add_add_fusion.1), channel_id=1, source_target_pairs={{0,6},{1,7},{2,4},{3,5},{4,2},{5,3},{6,0},{7,1},{8,14},{9,15},{10,... | collective-permute-start | bytes 172040 | tf_op jit(solution)/shard_map/ppermute | solution.py:543
  62.4 1.8 %collective-permute-start.21 = (f32[112,128]{1,0:T(8,128)S(1)}, f32[112,128]{1,0:T(8,128)S(1)}, u32[]{:S(2)}, u32[]{:S(2)}) collective-permute-start(f32[112,128]{1,0:T(8,128)S(1)} %add_add_fusion.1), channel_id=1, source_target_pairs={{0,2},{1,3},{2,0},{3,1},{4,6},{5,7},{6,4},{7,5},{8,10},{9,11},{10,... | collective-permute-start | bytes 172040 | tf_op jit(solution)/shard_map/ppermute | solution.py:543
  64.2 1.7 %collective-permute-done.23 = f32[112,128]{1,0:T(8,128)S(1)} collective-permute-done((f32[112,128]{1,0:T(8,128)S(1)}, f32[112,128]{1,0:T(8,128)S(1)}, u32[]{:S(2)}, u32[]{:S(2)}) %collective-permute-start.23) | collective-permute-done | bytes 57376 | tf_op jit(solution)/shard_map/ppermute | solution.py:543
  65.9 1.3 %collective-permute-done.22 = f32[112,128]{1,0:T(8,128)S(1)} collective-permute-done((f32[112,128]{1,0:T(8,128)S(1)}, f32[112,128]{1,0:T(8,128)S(1)}, u32[]{:S(2)}, u32[]{:S(2)}) %collective-permute-start.22) | collective-permute-done | bytes 57376 | tf_op jit(solution)/shard_map/ppermute | solution.py:543
  68.6 8.5 %shard_map.75 = (f32[2048,64]{1,0:T(8,128)}, f32[64,64]{1,0:T(8,128)}, f32[64,2048]{1,0:T(8,128)}) custom-call(f32[224,128]{1,0:T(8,128)S(1)} %pad_maximum_fusion.1.sums_ref, f32[64,2048]{1,0:T(8,128)S(1)} %get-tuple-element.56.orient_ref, f32[64,64]{1,0:T(8,128)S(1)} %get-tuple-element.57.basis_ref, f32[384,64]{1,0:T(8,128)S(1)} %get-tuple-element.58.table_ref, ...), custom_call_target="tpu_custom_call" | custom-call | tf_op jit(solution)/shard_map/pallas_call | solution.py:220
  (55 shorter events, 15.5 us)
Async XLA Ops:
  2.3 9.3 %collective-permute-start = (f32[64,512]{1,0:T(8,128)S(1)}, f32[64,512]{1,0:T(8,128)S(1)}, u32[]{:S(2)}, u32[]{:S(2)}) collective-permute-start(f32[64,512]{1,0:T(8,128)S(1)} %get-tuple-element.34), channel_id=1, source_target_pairs={{0,8},{8,16},{16,24},{24,0},{1,9},{9,17},{17,25},{25,1},{2,10},{10... | collective-permute-start | bytes 393224 | tf_op jit(solution)/shard_map/ppermute | solution.py:568
  5.3 7.5 %collective-permute-start.1 = (f32[64,512]{1,0:T(8,128)S(1)}, f32[64,512]{1,0:T(8,128)S(1)}, u32[]{:S(2)}, u32[]{:S(2)}) collective-permute-start(f32[64,512]{1,0:T(8,128)S(1)} %get-tuple-element.35), channel_id=1, source_target_pairs={{0,24},{8,0},{16,8},{24,16},{1,25},{9,1},{17,9},{25,17},{2,26},{10... | collective-permute-start | bytes 393224 | tf_op jit(solution)/shard_map/ppermute | solution.py:572
  6.3 5.3 %collective-permute-start.2 = (f32[64,128]{1,0:T(8,128)S(1)}, f32[64,128]{1,0:T(8,128)S(1)}, u32[]{:S(2)}, u32[]{:S(2)}) collective-permute-start(f32[64,128]{1,0:T(8,128)S(1)} %get-tuple-element.36), channel_id=1, source_target_pairs={{0,1},{1,2},{2,3},{3,4},{4,5},{5,6},{6,7},{7,0},{8,9},{9,10},{10,1... | collective-permute-start | bytes 98312 | tf_op jit(solution)/shard_map/ppermute | solution.py:568
  6.3 5.3 %collective-permute-start.3 = (f32[64,128]{1,0:T(8,128)S(1)}, f32[64,128]{1,0:T(8,128)S(1)}, u32[]{:S(2)}, u32[]{:S(2)}) collective-permute-start(f32[64,128]{1,0:T(8,128)S(1)} %get-tuple-element.37), channel_id=1, source_target_pairs={{0,7},{1,0},{2,1},{3,2},{4,3},{5,4},{6,5},{7,6},{8,15},{9,8},{10,9... | collective-permute-start | bytes 98312 | tf_op jit(solution)/shard_map/ppermute | solution.py:572
  13.5 6.5 %collective-permute-start.4 = (f32[64,512]{1,0:T(8,128)S(1)}, f32[64,512]{1,0:T(8,128)S(1)}, u32[]{:S(2)}, u32[]{:S(2)}) collective-permute-start(f32[64,512]{1,0:T(8,128)S(1)} %get-tuple-element.42), channel_id=1, source_target_pairs={{0,24},{8,0},{16,8},{24,16},{1,25},{9,1},{17,9},{25,17},{2,26},{10... | collective-permute-start | bytes 393224 | tf_op jit(solution)/shard_map/ppermute | solution.py:572
  15.0 5.0 %collective-permute-start.5 = (f32[64,256]{1,0:T(8,128)S(1)}, f32[64,256]{1,0:T(8,128)S(1)}, u32[]{:S(2)}, u32[]{:S(2)}) collective-permute-start(f32[64,256]{1,0:T(8,128)S(1)} %get-tuple-element.43), channel_id=1, source_target_pairs={{0,7},{1,0},{2,1},{3,2},{4,3},{5,4},{6,5},{7,6},{8,15},{9,8},{10,9... | collective-permute-start | bytes 196616 | tf_op jit(solution)/shard_map/ppermute | solution.py:572
  20.4 1.4 %collective-permute-start.6 = (f32[224,128]{1,0:T(8,128)S(1)}, f32[224,128]{1,0:T(8,128)S(1)}, u32[]{:S(2)}, u32[]{:S(2)}) collective-permute-start(f32[224,128]{1,0:T(8,128)S(1)} %get-tuple-element.47), channel_id=1, source_target_pairs={{0,1},{1,0},{2,3},{3,2},{4,5},{5,4},{6,7},{7,6},{8,9},{9,8},{10,11... | collective-permute-start | bytes 344072 | tf_op jit(solution)/shard_map/ppermute | solution.py:543
  21.8 4.2 %collective-permute-start.8 = (f32[112,128]{1,0:T(8,128)S(1)}, f32[112,128]{1,0:T(8,128)S(1)}, u32[]{:S(2)}, u32[]{:S(2)}) collective-permute-start(f32[112,128]{1,0:T(8,128)S(1)} %slice_select_fusion.1), channel_id=1, source_target_pairs={{0,16},{1,17},{2,18},{3,19},{4,20},{5,21},{6,22},{7,23},{8,24},{9,... | collective-permute-start | bytes 172040 | tf_op jit(solution)/shard_map/ppermute | solution.py:543
  22.9 5.3 %collective-permute-start.9 = (f32[112,128]{1,0:T(8,128)S(1)}, f32[112,128]{1,0:T(8,128)S(1)}, u32[]{:S(2)}, u32[]{:S(2)}) collective-permute-start(f32[112,128]{1,0:T(8,128)S(1)} %slice_select_fusion.1), channel_id=1, source_target_pairs={{0,24},{1,25},{2,26},{3,27},{4,28},{5,29},{6,30},{7,31},{8,16},{9,... | collective-permute-start | bytes 172040 | tf_op jit(solution)/shard_map/ppermute | solution.py:543
  24.3 4.2 %collective-permute-start.7 = (f32[112,128]{1,0:T(8,128)S(1)}, f32[112,128]{1,0:T(8,128)S(1)}, u32[]{:S(2)}, u32[]{:S(2)}) collective-permute-start(f32[112,128]{1,0:T(8,128)S(1)} %slice_select_fusion.1), channel_id=1, source_target_pairs={{0,8},{1,9},{2,10},{3,11},{4,12},{5,13},{6,14},{7,15},{8,0},{9,1},... | collective-permute-start | bytes 172040 | tf_op jit(solution)/shard_map/ppermute | solution.py:543
  25.4 5.1 %collective-permute-start.10 = (f32[64,128]{1,0:T(8,128)S(1)}, f32[64,128]{1,0:T(8,128)S(1)}, u32[]{:S(2)}, u32[]{:S(2)}) collective-permute-start(f32[64,128]{1,0:T(8,128)S(1)} %get-tuple-element.46.y_last_ref), channel_id=1, source_target_pairs={{0,1},{1,2},{2,3},{3,4},{4,5},{5,6},{6,7},{7,0},{8,9},{9,10},{10,1... | collective-permute-start | bytes 98312 | tf_op jit(solution)/shard_map/ppermute | solution.py:568
  30.5 6.6 %collective-permute-start.15 = (f32[112,128]{1,0:T(8,128)S(1)}, f32[112,128]{1,0:T(8,128)S(1)}, u32[]{:S(2)}, u32[]{:S(2)}) collective-permute-start(f32[112,128]{1,0:T(8,128)S(1)} %add_add_fusion.3), channel_id=1, source_target_pairs={{0,6},{1,7},{2,4},{3,5},{4,2},{5,3},{6,0},{7,1},{8,14},{9,15},{10,... | collective-permute-start | bytes 172040 | tf_op jit(solution)/shard_map/ppermute | solution.py:543
  32.1 6.0 %collective-permute-start.14 = (f32[112,128]{1,0:T(8,128)S(1)}, f32[112,128]{1,0:T(8,128)S(1)}, u32[]{:S(2)}, u32[]{:S(2)}) collective-permute-start(f32[112,128]{1,0:T(8,128)S(1)} %add_add_fusion.3), channel_id=1, source_target_pairs={{0,4},{1,5},{2,6},{3,7},{4,0},{5,1},{6,2},{7,3},{8,12},{9,13},{10,... | collective-permute-start | bytes 172040 | tf_op jit(solution)/shard_map/ppermute | solution.py:543
  32.1 6.0 %collective-permute-start.13 = (f32[112,128]{1,0:T(8,128)S(1)}, f32[112,128]{1,0:T(8,128)S(1)}, u32[]{:S(2)}, u32[]{:S(2)}) collective-permute-start(f32[112,128]{1,0:T(8,128)S(1)} %add_add_fusion.3), channel_id=1, source_target_pairs={{0,2},{1,3},{2,0},{3,1},{4,6},{5,7},{6,4},{7,5},{8,10},{9,11},{10,... | collective-permute-start | bytes 172040 | tf_op jit(solution)/shard_map/ppermute | solution.py:543
  38.1 3.3 %collective-permute-start.16 = (f32[112,128]{1,0:T(8,128)S(1)}, f32[112,128]{1,0:T(8,128)S(1)}, u32[]{:S(2)}, u32[]{:S(2)}) collective-permute-start(f32[112,128]{1,0:T(8,128)S(1)} %add_add_fusion.2), channel_id=1, source_target_pairs={{0,1},{1,0},{2,3},{3,2},{4,5},{5,4},{6,7},{7,6},{8,9},{9,8},{10,11... | collective-permute-start | bytes 172040 | tf_op jit(solution)/shard_map/ppermute | solution.py:543
  38.2 10.7 %collective-permute-start.12 = (f32[64,640]{1,0:T(8,128)S(1)}, f32[64,640]{1,0:T(8,128)S(1)}, u32[]{:S(2)}, u32[]{:S(2)}) collective-permute-start(f32[64,640]{1,0:T(8,128)S(1)} %get-tuple-element.49), channel_id=1, source_target_pairs={{0,8},{8,16},{16,24},{24,0},{1,9},{9,17},{17,25},{25,1},{2,10},{10... | collective-permute-start | bytes 491528 | tf_op jit(solution)/shard_map/ppermute | solution.py:568
  39.0 9.9 %collective-permute-start.11 = (f32[64,640]{1,0:T(8,128)S(1)}, f32[64,640]{1,0:T(8,128)S(1)}, u32[]{:S(2)}, u32[]{:S(2)}) collective-permute-start(f32[64,640]{1,0:T(8,128)S(1)} %shard_map.72), channel_id=1, source_target_pairs={{0,24},{8,0},{16,8},{24,16},{1,25},{9,1},{17,9},{25,17},{2,26},{10... | collective-permute-start | bytes 491528 | tf_op jit(solution)/shard_map/ppermute | solution.py:572
  51.8 1.4 %collective-permute-start.17 = (f32[224,128]{1,0:T(8,128)S(1)}, f32[224,128]{1,0:T(8,128)S(1)}, u32[]{:S(2)}, u32[]{:S(2)}) collective-permute-start(f32[224,128]{1,0:T(8,128)S(1)} %get-tuple-element.55), channel_id=1, source_target_pairs={{0,1},{1,0},{2,3},{3,2},{4,5},{5,4},{6,7},{7,6},{8,9},{9,8},{10,11... | collective-permute-start | bytes 344072 | tf_op jit(solution)/shard_map/ppermute | solution.py:543
  53.3 4.2 %collective-permute-start.19 = (f32[112,128]{1,0:T(8,128)S(1)}, f32[112,128]{1,0:T(8,128)S(1)}, u32[]{:S(2)}, u32[]{:S(2)}) collective-permute-start(f32[112,128]{1,0:T(8,128)S(1)} %slice_select_fusion), channel_id=1, source_target_pairs={{0,16},{1,17},{2,18},{3,19},{4,20},{5,21},{6,22},{7,23},{8,24},{9,... | collective-permute-start | bytes 172040 | tf_op jit(solution)/shard_map/ppermute | solution.py:543
  54.2 5.2 %collective-permute-start.20 = (f32[112,128]{1,0:T(8,128)S(1)}, f32[112,128]{1,0:T(8,128)S(1)}, u32[]{:S(2)}, u32[]{:S(2)}) collective-permute-start(f32[112,128]{1,0:T(8,128)S(1)} %slice_select_fusion), channel_id=1, source_target_pairs={{0,24},{1,25},{2,26},{3,27},{4,28},{5,29},{6,30},{7,31},{8,16},{9,... | collective-permute-start | bytes 172040 | tf_op jit(solution)/shard_map/ppermute | solution.py:543
  55.3 4.4 %collective-permute-start.18 = (f32[112,128]{1,0:T(8,128)S(1)}, f32[112,128]{1,0:T(8,128)S(1)}, u32[]{:S(2)}, u32[]{:S(2)}) collective-permute-start(f32[112,128]{1,0:T(8,128)S(1)} %slice_select_fusion), channel_id=1, source_target_pairs={{0,8},{1,9},{2,10},{3,11},{4,12},{5,13},{6,14},{7,15},{8,0},{9,1},... | collective-permute-start | bytes 172040 | tf_op jit(solution)/shard_map/ppermute | solution.py:543
  59.7 6.1 %collective-permute-start.23 = (f32[112,128]{1,0:T(8,128)S(1)}, f32[112,128]{1,0:T(8,128)S(1)}, u32[]{:S(2)}, u32[]{:S(2)}) collective-permute-start(f32[112,128]{1,0:T(8,128)S(1)} %add_add_fusion.1), channel_id=1, source_target_pairs={{0,6},{1,7},{2,4},{3,5},{4,2},{5,3},{6,0},{7,1},{8,14},{9,15},{10,... | collective-permute-start | bytes 172040 | tf_op jit(solution)/shard_map/ppermute | solution.py:543
  61.2 6.0 %collective-permute-start.22 = (f32[112,128]{1,0:T(8,128)S(1)}, f32[112,128]{1,0:T(8,128)S(1)}, u32[]{:S(2)}, u32[]{:S(2)}) collective-permute-start(f32[112,128]{1,0:T(8,128)S(1)} %add_add_fusion.1), channel_id=1, source_target_pairs={{0,4},{1,5},{2,6},{3,7},{4,0},{5,1},{6,2},{7,3},{8,12},{9,13},{10,... | collective-permute-start | bytes 172040 | tf_op jit(solution)/shard_map/ppermute | solution.py:543
  62.4 4.8 %collective-permute-start.21 = (f32[112,128]{1,0:T(8,128)S(1)}, f32[112,128]{1,0:T(8,128)S(1)}, u32[]{:S(2)}, u32[]{:S(2)}) collective-permute-start(f32[112,128]{1,0:T(8,128)S(1)} %add_add_fusion.1), channel_id=1, source_target_pairs={{0,2},{1,3},{2,0},{3,1},{4,6},{5,7},{6,4},{7,5},{8,10},{9,11},{10,... | collective-permute-start | bytes 172040 | tf_op jit(solution)/shard_map/ppermute | solution.py:543
  (5 other events, 26.5 us)

commit v5 on v4

--- a/solution.py
+++ b/solution.py
@@ -183,7 +183,6 @@
                 at = place[:, :width]
                 out[b] = jnp.where(at == j, upper, jnp.where(at == j + 1, lower, out[b]))
             over = 1.0 / (p * q - o * o)
-            p, o, q = p * over, o * over, q * over
 
             def solve(value):
                 width = value.shape[1]
@@ -193,19 +192,28 @@
                     p[:, :width] * lower - o[:, :width] * upper,
                 )
 
+            def remove(value, left, right, up, low, scale):
+                width = value.shape[1]
+                part = left[:, :width] * up + right[:, :width] * low
+                return value - (part if scale is None else part * scale[:, :width])
+
             later = [solve(cols[b][n]) for n in range(j + 2, group)]
             pivots = [solve(f[b]) for f in fields]
-            for c in range(b, blocks):
+            if j < group - 2:
+                left = jnp.where(place > j + 1, first, 0.0)
+                right = jnp.where(place > j + 1, second, 0.0)
+                for n, (up, low) in enumerate(later):
+                    cols[b][j + 2 + n] = remove(cols[b][j + 2 + n], left, right, up, low, over)
+                for f, (up, low) in zip(fields, pivots):
+                    f[b] = remove(f[b], left, right, up, low, over)
+            later = [(up * over, low * over) for up, low in later]
+            pivots = [(up * over[:, :up.shape[1]], low * over[:, :up.shape[1]]) for up, low in pivots]
+            for c in range(b + 1, blocks):
                 left, right = cols[c][j], cols[c][j + 1]
-                if c == b:
-                    if j == group - 2:
-                        continue
-                    left, right = jnp.where(place > j + 1, left, 0.0), jnp.where(place > j + 1, right, 0.0)
                 for n, (up, low) in enumerate(later):
-                    cols[c][j + 2 + n] = cols[c][j + 2 + n] - left * up - right * low
+                    cols[c][j + 2 + n] = remove(cols[c][j + 2 + n], left, right, up, low, None)
                 for f, (up, low) in zip(fields, pivots):
-                    width = up.shape[1]
-                    f[c] = f[c] - left[:, :width] * up - right[:, :width] * low
+                    f[c] = remove(f[c], left, right, up, low, None)
         if b < len(meanwhile):
             meanwhile[b]()
     done = [jnp.concatenate(d, axis=0) for d in done]
@@ -488,13 +496,13 @@
 
 
 def last_kernel(
-    cells, sums_ref, orient_ref, basis_ref, table_ref, mean_ref, e_ref, field_ref, x_ref, s_ref, v_ref, x_buffer, sems
+    cells, sums_ref, orient_ref, basis_ref, table_ref, mean_ref, e_ref, field_ref, x_ref, s_ref, v_ref, x_buffer, v_buffer, sems
 ):
     inverse, new = orient_stage(
         cells, sums_ref[...], orient_ref[...], table_ref[...], mean_ref[...], e_ref[...], basis_ref[...]
     )
     count = new.shape[1]
-    parts = sems.shape[0]
+    parts = v_buffer.shape[0]
     chunk = field_ref.shape[1] // parts
 
     copies = [
@@ -515,7 +523,13 @@
         three(new_halves, new_halves, (1, 1)) * (1.0 / count), meanwhile=[x_part(n) for n in range(parts)]
     )
     s_ref[...] = upper_v.T
-    v_ref[...] = apply(inverse_v, new)
+    wide = count // parts
+    for n in range(parts):
+        v_buffer[n] = apply(inverse_v, new[:, n * wide:(n + 1) * wide])
+        copies.append(
+            pltpu.make_async_copy(v_buffer.at[n], v_ref.at[:, pl.ds(n * wide, wide)], sems.at[parts + n])
+        )
+        copies[-1].start()
     for copy in copies:
         copy.wait()
 
@@ -623,8 +637,12 @@
     )
     new_spatial, new_coupling, new_orient = call(
         functools.partial(last_kernel, cells), [(sites, rank), (rank, rank), (rank, count)],
-        all_sum(part), new, inverse, table, mean, directions, field, far_out=(0,),
-        scratch=(pltpu.VMEM((sites, rank), jnp.float32), pltpu.SemaphoreType.DMA((4,))),
+        all_sum(part), new, inverse, table, mean, directions, field, far_out=(0, 2),
+        scratch=(
+            pltpu.VMEM((sites, rank), jnp.float32),
+            pltpu.VMEM((4, rank, count // 4), jnp.float32),
+            pltpu.SemaphoreType.DMA((8,)),
+        ),
     )
     return new_spatial.reshape(spatial_factor.shape), new_coupling, new_orient.T
 

time: 77.4 us -> 77 us (level)
  no operation moved by 1% of the time
where the time goes in v5:
time: 77 us; the launch traced here: 76.9 us
  starting transfers between devices  30.9 us (40%)
  Pallas kernels  24.2 us (31%)
  waiting for transfers between devices  19.4 us (25%)
  local copies, waits for them, and re-layouts  1.23 us (2%)
  between operations  1.02 us (1%)
    pallas_call x9, Pallas kernels, call(): pl.pallas_call(body, out_shape=[jax.ShapeDtypeStruct(shape, jnp.float32)...  24.2 us
    ppermute x16, starting transfers between devices, swapped(): lax.ppermute(value, ('gx', 'gy'), [(i, i ^ bits) for i in range(count)])  16.2 us
    ppermute x16, waiting for transfers between devices, swapped(): lax.ppermute(value, ('gx', 'gy'), [(i, i ^ bits) for i in range(count)])  16.1 us
    ppermute x5, starting transfers between devices, down(): return lax.ppermute(value, axis, shifted(axis, False))  11 us
    ppermute x4, starting transfers between devices, up(): return lax.ppermute(value, axis, shifted(axis, True))  3.69 us
    ppermute x4, waiting for transfers between devices, up(): return lax.ppermute(value, axis, shifted(axis, True))  2.08 us
  transfers between devices with their start and end apart: 25, of which 15 were waited for; matrix products, arithmetic and copies ran while one was open for 0% of the time, Pallas kernels for 15%

profile of v5, /device:TPU:0, one launch (start us, length us, event | category | flops | bytes accessed | tf_op | source)
XLA Modules:
  0.0 76.9 jit_solution(8003781605812356088)
XLA Ops:
  2.3 3.0 %collective-permute-start = (f32[64,512]{1,0:T(8,128)S(1)}, f32[64,512]{1,0:T(8,128)S(1)}, u32[]{:S(2)}, u32[]{:S(2)}) collective-permute-start(f32[64,512]{1,0:T(8,128)S(1)} %get-tuple-element.34), channel_id=1, source_target_pairs={{0,8},{8,16},{16,24},{24,0},{1,9},{9,17},{17,25},{25,1},{2,10},{10... | collective-permute-start | bytes 393224 | tf_op jit(solution)/shard_map/ppermute | solution.py:582
  6.3 3.5 %collective-permute-start.3 = (f32[64,128]{1,0:T(8,128)S(1)}, f32[64,128]{1,0:T(8,128)S(1)}, u32[]{:S(2)}, u32[]{:S(2)}) collective-permute-start(f32[64,128]{1,0:T(8,128)S(1)} %get-tuple-element.37), channel_id=1, source_target_pairs={{0,7},{1,0},{2,1},{3,2},{4,3},{5,4},{6,5},{7,6},{8,15},{9,8},{10,9... | collective-permute-start | bytes 98312 | tf_op jit(solution)/shard_map/ppermute | solution.py:586
  9.8 1.7 %shard_map.68 = (f32[384,64]{1,0:T(8,128)S(1)}, f32[64,1]{1,0:T(8,128)S(1)}, f32[64,512]{1,0:T(8,128)S(1)}, f32[64,1]{1,0:T(8,128)S(1)}) custom-call(f32[64,2048]{1,0:T(8,128)S(1)} %bitcast.4, f32[3,2048]{1,0:T(4,128)S(1)} %copy-done.2, f32[64,64]{1,0:T(8,128)S(1)} %copy-done.3), custom_call_target="tpu_custom_call" | custom-call | tf_op jit(solution)/shard_map/pallas_call | solution.py:228
  13.5 1.5 %collective-permute-start.4 = (f32[64,512]{1,0:T(8,128)S(1)}, f32[64,512]{1,0:T(8,128)S(1)}, u32[]{:S(2)}, u32[]{:S(2)}) collective-permute-start(f32[64,512]{1,0:T(8,128)S(1)} %get-tuple-element.42), channel_id=1, source_target_pairs={{0,24},{8,0},{16,8},{24,16},{1,25},{9,1},{17,9},{25,17},{2,26},{10... | collective-permute-start | bytes 393224 | tf_op jit(solution)/shard_map/ppermute | solution.py:586
  15.0 2.4 %collective-permute-start.5 = (f32[64,256]{1,0:T(8,128)S(1)}, f32[64,256]{1,0:T(8,128)S(1)}, u32[]{:S(2)}, u32[]{:S(2)}) collective-permute-start(f32[64,256]{1,0:T(8,128)S(1)} %get-tuple-element.43), channel_id=1, source_target_pairs={{0,7},{1,0},{2,1},{3,2},{4,3},{5,4},{6,5},{7,6},{8,15},{9,8},{10,9... | collective-permute-start | bytes 196616 | tf_op jit(solution)/shard_map/ppermute | solution.py:586
  17.5 2.6 %shard_map.69 = (f32[64,2048]{1,0:T(8,128)S(1)}, f32[256,128]{1,0:T(8,128)S(1)}, f32[64,512]{1,0:T(8,128)S(1)}, f32[64,128]{1,0:T(8,128)S(1)}) custom-call(f32[64,2048]{1,0:T(8,128)S(1)} %get-tuple-element.33.field_ref, f32[64,512]{1,0:T(8,128)S(1)} %collective-permute-done.xb, f32[64,512]{1,0:T(8,128)S(1)} %collective-permute-done.1.xa, ...), custom_call_target="tpu_custom_call" | custom-call | flops 1000000000 | bytes 8000000 | tf_op jit(solution)/shard_map/pallas_call | solution.py:228
  20.5 1.3 %collective-permute-done.6 = f32[224,128]{1,0:T(8,128)S(1)} collective-permute-done((f32[224,128]{1,0:T(8,128)S(1)}, f32[224,128]{1,0:T(8,128)S(1)}, u32[]{:S(2)}, u32[]{:S(2)}) %collective-permute-start.6) | collective-permute-done | bytes 114720 | tf_op jit(solution)/shard_map/ppermute | solution.py:557
  22.9 1.4 %collective-permute-start.9 = (f32[112,128]{1,0:T(8,128)S(1)}, f32[112,128]{1,0:T(8,128)S(1)}, u32[]{:S(2)}, u32[]{:S(2)}) collective-permute-start(f32[112,128]{1,0:T(8,128)S(1)} %slice_select_fusion.1), channel_id=1, source_target_pairs={{0,24},{1,25},{2,26},{3,27},{4,28},{5,29},{6,30},{7,31},{8,16},{9,... | collective-permute-start | bytes 172040 | tf_op jit(solution)/shard_map/ppermute | solution.py:557
  26.1 2.1 %collective-permute-done.9 = f32[112,128]{1,0:T(8,128)S(1)} collective-permute-done((f32[112,128]{1,0:T(8,128)S(1)}, f32[112,128]{1,0:T(8,128)S(1)}, u32[]{:S(2)}, u32[]{:S(2)}) %collective-permute-start.9) | collective-permute-done | bytes 57376 | tf_op jit(solution)/shard_map/ppermute | solution.py:557
  28.5 2.1 %collective-permute-done.10.yb = f32[64,128]{1,0:T(8,128)S(1)} collective-permute-done((f32[64,128]{1,0:T(8,128)S(1)}, f32[64,128]{1,0:T(8,128)S(1)}, u32[]{:S(2)}, u32[]{:S(2)}) %collective-permute-start.10) | collective-permute-done | bytes 32800 | tf_op jit(solution)/shard_map/ppermute | solution.py:582
  30.5 1.6 %collective-permute-start.15 = (f32[112,128]{1,0:T(8,128)S(1)}, f32[112,128]{1,0:T(8,128)S(1)}, u32[]{:S(2)}, u32[]{:S(2)}) collective-permute-start(f32[112,128]{1,0:T(8,128)S(1)} %add_add_fusion.3), channel_id=1, source_target_pairs={{0,6},{1,7},{2,4},{3,5},{4,2},{5,3},{6,0},{7,1},{8,14},{9,15},{10,... | collective-permute-start | bytes 172040 | tf_op jit(solution)/shard_map/ppermute | solution.py:557
  32.1 2.8 %collective-permute-start.13 = (f32[112,128]{1,0:T(8,128)S(1)}, f32[112,128]{1,0:T(8,128)S(1)}, u32[]{:S(2)}, u32[]{:S(2)}) collective-permute-start(f32[112,128]{1,0:T(8,128)S(1)} %add_add_fusion.3), channel_id=1, source_target_pairs={{0,2},{1,3},{2,0},{3,1},{4,6},{5,7},{6,4},{7,5},{8,10},{9,11},{10,... | collective-permute-start | bytes 172040 | tf_op jit(solution)/shard_map/ppermute | solution.py:557
  34.9 2.2 %collective-permute-done.15 = f32[112,128]{1,0:T(8,128)S(1)} collective-permute-done((f32[112,128]{1,0:T(8,128)S(1)}, f32[112,128]{1,0:T(8,128)S(1)}, u32[]{:S(2)}, u32[]{:S(2)}) %collective-permute-start.15) | collective-permute-done | bytes 57376 | tf_op jit(solution)/shard_map/ppermute | solution.py:557
  39.0 2.5 %collective-permute-start.11 = (f32[64,640]{1,0:T(8,128)S(1)}, f32[64,640]{1,0:T(8,128)S(1)}, u32[]{:S(2)}, u32[]{:S(2)}) collective-permute-start(f32[64,640]{1,0:T(8,128)S(1)} %shard_map.72), channel_id=1, source_target_pairs={{0,24},{8,0},{16,8},{24,16},{1,25},{9,1},{17,9},{25,17},{2,26},{10... | collective-permute-start | bytes 491528 | tf_op jit(solution)/shard_map/ppermute | solution.py:586
  41.5 7.2 %shard_map.73 = (f32[64,512]{1,0:T(8,128)S(1)}, f32[64,1]{1,0:T(8,128)S(1)}, f32[64,1]{1,0:T(8,128)S(1)}, f32[64,2048]{1,0:T(8,128)S(1)}, f32[64,64]{1,0:T(8,128)S(1)}, /*index=5*/f32[384,64]{1,0:T(8,128)S(1)}) custom-call(f32[224,128]{1,0:T(8,128)S(1)} %pad_maximum_fusion.sums_ref, f32[64,2048]{1,0:T(8,128)S(1)} %bitcast.5, ...), custom_call_target="tpu_custom_call" | custom-call | flops 1 | bytes 1 | tf_op jit(solution)/shard_map/pallas_call | solution.py:228
  48.7 2.9 %shard_map.74 = (f32[64,2048]{1,0:T(8,128)S(1)}, f32[224,128]{1,0:T(8,128)S(1)}) custom-call(f32[64,2048]{1,0:T(8,128)S(1)} %get-tuple-element.41.field_ref, f32[64,512]{1,0:T(8,128)S(1)} %collective-permute-done.4.xa, f32[64,256]{1,0:T(8,128)S(1)} %collective-permute-done.5.ya, f32[64,128]{1,0:T(8,128)S(1)} %collective-permute-done.10.yb, ...), custom_call_target="tpu_custom_call" | custom-call | tf_op jit(solution)/shard_map/pallas_call | solution.py:228
  51.7 1.3 %collective-permute-done.17 = f32[224,128]{1,0:T(8,128)S(1)} collective-permute-done((f32[224,128]{1,0:T(8,128)S(1)}, f32[224,128]{1,0:T(8,128)S(1)}, u32[]{:S(2)}, u32[]{:S(2)}) %collective-permute-start.17) | collective-permute-done | bytes 114720 | tf_op jit(solution)/shard_map/ppermute | solution.py:557
  55.3 1.3 %collective-permute-start.18 = (f32[112,128]{1,0:T(8,128)S(1)}, f32[112,128]{1,0:T(8,128)S(1)}, u32[]{:S(2)}, u32[]{:S(2)}) collective-permute-start(f32[112,128]{1,0:T(8,128)S(1)} %slice_select_fusion), channel_id=1, source_target_pairs={{0,8},{1,9},{2,10},{3,11},{4,12},{5,13},{6,14},{7,15},{8,0},{9,1},... | collective-permute-start | bytes 172040 | tf_op jit(solution)/shard_map/ppermute | solution.py:557
  57.3 2.1 %collective-permute-done.20 = f32[112,128]{1,0:T(8,128)S(1)} collective-permute-done((f32[112,128]{1,0:T(8,128)S(1)}, f32[112,128]{1,0:T(8,128)S(1)}, u32[]{:S(2)}, u32[]{:S(2)}) %collective-permute-start.20) | collective-permute-done | bytes 57376 | tf_op jit(solution)/shard_map/ppermute | solution.py:557
  59.5 1.7 %collective-permute-start.23 = (f32[112,128]{1,0:T(8,128)S(1)}, f32[112,128]{1,0:T(8,128)S(1)}, u32[]{:S(2)}, u32[]{:S(2)}) collective-permute-start(f32[112,128]{1,0:T(8,128)S(1)} %add_add_fusion.1), channel_id=1, source_target_pairs={{0,6},{1,7},{2,4},{3,5},{4,2},{5,3},{6,0},{7,1},{8,14},{9,15},{10,... | collective-permute-start | bytes 172040 | tf_op jit(solution)/shard_map/ppermute | solution.py:557
  62.4 1.6 %collective-permute-start.21 = (f32[112,128]{1,0:T(8,128)S(1)}, f32[112,128]{1,0:T(8,128)S(1)}, u32[]{:S(2)}, u32[]{:S(2)}) collective-permute-start(f32[112,128]{1,0:T(8,128)S(1)} %add_add_fusion.1), channel_id=1, source_target_pairs={{0,2},{1,3},{2,0},{3,1},{4,6},{5,7},{6,4},{7,5},{8,10},{9,11},{10,... | collective-permute-start | bytes 172040 | tf_op jit(solution)/shard_map/ppermute | solution.py:557
  64.0 2.1 %collective-permute-done.23 = f32[112,128]{1,0:T(8,128)S(1)} collective-permute-done((f32[112,128]{1,0:T(8,128)S(1)}, f32[112,128]{1,0:T(8,128)S(1)}, u32[]{:S(2)}, u32[]{:S(2)}) %collective-permute-start.23) | collective-permute-done | bytes 57376 | tf_op jit(solution)/shard_map/ppermute | solution.py:557
  67.3 1.2 %collective-permute-done.24 = f32[112,128]{1,0:T(8,128)S(1)} collective-permute-done((f32[112,128]{1,0:T(8,128)S(1)}, f32[112,128]{1,0:T(8,128)S(1)}, u32[]{:S(2)}, u32[]{:S(2)}) %collective-permute-start.24) | collective-permute-done | bytes 57376 | tf_op jit(solution)/shard_map/ppermute | solution.py:557
  68.5 8.2 %shard_map.75 = (f32[2048,64]{1,0:T(8,128)}, f32[64,64]{1,0:T(8,128)}, f32[64,2048]{1,0:T(8,128)}) custom-call(f32[224,128]{1,0:T(8,128)S(1)} %pad_maximum_fusion.1.sums_ref, f32[64,2048]{1,0:T(8,128)S(1)} %get-tuple-element.56.orient_ref, f32[64,64]{1,0:T(8,128)S(1)} %get-tuple-element.57.basis_ref, f32[384,64]{1,0:T(8,128)S(1)} %get-tuple-element.58.table_ref, ...), custom_call_target="tpu_custom_call" | custom-call | tf_op jit(solution)/shard_map/pallas_call | solution.py:228
  (55 shorter events, 15.4 us)
Async XLA Ops:
  2.3 9.3 %collective-permute-start = (f32[64,512]{1,0:T(8,128)S(1)}, f32[64,512]{1,0:T(8,128)S(1)}, u32[]{:S(2)}, u32[]{:S(2)}) collective-permute-start(f32[64,512]{1,0:T(8,128)S(1)} %get-tuple-element.34), channel_id=1, source_target_pairs={{0,8},{8,16},{16,24},{24,0},{1,9},{9,17},{17,25},{25,1},{2,10},{10... | collective-permute-start | bytes 393224 | tf_op jit(solution)/shard_map/ppermute | solution.py:582
  5.3 7.5 %collective-permute-start.1 = (f32[64,512]{1,0:T(8,128)S(1)}, f32[64,512]{1,0:T(8,128)S(1)}, u32[]{:S(2)}, u32[]{:S(2)}) collective-permute-start(f32[64,512]{1,0:T(8,128)S(1)} %get-tuple-element.35), channel_id=1, source_target_pairs={{0,24},{8,0},{16,8},{24,16},{1,25},{9,1},{17,9},{25,17},{2,26},{10... | collective-permute-start | bytes 393224 | tf_op jit(solution)/shard_map/ppermute | solution.py:586
  6.3 5.3 %collective-permute-start.2 = (f32[64,128]{1,0:T(8,128)S(1)}, f32[64,128]{1,0:T(8,128)S(1)}, u32[]{:S(2)}, u32[]{:S(2)}) collective-permute-start(f32[64,128]{1,0:T(8,128)S(1)} %get-tuple-element.36), channel_id=1, source_target_pairs={{0,1},{1,2},{2,3},{3,4},{4,5},{5,6},{6,7},{7,0},{8,9},{9,10},{10,1... | collective-permute-start | bytes 98312 | tf_op jit(solution)/shard_map/ppermute | solution.py:582
  6.3 5.3 %collective-permute-start.3 = (f32[64,128]{1,0:T(8,128)S(1)}, f32[64,128]{1,0:T(8,128)S(1)}, u32[]{:S(2)}, u32[]{:S(2)}) collective-permute-start(f32[64,128]{1,0:T(8,128)S(1)} %get-tuple-element.37), channel_id=1, source_target_pairs={{0,7},{1,0},{2,1},{3,2},{4,3},{5,4},{6,5},{7,6},{8,15},{9,8},{10,9... | collective-permute-start | bytes 98312 | tf_op jit(solution)/shard_map/ppermute | solution.py:586
  13.5 6.5 %collective-permute-start.4 = (f32[64,512]{1,0:T(8,128)S(1)}, f32[64,512]{1,0:T(8,128)S(1)}, u32[]{:S(2)}, u32[]{:S(2)}) collective-permute-start(f32[64,512]{1,0:T(8,128)S(1)} %get-tuple-element.42), channel_id=1, source_target_pairs={{0,24},{8,0},{16,8},{24,16},{1,25},{9,1},{17,9},{25,17},{2,26},{10... | collective-permute-start | bytes 393224 | tf_op jit(solution)/shard_map/ppermute | solution.py:586
  15.0 5.0 %collective-permute-start.5 = (f32[64,256]{1,0:T(8,128)S(1)}, f32[64,256]{1,0:T(8,128)S(1)}, u32[]{:S(2)}, u32[]{:S(2)}) collective-permute-start(f32[64,256]{1,0:T(8,128)S(1)} %get-tuple-element.43), channel_id=1, source_target_pairs={{0,7},{1,0},{2,1},{3,2},{4,3},{5,4},{6,5},{7,6},{8,15},{9,8},{10,9... | collective-permute-start | bytes 196616 | tf_op jit(solution)/shard_map/ppermute | solution.py:586
  20.4 1.4 %collective-permute-start.6 = (f32[224,128]{1,0:T(8,128)S(1)}, f32[224,128]{1,0:T(8,128)S(1)}, u32[]{:S(2)}, u32[]{:S(2)}) collective-permute-start(f32[224,128]{1,0:T(8,128)S(1)} %get-tuple-element.47), channel_id=1, source_target_pairs={{0,1},{1,0},{2,3},{3,2},{4,5},{5,4},{6,7},{7,6},{8,9},{9,8},{10,11... | collective-permute-start | bytes 344072 | tf_op jit(solution)/shard_map/ppermute | solution.py:557
  21.8 4.2 %collective-permute-start.8 = (f32[112,128]{1,0:T(8,128)S(1)}, f32[112,128]{1,0:T(8,128)S(1)}, u32[]{:S(2)}, u32[]{:S(2)}) collective-permute-start(f32[112,128]{1,0:T(8,128)S(1)} %slice_select_fusion.1), channel_id=1, source_target_pairs={{0,16},{1,17},{2,18},{3,19},{4,20},{5,21},{6,22},{7,23},{8,24},{9,... | collective-permute-start | bytes 172040 | tf_op jit(solution)/shard_map/ppermute | solution.py:557
  22.9 5.3 %collective-permute-start.9 = (f32[112,128]{1,0:T(8,128)S(1)}, f32[112,128]{1,0:T(8,128)S(1)}, u32[]{:S(2)}, u32[]{:S(2)}) collective-permute-start(f32[112,128]{1,0:T(8,128)S(1)} %slice_select_fusion.1), channel_id=1, source_target_pairs={{0,24},{1,25},{2,26},{3,27},{4,28},{5,29},{6,30},{7,31},{8,16},{9,... | collective-permute-start | bytes 172040 | tf_op jit(solution)/shard_map/ppermute | solution.py:557
  24.3 4.2 %collective-permute-start.7 = (f32[112,128]{1,0:T(8,128)S(1)}, f32[112,128]{1,0:T(8,128)S(1)}, u32[]{:S(2)}, u32[]{:S(2)}) collective-permute-start(f32[112,128]{1,0:T(8,128)S(1)} %slice_select_fusion.1), channel_id=1, source_target_pairs={{0,8},{1,9},{2,10},{3,11},{4,12},{5,13},{6,14},{7,15},{8,0},{9,1},... | collective-permute-start | bytes 172040 | tf_op jit(solution)/shard_map/ppermute | solution.py:557
  25.4 5.1 %collective-permute-start.10 = (f32[64,128]{1,0:T(8,128)S(1)}, f32[64,128]{1,0:T(8,128)S(1)}, u32[]{:S(2)}, u32[]{:S(2)}) collective-permute-start(f32[64,128]{1,0:T(8,128)S(1)} %get-tuple-element.46.y_last_ref), channel_id=1, source_target_pairs={{0,1},{1,2},{2,3},{3,4},{4,5},{5,6},{6,7},{7,0},{8,9},{9,10},{10,1... | collective-permute-start | bytes 98312 | tf_op jit(solution)/shard_map/ppermute | solution.py:582
  30.5 6.6 %collective-permute-start.15 = (f32[112,128]{1,0:T(8,128)S(1)}, f32[112,128]{1,0:T(8,128)S(1)}, u32[]{:S(2)}, u32[]{:S(2)}) collective-permute-start(f32[112,128]{1,0:T(8,128)S(1)} %add_add_fusion.3), channel_id=1, source_target_pairs={{0,6},{1,7},{2,4},{3,5},{4,2},{5,3},{6,0},{7,1},{8,14},{9,15},{10,... | collective-permute-start | bytes 172040 | tf_op jit(solution)/shard_map/ppermute | solution.py:557
  32.1 6.0 %collective-permute-start.14 = (f32[112,128]{1,0:T(8,128)S(1)}, f32[112,128]{1,0:T(8,128)S(1)}, u32[]{:S(2)}, u32[]{:S(2)}) collective-permute-start(f32[112,128]{1,0:T(8,128)S(1)} %add_add_fusion.3), channel_id=1, source_target_pairs={{0,4},{1,5},{2,6},{3,7},{4,0},{5,1},{6,2},{7,3},{8,12},{9,13},{10,... | collective-permute-start | bytes 172040 | tf_op jit(solution)/shard_map/ppermute | solution.py:557
  32.1 6.0 %collective-permute-start.13 = (f32[112,128]{1,0:T(8,128)S(1)}, f32[112,128]{1,0:T(8,128)S(1)}, u32[]{:S(2)}, u32[]{:S(2)}) collective-permute-start(f32[112,128]{1,0:T(8,128)S(1)} %add_add_fusion.3), channel_id=1, source_target_pairs={{0,2},{1,3},{2,0},{3,1},{4,6},{5,7},{6,4},{7,5},{8,10},{9,11},{10,... | collective-permute-start | bytes 172040 | tf_op jit(solution)/shard_map/ppermute | solution.py:557
  38.1 3.3 %collective-permute-start.16 = (f32[112,128]{1,0:T(8,128)S(1)}, f32[112,128]{1,0:T(8,128)S(1)}, u32[]{:S(2)}, u32[]{:S(2)}) collective-permute-start(f32[112,128]{1,0:T(8,128)S(1)} %add_add_fusion.2), channel_id=1, source_target_pairs={{0,1},{1,0},{2,3},{3,2},{4,5},{5,4},{6,7},{7,6},{8,9},{9,8},{10,11... | collective-permute-start | bytes 172040 | tf_op jit(solution)/shard_map/ppermute | solution.py:557
  38.2 10.5 %collective-permute-start.12 = (f32[64,640]{1,0:T(8,128)S(1)}, f32[64,640]{1,0:T(8,128)S(1)}, u32[]{:S(2)}, u32[]{:S(2)}) collective-permute-start(f32[64,640]{1,0:T(8,128)S(1)} %get-tuple-element.49), channel_id=1, source_target_pairs={{0,8},{8,16},{16,24},{24,0},{1,9},{9,17},{17,25},{25,1},{2,10},{10... | collective-permute-start | bytes 491528 | tf_op jit(solution)/shard_map/ppermute | solution.py:582
  39.0 9.7 %collective-permute-start.11 = (f32[64,640]{1,0:T(8,128)S(1)}, f32[64,640]{1,0:T(8,128)S(1)}, u32[]{:S(2)}, u32[]{:S(2)}) collective-permute-start(f32[64,640]{1,0:T(8,128)S(1)} %shard_map.72), channel_id=1, source_target_pairs={{0,24},{8,0},{16,8},{24,16},{1,25},{9,1},{17,9},{25,17},{2,26},{10... | collective-permute-start | bytes 491528 | tf_op jit(solution)/shard_map/ppermute | solution.py:586
  51.6 1.4 %collective-permute-start.17 = (f32[224,128]{1,0:T(8,128)S(1)}, f32[224,128]{1,0:T(8,128)S(1)}, u32[]{:S(2)}, u32[]{:S(2)}) collective-permute-start(f32[224,128]{1,0:T(8,128)S(1)} %get-tuple-element.55), channel_id=1, source_target_pairs={{0,1},{1,0},{2,3},{3,2},{4,5},{5,4},{6,7},{7,6},{8,9},{9,8},{10,11... | collective-permute-start | bytes 344072 | tf_op jit(solution)/shard_map/ppermute | solution.py:557
  53.1 4.2 %collective-permute-start.19 = (f32[112,128]{1,0:T(8,128)S(1)}, f32[112,128]{1,0:T(8,128)S(1)}, u32[]{:S(2)}, u32[]{:S(2)}) collective-permute-start(f32[112,128]{1,0:T(8,128)S(1)} %slice_select_fusion), channel_id=1, source_target_pairs={{0,16},{1,17},{2,18},{3,19},{4,20},{5,21},{6,22},{7,23},{8,24},{9,... | collective-permute-start | bytes 172040 | tf_op jit(solution)/shard_map/ppermute | solution.py:557
  54.2 5.2 %collective-permute-start.20 = (f32[112,128]{1,0:T(8,128)S(1)}, f32[112,128]{1,0:T(8,128)S(1)}, u32[]{:S(2)}, u32[]{:S(2)}) collective-permute-start(f32[112,128]{1,0:T(8,128)S(1)} %slice_select_fusion), channel_id=1, source_target_pairs={{0,24},{1,25},{2,26},{3,27},{4,28},{5,29},{6,30},{7,31},{8,16},{9,... | collective-permute-start | bytes 172040 | tf_op jit(solution)/shard_map/ppermute | solution.py:557
  55.3 4.2 %collective-permute-start.18 = (f32[112,128]{1,0:T(8,128)S(1)}, f32[112,128]{1,0:T(8,128)S(1)}, u32[]{:S(2)}, u32[]{:S(2)}) collective-permute-start(f32[112,128]{1,0:T(8,128)S(1)} %slice_select_fusion), channel_id=1, source_target_pairs={{0,8},{1,9},{2,10},{3,11},{4,12},{5,13},{6,14},{7,15},{8,0},{9,1},... | collective-permute-start | bytes 172040 | tf_op jit(solution)/shard_map/ppermute | solution.py:557
  59.5 6.5 %collective-permute-start.23 = (f32[112,128]{1,0:T(8,128)S(1)}, f32[112,128]{1,0:T(8,128)S(1)}, u32[]{:S(2)}, u32[]{:S(2)}) collective-permute-start(f32[112,128]{1,0:T(8,128)S(1)} %add_add_fusion.1), channel_id=1, source_target_pairs={{0,6},{1,7},{2,4},{3,5},{4,2},{5,3},{6,0},{7,1},{8,14},{9,15},{10,... | collective-permute-start | bytes 172040 | tf_op jit(solution)/shard_map/ppermute | solution.py:557
  61.2 5.9 %collective-permute-start.22 = (f32[112,128]{1,0:T(8,128)S(1)}, f32[112,128]{1,0:T(8,128)S(1)}, u32[]{:S(2)}, u32[]{:S(2)}) collective-permute-start(f32[112,128]{1,0:T(8,128)S(1)} %add_add_fusion.1), channel_id=1, source_target_pairs={{0,4},{1,5},{2,6},{3,7},{4,0},{5,1},{6,2},{7,3},{8,12},{9,13},{10,... | collective-permute-start | bytes 172040 | tf_op jit(solution)/shard_map/ppermute | solution.py:557
  62.4 4.8 %collective-permute-start.21 = (f32[112,128]{1,0:T(8,128)S(1)}, f32[112,128]{1,0:T(8,128)S(1)}, u32[]{:S(2)}, u32[]{:S(2)}) collective-permute-start(f32[112,128]{1,0:T(8,128)S(1)} %add_add_fusion.1), channel_id=1, source_target_pairs={{0,2},{1,3},{2,0},{3,1},{4,6},{5,7},{6,4},{7,5},{8,10},{9,11},{10,... | collective-permute-start | bytes 172040 | tf_op jit(solution)/shard_map/ppermute | solution.py:557
  (5 other events, 26.5 us)

commit v6 on v5

--- a/solution.py
+++ b/solution.py
@@ -139,7 +139,7 @@
     total = blocks[0] + blocks[1] + blocks[2] + blocks[3] + blocks[4] + blocks[5]
     spread = jnp.broadcast_to(mean, (rank, rank))
     first = (1.0 - tumble) * gram + tumble * spread * spread.T
-    weights = mm(jnp.concatenate([first, -courant * total, courant * table], axis=0), into)
+    weights = apply(jnp.concatenate([first, -courant * total, courant * table], axis=0), into)
     weights = jnp.concatenate([weights[b * rank:(b + 1) * rank] for b in range(8)], axis=1)
     return weights, mm(into, spread, (0, 0))[:, :1]
 
@@ -454,9 +454,9 @@
     spread = jnp.broadcast_to(mean, (rank, rank))
     solved = (1.0 + tumble) * unit(rank) - tumble * spread * spread.T + courant * mm(inverse, drift, (0, 0))
     rows = [(1.0 - tumble) * upper] + [courant * mm(inverse, part) for part in inner]
-    rows = mm(jnp.concatenate(rows, axis=0), solved)
+    rows = apply(jnp.concatenate(rows, axis=0), solved)
     mid_mean = mm(rows[:rank], spread)[:, :1]
-    moved = apply(rows if basis is None else mm(rows, basis), orient)
+    moved = apply(rows if basis is None else apply(rows, basis), orient)
     new = moved[:rank] + mid_mean * (tumble / (1.0 - tumble))
     for d in range(3):
         new = new + plus[d:d + 1] * moved[(1 + 2 * d) * rank:(2 + 2 * d) * rank]

time: 77 us -> 76.5 us (level)
  Pallas kernels: 24.2 us -> 22.8 us
  waiting for transfers between devices: 19.4 us -> 20.3 us
    pallas_call x9, Pallas kernels: 24.2 us -> 22.8 us  [call(): pl.pallas_call(body, out_shape=[jax.ShapeDtypeStruct(shape, jnp.float32)...]
  transfers between devices with their start and end apart: 25 -> 25, of which waited for: 15 -> 17; matrix products, arithmetic and copies ran while one was open for 0% -> 0% of each run, Pallas kernels for 15% -> 14%
where the time goes in v6:
time: 76.5 us; the launch traced here: 76.3 us
  starting transfers between devices  30.9 us (40%)
  Pallas kernels  22.8 us (30%)
  waiting for transfers between devices  20.3 us (27%)
  local copies, waits for them, and re-layouts  1.23 us (2%)
  between operations  0.98 us (1%)
    pallas_call x9, Pallas kernels, call(): pl.pallas_call(body, out_shape=[jax.ShapeDtypeStruct(shape, jnp.float32)...  22.8 us
    ppermute x16, waiting for transfers between devices, swapped(): lax.ppermute(value, ('gx', 'gy'), [(i, i ^ bits) for i in range(count)])  16.3 us
    ppermute x16, starting transfers between devices, swapped(): lax.ppermute(value, ('gx', 'gy'), [(i, i ^ bits) for i in range(count)])  16.2 us
    ppermute x5, starting transfers between devices, down(): return lax.ppermute(value, axis, shifted(axis, False))  11 us
    ppermute x4, starting transfers between devices, up(): return lax.ppermute(value, axis, shifted(axis, True))  3.69 us
    ppermute x4, waiting for transfers between devices, up(): return lax.ppermute(value, axis, shifted(axis, True))  2.2 us
    ppermute x5, waiting for transfers between devices, down(): return lax.ppermute(value, axis, shifted(axis, False))  1.72 us
  transfers between devices with their start and end apart: 25, of which 17 were waited for; matrix products, arithmetic and copies ran while one was open for 0% of the time, Pallas kernels for 14%

profile of v6, /device:TPU:0, one launch (start us, length us, event | category | flops | bytes accessed | tf_op | source)
XLA Modules:
  0.0 76.3 jit_solution(6874075941731318440)
XLA Ops:
  2.3 3.0 %collective-permute-start = (f32[64,512]{1,0:T(8,128)S(1)}, f32[64,512]{1,0:T(8,128)S(1)}, u32[]{:S(2)}, u32[]{:S(2)}) collective-permute-start(f32[64,512]{1,0:T(8,128)S(1)} %get-tuple-element.34), channel_id=1, source_target_pairs={{0,8},{8,16},{16,24},{24,0},{1,9},{9,17},{17,25},{25,1},{2,10},{10... | collective-permute-start | bytes 393224 | tf_op jit(solution)/shard_map/ppermute | solution.py:582
  6.3 3.5 %collective-permute-start.3 = (f32[64,128]{1,0:T(8,128)S(1)}, f32[64,128]{1,0:T(8,128)S(1)}, u32[]{:S(2)}, u32[]{:S(2)}) collective-permute-start(f32[64,128]{1,0:T(8,128)S(1)} %get-tuple-element.37), channel_id=1, source_target_pairs={{0,7},{1,0},{2,1},{3,2},{4,3},{5,4},{6,5},{7,6},{8,15},{9,8},{10,9... | collective-permute-start | bytes 98312 | tf_op jit(solution)/shard_map/ppermute | solution.py:586
  9.8 1.5 %shard_map.68 = (f32[384,64]{1,0:T(8,128)S(1)}, f32[64,1]{1,0:T(8,128)S(1)}, f32[64,512]{1,0:T(8,128)S(1)}, f32[64,1]{1,0:T(8,128)S(1)}) custom-call(f32[64,2048]{1,0:T(8,128)S(1)} %bitcast.4, f32[3,2048]{1,0:T(4,128)S(1)} %copy-done.2, f32[64,64]{1,0:T(8,128)S(1)} %copy-done.3), custom_call_target="tpu_custom_call" | custom-call | tf_op jit(solution)/shard_map/pallas_call | solution.py:228
  11.4 1.3 %collective-permute-done.1.xa = f32[64,512]{1,0:T(8,128)S(1)} collective-permute-done((f32[64,512]{1,0:T(8,128)S(1)}, f32[64,512]{1,0:T(8,128)S(1)}, u32[]{:S(2)}, u32[]{:S(2)}) %collective-permute-start.1) | collective-permute-done | bytes 131104 | tf_op jit(solution)/shard_map/ppermute | solution.py:586
  13.5 1.5 %collective-permute-start.4 = (f32[64,512]{1,0:T(8,128)S(1)}, f32[64,512]{1,0:T(8,128)S(1)}, u32[]{:S(2)}, u32[]{:S(2)}) collective-permute-start(f32[64,512]{1,0:T(8,128)S(1)} %get-tuple-element.42), channel_id=1, source_target_pairs={{0,24},{8,0},{16,8},{24,16},{1,25},{9,1},{17,9},{25,17},{2,26},{10... | collective-permute-start | bytes 393224 | tf_op jit(solution)/shard_map/ppermute | solution.py:586
  15.0 2.4 %collective-permute-start.5 = (f32[64,256]{1,0:T(8,128)S(1)}, f32[64,256]{1,0:T(8,128)S(1)}, u32[]{:S(2)}, u32[]{:S(2)}) collective-permute-start(f32[64,256]{1,0:T(8,128)S(1)} %get-tuple-element.43), channel_id=1, source_target_pairs={{0,7},{1,0},{2,1},{3,2},{4,3},{5,4},{6,5},{7,6},{8,15},{9,8},{10,9... | collective-permute-start | bytes 196616 | tf_op jit(solution)/shard_map/ppermute | solution.py:586
  17.5 2.6 %shard_map.69 = (f32[64,2048]{1,0:T(8,128)S(1)}, f32[256,128]{1,0:T(8,128)S(1)}, f32[64,512]{1,0:T(8,128)S(1)}, f32[64,128]{1,0:T(8,128)S(1)}) custom-call(f32[64,2048]{1,0:T(8,128)S(1)} %get-tuple-element.33.field_ref, f32[64,512]{1,0:T(8,128)S(1)} %collective-permute-done.xb, f32[64,512]{1,0:T(8,128)S(1)} %collective-permute-done.1.xa, ...), custom_call_target="tpu_custom_call" | custom-call | flops 1000000000 | bytes 8000000 | tf_op jit(solution)/shard_map/pallas_call | solution.py:228
  20.5 1.3 %collective-permute-done.6 = f32[224,128]{1,0:T(8,128)S(1)} collective-permute-done((f32[224,128]{1,0:T(8,128)S(1)}, f32[224,128]{1,0:T(8,128)S(1)}, u32[]{:S(2)}, u32[]{:S(2)}) %collective-permute-start.6) | collective-permute-done | bytes 114720 | tf_op jit(solution)/shard_map/ppermute | solution.py:557
  22.9 1.4 %collective-permute-start.9 = (f32[112,128]{1,0:T(8,128)S(1)}, f32[112,128]{1,0:T(8,128)S(1)}, u32[]{:S(2)}, u32[]{:S(2)}) collective-permute-start(f32[112,128]{1,0:T(8,128)S(1)} %slice_select_fusion.1), channel_id=1, source_target_pairs={{0,24},{1,25},{2,26},{3,27},{4,28},{5,29},{6,30},{7,31},{8,16},{9,... | collective-permute-start | bytes 172040 | tf_op jit(solution)/shard_map/ppermute | solution.py:557
  26.1 2.1 %collective-permute-done.9 = f32[112,128]{1,0:T(8,128)S(1)} collective-permute-done((f32[112,128]{1,0:T(8,128)S(1)}, f32[112,128]{1,0:T(8,128)S(1)}, u32[]{:S(2)}, u32[]{:S(2)}) %collective-permute-start.9) | collective-permute-done | bytes 57376 | tf_op jit(solution)/shard_map/ppermute | solution.py:557
  28.5 2.1 %collective-permute-done.10.yb = f32[64,128]{1,0:T(8,128)S(1)} collective-permute-done((f32[64,128]{1,0:T(8,128)S(1)}, f32[64,128]{1,0:T(8,128)S(1)}, u32[]{:S(2)}, u32[]{:S(2)}) %collective-permute-start.10) | collective-permute-done | bytes 32800 | tf_op jit(solution)/shard_map/ppermute | solution.py:582
  30.5 1.6 %collective-permute-start.15 = (f32[112,128]{1,0:T(8,128)S(1)}, f32[112,128]{1,0:T(8,128)S(1)}, u32[]{:S(2)}, u32[]{:S(2)}) collective-permute-start(f32[112,128]{1,0:T(8,128)S(1)} %add_add_fusion.3), channel_id=1, source_target_pairs={{0,6},{1,7},{2,4},{3,5},{4,2},{5,3},{6,0},{7,1},{8,14},{9,15},{10,... | collective-permute-start | bytes 172040 | tf_op jit(solution)/shard_map/ppermute | solution.py:557
  32.1 2.8 %collective-permute-start.13 = (f32[112,128]{1,0:T(8,128)S(1)}, f32[112,128]{1,0:T(8,128)S(1)}, u32[]{:S(2)}, u32[]{:S(2)}) collective-permute-start(f32[112,128]{1,0:T(8,128)S(1)} %add_add_fusion.3), channel_id=1, source_target_pairs={{0,2},{1,3},{2,0},{3,1},{4,6},{5,7},{6,4},{7,5},{8,10},{9,11},{10,... | collective-permute-start | bytes 172040 | tf_op jit(solution)/shard_map/ppermute | solution.py:557
  34.9 2.2 %collective-permute-done.15 = f32[112,128]{1,0:T(8,128)S(1)} collective-permute-done((f32[112,128]{1,0:T(8,128)S(1)}, f32[112,128]{1,0:T(8,128)S(1)}, u32[]{:S(2)}, u32[]{:S(2)}) %collective-permute-start.15) | collective-permute-done | bytes 57376 | tf_op jit(solution)/shard_map/ppermute | solution.py:557
  39.0 2.5 %collective-permute-start.11 = (f32[64,640]{1,0:T(8,128)S(1)}, f32[64,640]{1,0:T(8,128)S(1)}, u32[]{:S(2)}, u32[]{:S(2)}) collective-permute-start(f32[64,640]{1,0:T(8,128)S(1)} %shard_map.72), channel_id=1, source_target_pairs={{0,24},{8,0},{16,8},{24,16},{1,25},{9,1},{17,9},{25,17},{2,26},{10... | collective-permute-start | bytes 491528 | tf_op jit(solution)/shard_map/ppermute | solution.py:586
  41.5 6.6 %shard_map.73 = (f32[64,512]{1,0:T(8,128)S(1)}, f32[64,1]{1,0:T(8,128)S(1)}, f32[64,1]{1,0:T(8,128)S(1)}, f32[64,2048]{1,0:T(8,128)S(1)}, f32[64,64]{1,0:T(8,128)S(1)}, /*index=5*/f32[384,64]{1,0:T(8,128)S(1)}) custom-call(f32[224,128]{1,0:T(8,128)S(1)} %pad_maximum_fusion.sums_ref, f32[64,2048]{1,0:T(8,128)S(1)} %bitcast.5, ...), custom_call_target="tpu_custom_call" | custom-call | flops 1 | bytes 1 | tf_op jit(solution)/shard_map/pallas_call | solution.py:228
  48.4 2.9 %shard_map.74 = (f32[64,2048]{1,0:T(8,128)S(1)}, f32[224,128]{1,0:T(8,128)S(1)}) custom-call(f32[64,2048]{1,0:T(8,128)S(1)} %get-tuple-element.41.field_ref, f32[64,512]{1,0:T(8,128)S(1)} %collective-permute-done.4.xa, f32[64,256]{1,0:T(8,128)S(1)} %collective-permute-done.5.ya, f32[64,128]{1,0:T(8,128)S(1)} %collective-permute-done.10.yb, ...), custom_call_target="tpu_custom_call" | custom-call | tf_op jit(solution)/shard_map/pallas_call | solution.py:228
  51.5 1.3 %collective-permute-done.17 = f32[224,128]{1,0:T(8,128)S(1)} collective-permute-done((f32[224,128]{1,0:T(8,128)S(1)}, f32[224,128]{1,0:T(8,128)S(1)}, u32[]{:S(2)}, u32[]{:S(2)}) %collective-permute-start.17) | collective-permute-done | bytes 114720 | tf_op jit(solution)/shard_map/ppermute | solution.py:557
  52.8 1.4 %collective-permute-start.19 = (f32[112,128]{1,0:T(8,128)S(1)}, f32[112,128]{1,0:T(8,128)S(1)}, u32[]{:S(2)}, u32[]{:S(2)}) collective-permute-start(f32[112,128]{1,0:T(8,128)S(1)} %slice_select_fusion), channel_id=1, source_target_pairs={{0,16},{1,17},{2,18},{3,19},{4,20},{5,21},{6,22},{7,23},{8,24},{9,... | collective-permute-start | bytes 172040 | tf_op jit(solution)/shard_map/ppermute | solution.py:557
  57.0 2.3 %collective-permute-done.20 = f32[112,128]{1,0:T(8,128)S(1)} collective-permute-done((f32[112,128]{1,0:T(8,128)S(1)}, f32[112,128]{1,0:T(8,128)S(1)}, u32[]{:S(2)}, u32[]{:S(2)}) %collective-permute-start.20) | collective-permute-done | bytes 57376 | tf_op jit(solution)/shard_map/ppermute | solution.py:557
  59.5 1.8 %collective-permute-start.23 = (f32[112,128]{1,0:T(8,128)S(1)}, f32[112,128]{1,0:T(8,128)S(1)}, u32[]{:S(2)}, u32[]{:S(2)}) collective-permute-start(f32[112,128]{1,0:T(8,128)S(1)} %add_add_fusion.1), channel_id=1, source_target_pairs={{0,6},{1,7},{2,4},{3,5},{4,2},{5,3},{6,0},{7,1},{8,14},{9,15},{10,... | collective-permute-start | bytes 172040 | tf_op jit(solution)/shard_map/ppermute | solution.py:557
  62.4 1.6 %collective-permute-start.21 = (f32[112,128]{1,0:T(8,128)S(1)}, f32[112,128]{1,0:T(8,128)S(1)}, u32[]{:S(2)}, u32[]{:S(2)}) collective-permute-start(f32[112,128]{1,0:T(8,128)S(1)} %add_add_fusion.1), channel_id=1, source_target_pairs={{0,2},{1,3},{2,0},{3,1},{4,6},{5,7},{6,4},{7,5},{8,10},{9,11},{10,... | collective-permute-start | bytes 172040 | tf_op jit(solution)/shard_map/ppermute | solution.py:557
  63.9 2.0 %collective-permute-done.23 = f32[112,128]{1,0:T(8,128)S(1)} collective-permute-done((f32[112,128]{1,0:T(8,128)S(1)}, f32[112,128]{1,0:T(8,128)S(1)}, u32[]{:S(2)}, u32[]{:S(2)}) %collective-permute-start.23) | collective-permute-done | bytes 57376 | tf_op jit(solution)/shard_map/ppermute | solution.py:557
  68.5 7.7 %shard_map.75 = (f32[2048,64]{1,0:T(8,128)}, f32[64,64]{1,0:T(8,128)}, f32[64,2048]{1,0:T(8,128)}) custom-call(f32[224,128]{1,0:T(8,128)S(1)} %pad_maximum_fusion.1.sums_ref, f32[64,2048]{1,0:T(8,128)S(1)} %get-tuple-element.56.orient_ref, f32[64,64]{1,0:T(8,128)S(1)} %get-tuple-element.57.basis_ref, f32[384,64]{1,0:T(8,128)S(1)} %get-tuple-element.58.table_ref, ...), custom_call_target="tpu_custom_call" | custom-call | tf_op jit(solution)/shard_map/pallas_call | solution.py:228
  (55 shorter events, 16.0 us)
Async XLA Ops:
  2.3 9.2 %collective-permute-start = (f32[64,512]{1,0:T(8,128)S(1)}, f32[64,512]{1,0:T(8,128)S(1)}, u32[]{:S(2)}, u32[]{:S(2)}) collective-permute-start(f32[64,512]{1,0:T(8,128)S(1)} %get-tuple-element.34), channel_id=1, source_target_pairs={{0,8},{8,16},{16,24},{24,0},{1,9},{9,17},{17,25},{25,1},{2,10},{10... | collective-permute-start | bytes 393224 | tf_op jit(solution)/shard_map/ppermute | solution.py:582
  5.3 7.5 %collective-permute-start.1 = (f32[64,512]{1,0:T(8,128)S(1)}, f32[64,512]{1,0:T(8,128)S(1)}, u32[]{:S(2)}, u32[]{:S(2)}) collective-permute-start(f32[64,512]{1,0:T(8,128)S(1)} %get-tuple-element.35), channel_id=1, source_target_pairs={{0,24},{8,0},{16,8},{24,16},{1,25},{9,1},{17,9},{25,17},{2,26},{10... | collective-permute-start | bytes 393224 | tf_op jit(solution)/shard_map/ppermute | solution.py:586
  6.3 5.1 %collective-permute-start.2 = (f32[64,128]{1,0:T(8,128)S(1)}, f32[64,128]{1,0:T(8,128)S(1)}, u32[]{:S(2)}, u32[]{:S(2)}) collective-permute-start(f32[64,128]{1,0:T(8,128)S(1)} %get-tuple-element.36), channel_id=1, source_target_pairs={{0,1},{1,2},{2,3},{3,4},{4,5},{5,6},{6,7},{7,0},{8,9},{9,10},{10,1... | collective-permute-start | bytes 98312 | tf_op jit(solution)/shard_map/ppermute | solution.py:582
  6.3 5.1 %collective-permute-start.3 = (f32[64,128]{1,0:T(8,128)S(1)}, f32[64,128]{1,0:T(8,128)S(1)}, u32[]{:S(2)}, u32[]{:S(2)}) collective-permute-start(f32[64,128]{1,0:T(8,128)S(1)} %get-tuple-element.37), channel_id=1, source_target_pairs={{0,7},{1,0},{2,1},{3,2},{4,3},{5,4},{6,5},{7,6},{8,15},{9,8},{10,9... | collective-permute-start | bytes 98312 | tf_op jit(solution)/shard_map/ppermute | solution.py:586
  13.5 6.5 %collective-permute-start.4 = (f32[64,512]{1,0:T(8,128)S(1)}, f32[64,512]{1,0:T(8,128)S(1)}, u32[]{:S(2)}, u32[]{:S(2)}) collective-permute-start(f32[64,512]{1,0:T(8,128)S(1)} %get-tuple-element.42), channel_id=1, source_target_pairs={{0,24},{8,0},{16,8},{24,16},{1,25},{9,1},{17,9},{25,17},{2,26},{10... | collective-permute-start | bytes 393224 | tf_op jit(solution)/shard_map/ppermute | solution.py:586
  15.0 5.0 %collective-permute-start.5 = (f32[64,256]{1,0:T(8,128)S(1)}, f32[64,256]{1,0:T(8,128)S(1)}, u32[]{:S(2)}, u32[]{:S(2)}) collective-permute-start(f32[64,256]{1,0:T(8,128)S(1)} %get-tuple-element.43), channel_id=1, source_target_pairs={{0,7},{1,0},{2,1},{3,2},{4,3},{5,4},{6,5},{7,6},{8,15},{9,8},{10,9... | collective-permute-start | bytes 196616 | tf_op jit(solution)/shard_map/ppermute | solution.py:586
  20.4 1.4 %collective-permute-start.6 = (f32[224,128]{1,0:T(8,128)S(1)}, f32[224,128]{1,0:T(8,128)S(1)}, u32[]{:S(2)}, u32[]{:S(2)}) collective-permute-start(f32[224,128]{1,0:T(8,128)S(1)} %get-tuple-element.47), channel_id=1, source_target_pairs={{0,1},{1,0},{2,3},{3,2},{4,5},{5,4},{6,7},{7,6},{8,9},{9,8},{10,11... | collective-permute-start | bytes 344072 | tf_op jit(solution)/shard_map/ppermute | solution.py:557
  21.8 4.2 %collective-permute-start.8 = (f32[112,128]{1,0:T(8,128)S(1)}, f32[112,128]{1,0:T(8,128)S(1)}, u32[]{:S(2)}, u32[]{:S(2)}) collective-permute-start(f32[112,128]{1,0:T(8,128)S(1)} %slice_select_fusion.1), channel_id=1, source_target_pairs={{0,16},{1,17},{2,18},{3,19},{4,20},{5,21},{6,22},{7,23},{8,24},{9,... | collective-permute-start | bytes 172040 | tf_op jit(solution)/shard_map/ppermute | solution.py:557
  22.9 5.3 %collective-permute-start.9 = (f32[112,128]{1,0:T(8,128)S(1)}, f32[112,128]{1,0:T(8,128)S(1)}, u32[]{:S(2)}, u32[]{:S(2)}) collective-permute-start(f32[112,128]{1,0:T(8,128)S(1)} %slice_select_fusion.1), channel_id=1, source_target_pairs={{0,24},{1,25},{2,26},{3,27},{4,28},{5,29},{6,30},{7,31},{8,16},{9,... | collective-permute-start | bytes 172040 | tf_op jit(solution)/shard_map/ppermute | solution.py:557
  24.3 4.2 %collective-permute-start.7 = (f32[112,128]{1,0:T(8,128)S(1)}, f32[112,128]{1,0:T(8,128)S(1)}, u32[]{:S(2)}, u32[]{:S(2)}) collective-permute-start(f32[112,128]{1,0:T(8,128)S(1)} %slice_select_fusion.1), channel_id=1, source_target_pairs={{0,8},{1,9},{2,10},{3,11},{4,12},{5,13},{6,14},{7,15},{8,0},{9,1},... | collective-permute-start | bytes 172040 | tf_op jit(solution)/shard_map/ppermute | solution.py:557
  25.4 5.1 %collective-permute-start.10 = (f32[64,128]{1,0:T(8,128)S(1)}, f32[64,128]{1,0:T(8,128)S(1)}, u32[]{:S(2)}, u32[]{:S(2)}) collective-permute-start(f32[64,128]{1,0:T(8,128)S(1)} %get-tuple-element.46.y_last_ref), channel_id=1, source_target_pairs={{0,1},{1,2},{2,3},{3,4},{4,5},{5,6},{6,7},{7,0},{8,9},{9,10},{10,1... | collective-permute-start | bytes 98312 | tf_op jit(solution)/shard_map/ppermute | solution.py:582
  30.5 6.6 %collective-permute-start.15 = (f32[112,128]{1,0:T(8,128)S(1)}, f32[112,128]{1,0:T(8,128)S(1)}, u32[]{:S(2)}, u32[]{:S(2)}) collective-permute-start(f32[112,128]{1,0:T(8,128)S(1)} %add_add_fusion.3), channel_id=1, source_target_pairs={{0,6},{1,7},{2,4},{3,5},{4,2},{5,3},{6,0},{7,1},{8,14},{9,15},{10,... | collective-permute-start | bytes 172040 | tf_op jit(solution)/shard_map/ppermute | solution.py:557
  32.1 6.0 %collective-permute-start.14 = (f32[112,128]{1,0:T(8,128)S(1)}, f32[112,128]{1,0:T(8,128)S(1)}, u32[]{:S(2)}, u32[]{:S(2)}) collective-permute-start(f32[112,128]{1,0:T(8,128)S(1)} %add_add_fusion.3), channel_id=1, source_target_pairs={{0,4},{1,5},{2,6},{3,7},{4,0},{5,1},{6,2},{7,3},{8,12},{9,13},{10,... | collective-permute-start | bytes 172040 | tf_op jit(solution)/shard_map/ppermute | solution.py:557
  32.1 6.0 %collective-permute-start.13 = (f32[112,128]{1,0:T(8,128)S(1)}, f32[112,128]{1,0:T(8,128)S(1)}, u32[]{:S(2)}, u32[]{:S(2)}) collective-permute-start(f32[112,128]{1,0:T(8,128)S(1)} %add_add_fusion.3), channel_id=1, source_target_pairs={{0,2},{1,3},{2,0},{3,1},{4,6},{5,7},{6,4},{7,5},{8,10},{9,11},{10,... | collective-permute-start | bytes 172040 | tf_op jit(solution)/shard_map/ppermute | solution.py:557
  38.1 3.3 %collective-permute-start.16 = (f32[112,128]{1,0:T(8,128)S(1)}, f32[112,128]{1,0:T(8,128)S(1)}, u32[]{:S(2)}, u32[]{:S(2)}) collective-permute-start(f32[112,128]{1,0:T(8,128)S(1)} %add_add_fusion.2), channel_id=1, source_target_pairs={{0,1},{1,0},{2,3},{3,2},{4,5},{5,4},{6,7},{7,6},{8,9},{9,8},{10,11... | collective-permute-start | bytes 172040 | tf_op jit(solution)/shard_map/ppermute | solution.py:557
  38.2 9.9 %collective-permute-start.12 = (f32[64,640]{1,0:T(8,128)S(1)}, f32[64,640]{1,0:T(8,128)S(1)}, u32[]{:S(2)}, u32[]{:S(2)}) collective-permute-start(f32[64,640]{1,0:T(8,128)S(1)} %get-tuple-element.49), channel_id=1, source_target_pairs={{0,8},{8,16},{16,24},{24,0},{1,9},{9,17},{17,25},{25,1},{2,10},{10... | collective-permute-start | bytes 491528 | tf_op jit(solution)/shard_map/ppermute | solution.py:582
  39.0 9.5 %collective-permute-start.11 = (f32[64,640]{1,0:T(8,128)S(1)}, f32[64,640]{1,0:T(8,128)S(1)}, u32[]{:S(2)}, u32[]{:S(2)}) collective-permute-start(f32[64,640]{1,0:T(8,128)S(1)} %shard_map.72), channel_id=1, source_target_pairs={{0,24},{8,0},{16,8},{24,16},{1,25},{9,1},{17,9},{25,17},{2,26},{10... | collective-permute-start | bytes 491528 | tf_op jit(solution)/shard_map/ppermute | solution.py:586
  51.4 1.4 %collective-permute-start.17 = (f32[224,128]{1,0:T(8,128)S(1)}, f32[224,128]{1,0:T(8,128)S(1)}, u32[]{:S(2)}, u32[]{:S(2)}) collective-permute-start(f32[224,128]{1,0:T(8,128)S(1)} %get-tuple-element.55), channel_id=1, source_target_pairs={{0,1},{1,0},{2,3},{3,2},{4,5},{5,4},{6,7},{7,6},{8,9},{9,8},{10,11... | collective-permute-start | bytes 344072 | tf_op jit(solution)/shard_map/ppermute | solution.py:557
  52.8 4.2 %collective-permute-start.19 = (f32[112,128]{1,0:T(8,128)S(1)}, f32[112,128]{1,0:T(8,128)S(1)}, u32[]{:S(2)}, u32[]{:S(2)}) collective-permute-start(f32[112,128]{1,0:T(8,128)S(1)} %slice_select_fusion), channel_id=1, source_target_pairs={{0,16},{1,17},{2,18},{3,19},{4,20},{5,21},{6,22},{7,23},{8,24},{9,... | collective-permute-start | bytes 172040 | tf_op jit(solution)/shard_map/ppermute | solution.py:557
  54.2 5.2 %collective-permute-start.20 = (f32[112,128]{1,0:T(8,128)S(1)}, f32[112,128]{1,0:T(8,128)S(1)}, u32[]{:S(2)}, u32[]{:S(2)}) collective-permute-start(f32[112,128]{1,0:T(8,128)S(1)} %slice_select_fusion), channel_id=1, source_target_pairs={{0,24},{1,25},{2,26},{3,27},{4,28},{5,29},{6,30},{7,31},{8,16},{9,... | collective-permute-start | bytes 172040 | tf_op jit(solution)/shard_map/ppermute | solution.py:557
  55.3 4.2 %collective-permute-start.18 = (f32[112,128]{1,0:T(8,128)S(1)}, f32[112,128]{1,0:T(8,128)S(1)}, u32[]{:S(2)}, u32[]{:S(2)}) collective-permute-start(f32[112,128]{1,0:T(8,128)S(1)} %slice_select_fusion), channel_id=1, source_target_pairs={{0,8},{1,9},{2,10},{3,11},{4,12},{5,13},{6,14},{7,15},{8,0},{9,1},... | collective-permute-start | bytes 172040 | tf_op jit(solution)/shard_map/ppermute | solution.py:557
  59.5 6.4 %collective-permute-start.23 = (f32[112,128]{1,0:T(8,128)S(1)}, f32[112,128]{1,0:T(8,128)S(1)}, u32[]{:S(2)}, u32[]{:S(2)}) collective-permute-start(f32[112,128]{1,0:T(8,128)S(1)} %add_add_fusion.1), channel_id=1, source_target_pairs={{0,6},{1,7},{2,4},{3,5},{4,2},{5,3},{6,0},{7,1},{8,14},{9,15},{10,... | collective-permute-start | bytes 172040 | tf_op jit(solution)/shard_map/ppermute | solution.py:557
  61.2 5.9 %collective-permute-start.22 = (f32[112,128]{1,0:T(8,128)S(1)}, f32[112,128]{1,0:T(8,128)S(1)}, u32[]{:S(2)}, u32[]{:S(2)}) collective-permute-start(f32[112,128]{1,0:T(8,128)S(1)} %add_add_fusion.1), channel_id=1, source_target_pairs={{0,4},{1,5},{2,6},{3,7},{4,0},{5,1},{6,2},{7,3},{8,12},{9,13},{10,... | collective-permute-start | bytes 172040 | tf_op jit(solution)/shard_map/ppermute | solution.py:557
  62.4 4.8 %collective-permute-start.21 = (f32[112,128]{1,0:T(8,128)S(1)}, f32[112,128]{1,0:T(8,128)S(1)}, u32[]{:S(2)}, u32[]{:S(2)}) collective-permute-start(f32[112,128]{1,0:T(8,128)S(1)} %add_add_fusion.1), channel_id=1, source_target_pairs={{0,2},{1,3},{2,0},{3,1},{4,6},{5,7},{6,4},{7,5},{8,10},{9,11},{10,... | collective-permute-start | bytes 172040 | tf_op jit(solution)/shard_map/ppermute | solution.py:557
  (5 other events, 26.5 us)

commit v7 on v6

--- a/solution.py
+++ b/solution.py
@@ -244,11 +244,15 @@
     y_first_ref[...], y_last_ref[...] = y_layer(slabs, dims, 0), y_layer(slabs, dims, dims[1] - 1)
 
 
-def table_kernel(orient_ref, e_ref, s_ref, table_ref, mean_ref, weight_ref, column_ref):
+def table_kernel(
+    dims, orient_ref, e_ref, s_ref, field_ref, table_ref, mean_ref, weight_ref, column_ref, first_ref, layers_ref
+):
     _, table, mean = tables(orient_ref[...], e_ref[...])
     table_ref[...] = table
     mean_ref[...] = mean
-    weight_ref[...], column_ref[...] = stage_weights(unit(mean.shape[0]), table, mean, s_ref[...].T)
+    weights, column = stage_weights(unit(mean.shape[0]), table, mean, s_ref[...].T)
+    weight_ref[...], column_ref[...] = weights, column
+    first_ref[...], layers_ref[...] = k_edges_inside(dims, field_ref[...], weights, column)
 
 
 CENTRE, X_BEHIND, X_AHEAD, Y_BEHIND, Y_AHEAD, Z_BEHIND, Z_AHEAD = range(7)
@@ -283,34 +287,53 @@
         )
 
 
-def k_edges(dims, field, weights, column, xb, xa, yb, ya):
+def k_edges_inside(dims, field, weights, column):
     lx, ly, lz = dims
     width = lx * lz
     w = Weights(weights, column)
     slabs = slabs_of(field, dims)
-    from_behind, from_ahead = w.one(xb, X_BEHIND), w.one(xa, X_AHEAD)
-    before = w.one(yb, Y_BEHIND)
+    none = jnp.zeros((field.shape[0], width), jnp.float32)
     part = w.times(slabs[0])
     first = (
-        w.whole(slabs[0], part, dims) + from_behind + w.one(slabs[1], X_AHEAD)
-        + y_behind(part[Y_BEHIND], before, dims)
-        + y_ahead(part[Y_AHEAD], roll(w.one(ya, Y_AHEAD), -lz), dims)
+        w.whole(slabs[0], part, dims) + w.one(slabs[1], X_AHEAD)
+        + y_behind(part[Y_BEHIND], none, dims) + y_ahead(part[Y_AHEAD], none, dims)
     )
     layers = jnp.concatenate([y_layer(slabs, dims, 0), y_layer(slabs, dims, 1)], axis=1)
     part = w.times(layers)
-    after = w.one(y_layer(slabs, dims, 2), Y_AHEAD)
     lane = lane_index(width)
-    over_y = [before + part[Y_AHEAD][:, width:], part[Y_BEHIND][:, :width] + after]
-    over_x = []
+    over_y = [
+        part[Y_AHEAD][:, width:], part[Y_BEHIND][:, :width] + w.one(y_layer(slabs, dims, 2), Y_AHEAD)
+    ]
+    sums = []
     for n in range(2):
         here = slice(n * width, (n + 1) * width)
-        over_x.append(
-            jnp.where(lane < lz, roll(from_behind[:, :width], -n * lz), roll(part[X_BEHIND][:, here], lz))
-            + jnp.where(
-                lane >= width - lz, roll(from_ahead[:, :width], -(n + 1) * lz), roll(part[X_AHEAD][:, here], -lz)
-            )
+        sums.append(
+            over_y[n] + jnp.where(lane < lz, 0.0, roll(part[X_BEHIND][:, here], lz))
+            + jnp.where(lane >= width - lz, 0.0, roll(part[X_AHEAD][:, here], -lz))
         )
-    return first, w.whole(layers, part, dims) + jnp.concatenate([x + y for x, y in zip(over_x, over_y)], axis=1)
+    return first, w.whole(layers, part, dims) + jnp.concatenate(sums, axis=1)
+
+
+def k_edges(dims, first, layers, weights, column, xb, xa, yb, ya):
+    lx, ly, lz = dims
+    width = lx * lz
+    w = Weights(weights, column)
+    from_behind, from_ahead = w.one(xb, X_BEHIND), w.one(xa[:, :width], X_AHEAD)
+    before, after = w.one(yb, Y_BEHIND), w.one(ya, Y_AHEAD)
+    lane = lane_index(width)
+    low, high = lane < lz, lane >= width - lz
+    first = first + from_behind
+    first = jnp.concatenate([
+        first[:, :width] + jnp.where(low, before, 0.0),
+        first[:, width:-width],
+        first[:, -width:] + jnp.where(high, roll(after, -lz), 0.0),
+    ], axis=1)
+    sides = [
+        jnp.where(low, roll(from_behind[:, :width], -n * lz), 0.0)
+        + jnp.where(high, roll(from_ahead, -(n + 1) * lz), 0.0)
+        for n in range(2)
+    ]
+    return first, layers + jnp.concatenate([sides[0] + before, sides[1]], axis=1)
 
 
 def k_stage(dims, field, weights, column, xb, xa, yb, ya, further=None):
@@ -394,9 +417,9 @@
         ref[:, x * slab:(x + 1) * slab] = value
 
 
-def edge_kernel(dims, field_ref, xb, xa, yb, ya, weight_ref, column_ref, first_ref, y_first_ref):
+def edge_kernel(dims, first, layers, xb, xa, yb, ya, weight_ref, column_ref, first_ref, y_first_ref):
     first_ref[...], y_first_ref[...] = k_edges(
-        dims, field_ref[...], weight_ref[...], column_ref[...], xb[...], xa[...], yb[...], ya[...]
+        dims, first[...], layers[...], weight_ref[...], column_ref[...], xb[...], xa[...], yb[...], ya[...]
     )
 
 
@@ -603,11 +626,14 @@
     basis = [(rank, count), (6 * rank, rank)]
     column_shape, weight_shape = (rank, 1), (rank, 8 * rank)
     orient = orient_factor.T
-    table, mean, weights, column = call(
-        table_kernel, [basis[1], column_shape, weight_shape, column_shape], orient, directions, coupling
+    table, mean, weights, column, first, y_first = call(
+        functools.partial(table_kernel, dims), [basis[1], column_shape, weight_shape, column_shape, slab, two_layers],
+        orient, directions, coupling, field,
     )
     near = (field, xb, xa, yb, ya, weights, column)
-    first, y_first = call(functools.partial(edge_kernel, dims), [slab, two_layers], *near)
+    first, y_first = call(
+        functools.partial(edge_kernel, dims), [slab, two_layers], first, y_first, *near[1:]
+    )
     xa, ya = down(first, "gx"), down(y_first, "gy")
     field, part, last, y_last = call(
         functools.partial(first_kernel, dims), [whole, (4 * rank, 2 * rank), slab, layer], *near, mean,

time: 76.5 us -> 76.1 us (level)
  transfers between devices with their start and end apart: 25 -> 25, of which waited for: 17 -> 16; matrix products, arithmetic and copies ran while one was open for 0% -> 0% of each run, Pallas kernels for 14% -> 15%
where the time goes in v7:
time: 76.1 us; the launch traced here: 75.9 us
  starting transfers between devices  30.9 us (41%)
  Pallas kernels  23 us (30%)
  waiting for transfers between devices  19.7 us (26%)
  local copies, waits for them, and re-layouts  1.23 us (2%)
  between operations  1 us (1%)
    pallas_call x9, Pallas kernels, call(): pl.pallas_call(body, out_shape=[jax.ShapeDtypeStruct(shape, jnp.float32)...  23 us
    ppermute x16, waiting for transfers between devices, swapped(): lax.ppermute(value, ('gx', 'gy'), [(i, i ^ bits) for i in range(count)])  16.4 us
    ppermute x16, starting transfers between devices, swapped(): lax.ppermute(value, ('gx', 'gy'), [(i, i ^ bits) for i in range(count)])  16.2 us
    ppermute x5, starting transfers between devices, down(): return lax.ppermute(value, axis, shifted(axis, False))  11 us
    ppermute x4, starting transfers between devices, up(): return lax.ppermute(value, axis, shifted(axis, True))  3.69 us
    ppermute x4, waiting for transfers between devices, up(): return lax.ppermute(value, axis, shifted(axis, True))  2.09 us
  transfers between devices with their start and end apart: 25, of which 16 were waited for; matrix products, arithmetic and copies ran while one was open for 0% of the time, Pallas kernels for 15%

profile of v7, /device:TPU:0, one launch (start us, length us, event | category | flops | bytes accessed | tf_op | source)
XLA Modules:
  0.0 75.9 jit_solution(2810604676683889440)
XLA Ops:
  2.3 3.0 %collective-permute-start = (f32[64,512]{1,0:T(8,128)S(1)}, f32[64,512]{1,0:T(8,128)S(1)}, u32[]{:S(2)}, u32[]{:S(2)}) collective-permute-start(f32[64,512]{1,0:T(8,128)S(1)} %get-tuple-element.36), channel_id=1, source_target_pairs={{0,8},{8,16},{16,24},{24,0},{1,9},{9,17},{17,25},{25,1},{2,10},{10... | collective-permute-start | bytes 393224 | tf_op jit(solution)/shard_map/ppermute | solution.py:605
  6.3 3.5 %collective-permute-start.3 = (f32[64,128]{1,0:T(8,128)S(1)}, f32[64,128]{1,0:T(8,128)S(1)}, u32[]{:S(2)}, u32[]{:S(2)}) collective-permute-start(f32[64,128]{1,0:T(8,128)S(1)} %get-tuple-element.39), channel_id=1, source_target_pairs={{0,7},{1,0},{2,1},{3,2},{4,3},{5,4},{6,5},{7,6},{8,15},{9,8},{10,9... | collective-permute-start | bytes 98312 | tf_op jit(solution)/shard_map/ppermute | solution.py:609
  9.8 2.1 %shard_map.68 = (f32[384,64]{1,0:T(8,128)S(1)}, f32[64,1]{1,0:T(8,128)S(1)}, f32[64,512]{1,0:T(8,128)S(1)}, f32[64,1]{1,0:T(8,128)S(1)}, f32[64,512]{1,0:T(8,128)S(1)}, /*index=5*/f32[64,256]{1,0:T(8,128)S(1)}) custom-call(f32[64,2048]{1,0:T(8,128)S(1)} %bitcast.4, f32[3,2048]{1,0:T(4,128)S(1)} %copy-done.2, f32[64,64]{1,0:T(8,128)S(1)} %copy-done.3, ...), custom_call_target="tpu_custom_call" | custom-call | tf_op jit(solution)/shard_map/pallas_call | solution.py:228
  13.2 1.5 %collective-permute-start.4 = (f32[64,512]{1,0:T(8,128)S(1)}, f32[64,512]{1,0:T(8,128)S(1)}, u32[]{:S(2)}, u32[]{:S(2)}) collective-permute-start(f32[64,512]{1,0:T(8,128)S(1)} %get-tuple-element.46), channel_id=1, source_target_pairs={{0,24},{8,0},{16,8},{24,16},{1,25},{9,1},{17,9},{25,17},{2,26},{10... | collective-permute-start | bytes 393224 | tf_op jit(solution)/shard_map/ppermute | solution.py:609
  14.6 2.4 %collective-permute-start.5 = (f32[64,256]{1,0:T(8,128)S(1)}, f32[64,256]{1,0:T(8,128)S(1)}, u32[]{:S(2)}, u32[]{:S(2)}) collective-permute-start(f32[64,256]{1,0:T(8,128)S(1)} %get-tuple-element.47), channel_id=1, source_target_pairs={{0,7},{1,0},{2,1},{3,2},{4,3},{5,4},{6,5},{7,6},{8,15},{9,8},{10,9... | collective-permute-start | bytes 196616 | tf_op jit(solution)/shard_map/ppermute | solution.py:609
  17.1 2.6 %shard_map.69 = (f32[64,2048]{1,0:T(8,128)S(1)}, f32[256,128]{1,0:T(8,128)S(1)}, f32[64,512]{1,0:T(8,128)S(1)}, f32[64,128]{1,0:T(8,128)S(1)}) custom-call(f32[64,2048]{1,0:T(8,128)S(1)} %get-tuple-element.35.field_ref, f32[64,512]{1,0:T(8,128)S(1)} %collective-permute-done.xb, f32[64,512]{1,0:T(8,128)S(1)} %collective-permute-done.1.xa, ...), custom_call_target="tpu_custom_call" | custom-call | flops 1000000000 | bytes 8000000 | tf_op jit(solution)/shard_map/pallas_call | solution.py:228
  20.1 1.3 %collective-permute-done.6 = f32[224,128]{1,0:T(8,128)S(1)} collective-permute-done((f32[224,128]{1,0:T(8,128)S(1)}, f32[224,128]{1,0:T(8,128)S(1)}, u32[]{:S(2)}, u32[]{:S(2)}) %collective-permute-start.6) | collective-permute-done | bytes 114720 | tf_op jit(solution)/shard_map/ppermute | solution.py:580
  22.5 1.4 %collective-permute-start.9 = (f32[112,128]{1,0:T(8,128)S(1)}, f32[112,128]{1,0:T(8,128)S(1)}, u32[]{:S(2)}, u32[]{:S(2)}) collective-permute-start(f32[112,128]{1,0:T(8,128)S(1)} %slice_select_fusion.1), channel_id=1, source_target_pairs={{0,24},{1,25},{2,26},{3,27},{4,28},{5,29},{6,30},{7,31},{8,16},{9,... | collective-permute-start | bytes 172040 | tf_op jit(solution)/shard_map/ppermute | solution.py:580
  25.7 2.1 %collective-permute-done.9 = f32[112,128]{1,0:T(8,128)S(1)} collective-permute-done((f32[112,128]{1,0:T(8,128)S(1)}, f32[112,128]{1,0:T(8,128)S(1)}, u32[]{:S(2)}, u32[]{:S(2)}) %collective-permute-start.9) | collective-permute-done | bytes 57376 | tf_op jit(solution)/shard_map/ppermute | solution.py:580
  28.1 2.1 %collective-permute-done.10.yb = f32[64,128]{1,0:T(8,128)S(1)} collective-permute-done((f32[64,128]{1,0:T(8,128)S(1)}, f32[64,128]{1,0:T(8,128)S(1)}, u32[]{:S(2)}, u32[]{:S(2)}) %collective-permute-start.10) | collective-permute-done | bytes 32800 | tf_op jit(solution)/shard_map/ppermute | solution.py:605
  30.1 1.6 %collective-permute-start.15 = (f32[112,128]{1,0:T(8,128)S(1)}, f32[112,128]{1,0:T(8,128)S(1)}, u32[]{:S(2)}, u32[]{:S(2)}) collective-permute-start(f32[112,128]{1,0:T(8,128)S(1)} %add_add_fusion.3), channel_id=1, source_target_pairs={{0,6},{1,7},{2,4},{3,5},{4,2},{5,3},{6,0},{7,1},{8,14},{9,15},{10,... | collective-permute-start | bytes 172040 | tf_op jit(solution)/shard_map/ppermute | solution.py:580
  31.7 2.8 %collective-permute-start.13 = (f32[112,128]{1,0:T(8,128)S(1)}, f32[112,128]{1,0:T(8,128)S(1)}, u32[]{:S(2)}, u32[]{:S(2)}) collective-permute-start(f32[112,128]{1,0:T(8,128)S(1)} %add_add_fusion.3), channel_id=1, source_target_pairs={{0,2},{1,3},{2,0},{3,1},{4,6},{5,7},{6,4},{7,5},{8,10},{9,11},{10,... | collective-permute-start | bytes 172040 | tf_op jit(solution)/shard_map/ppermute | solution.py:580
  34.5 2.2 %collective-permute-done.15 = f32[112,128]{1,0:T(8,128)S(1)} collective-permute-done((f32[112,128]{1,0:T(8,128)S(1)}, f32[112,128]{1,0:T(8,128)S(1)}, u32[]{:S(2)}, u32[]{:S(2)}) %collective-permute-start.15) | collective-permute-done | bytes 57376 | tf_op jit(solution)/shard_map/ppermute | solution.py:580
  38.6 2.5 %collective-permute-start.11 = (f32[64,640]{1,0:T(8,128)S(1)}, f32[64,640]{1,0:T(8,128)S(1)}, u32[]{:S(2)}, u32[]{:S(2)}) collective-permute-start(f32[64,640]{1,0:T(8,128)S(1)} %shard_map.72), channel_id=1, source_target_pairs={{0,24},{8,0},{16,8},{24,16},{1,25},{9,1},{17,9},{25,17},{2,26},{10... | collective-permute-start | bytes 491528 | tf_op jit(solution)/shard_map/ppermute | solution.py:609
  41.1 6.6 %shard_map.73 = (f32[64,512]{1,0:T(8,128)S(1)}, f32[64,1]{1,0:T(8,128)S(1)}, f32[64,1]{1,0:T(8,128)S(1)}, f32[64,2048]{1,0:T(8,128)S(1)}, f32[64,64]{1,0:T(8,128)S(1)}, /*index=5*/f32[384,64]{1,0:T(8,128)S(1)}) custom-call(f32[224,128]{1,0:T(8,128)S(1)} %pad_maximum_fusion.sums_ref, f32[64,2048]{1,0:T(8,128)S(1)} %bitcast.5, ...), custom_call_target="tpu_custom_call" | custom-call | flops 1 | bytes 1 | tf_op jit(solution)/shard_map/pallas_call | solution.py:228
  48.1 2.9 %shard_map.74 = (f32[64,2048]{1,0:T(8,128)S(1)}, f32[224,128]{1,0:T(8,128)S(1)}) custom-call(f32[64,2048]{1,0:T(8,128)S(1)} %get-tuple-element.43.field_ref, f32[64,512]{1,0:T(8,128)S(1)} %collective-permute-done.4.xa, f32[64,256]{1,0:T(8,128)S(1)} %collective-permute-done.5.ya, f32[64,128]{1,0:T(8,128)S(1)} %collective-permute-done.10.yb, ...), custom_call_target="tpu_custom_call" | custom-call | tf_op jit(solution)/shard_map/pallas_call | solution.py:228
  51.1 1.3 %collective-permute-done.17 = f32[224,128]{1,0:T(8,128)S(1)} collective-permute-done((f32[224,128]{1,0:T(8,128)S(1)}, f32[224,128]{1,0:T(8,128)S(1)}, u32[]{:S(2)}, u32[]{:S(2)}) %collective-permute-start.17) | collective-permute-done | bytes 114720 | tf_op jit(solution)/shard_map/ppermute | solution.py:580
  52.4 1.4 %collective-permute-start.19 = (f32[112,128]{1,0:T(8,128)S(1)}, f32[112,128]{1,0:T(8,128)S(1)}, u32[]{:S(2)}, u32[]{:S(2)}) collective-permute-start(f32[112,128]{1,0:T(8,128)S(1)} %slice_select_fusion), channel_id=1, source_target_pairs={{0,16},{1,17},{2,18},{3,19},{4,20},{5,21},{6,22},{7,23},{8,24},{9,... | collective-permute-start | bytes 172040 | tf_op jit(solution)/shard_map/ppermute | solution.py:580
  56.7 2.4 %collective-permute-done.20 = f32[112,128]{1,0:T(8,128)S(1)} collective-permute-done((f32[112,128]{1,0:T(8,128)S(1)}, f32[112,128]{1,0:T(8,128)S(1)}, u32[]{:S(2)}, u32[]{:S(2)}) %collective-permute-start.20) | collective-permute-done | bytes 57376 | tf_op jit(solution)/shard_map/ppermute | solution.py:580
  59.1 1.8 %collective-permute-start.23 = (f32[112,128]{1,0:T(8,128)S(1)}, f32[112,128]{1,0:T(8,128)S(1)}, u32[]{:S(2)}, u32[]{:S(2)}) collective-permute-start(f32[112,128]{1,0:T(8,128)S(1)} %add_add_fusion.1), channel_id=1, source_target_pairs={{0,6},{1,7},{2,4},{3,5},{4,2},{5,3},{6,0},{7,1},{8,14},{9,15},{10,... | collective-permute-start | bytes 172040 | tf_op jit(solution)/shard_map/ppermute | solution.py:580
  62.0 1.6 %collective-permute-start.21 = (f32[112,128]{1,0:T(8,128)S(1)}, f32[112,128]{1,0:T(8,128)S(1)}, u32[]{:S(2)}, u32[]{:S(2)}) collective-permute-start(f32[112,128]{1,0:T(8,128)S(1)} %add_add_fusion.1), channel_id=1, source_target_pairs={{0,2},{1,3},{2,0},{3,1},{4,6},{5,7},{6,4},{7,5},{8,10},{9,11},{10,... | collective-permute-start | bytes 172040 | tf_op jit(solution)/shard_map/ppermute | solution.py:580
  63.6 2.0 %collective-permute-done.23 = f32[112,128]{1,0:T(8,128)S(1)} collective-permute-done((f32[112,128]{1,0:T(8,128)S(1)}, f32[112,128]{1,0:T(8,128)S(1)}, u32[]{:S(2)}, u32[]{:S(2)}) %collective-permute-start.23) | collective-permute-done | bytes 57376 | tf_op jit(solution)/shard_map/ppermute | solution.py:580
  65.5 1.2 %collective-permute-done.22 = f32[112,128]{1,0:T(8,128)S(1)} collective-permute-done((f32[112,128]{1,0:T(8,128)S(1)}, f32[112,128]{1,0:T(8,128)S(1)}, u32[]{:S(2)}, u32[]{:S(2)}) %collective-permute-start.22) | collective-permute-done | bytes 57376 | tf_op jit(solution)/shard_map/ppermute | solution.py:580
  68.1 7.7 %shard_map.75 = (f32[2048,64]{1,0:T(8,128)}, f32[64,64]{1,0:T(8,128)}, f32[64,2048]{1,0:T(8,128)}) custom-call(f32[224,128]{1,0:T(8,128)S(1)} %pad_maximum_fusion.1.sums_ref, f32[64,2048]{1,0:T(8,128)S(1)} %get-tuple-element.60.orient_ref, f32[64,64]{1,0:T(8,128)S(1)} %get-tuple-element.61.basis_ref, f32[384,64]{1,0:T(8,128)S(1)} %get-tuple-element.62.table_ref, ...), custom_call_target="tpu_custom_call" | custom-call | tf_op jit(solution)/shard_map/pallas_call | solution.py:228
  (55 shorter events, 15.1 us)
Async XLA Ops:
  2.3 9.7 %collective-permute-start = (f32[64,512]{1,0:T(8,128)S(1)}, f32[64,512]{1,0:T(8,128)S(1)}, u32[]{:S(2)}, u32[]{:S(2)}) collective-permute-start(f32[64,512]{1,0:T(8,128)S(1)} %get-tuple-element.36), channel_id=1, source_target_pairs={{0,8},{8,16},{16,24},{24,0},{1,9},{9,17},{17,25},{25,1},{2,10},{10... | collective-permute-start | bytes 393224 | tf_op jit(solution)/shard_map/ppermute | solution.py:605
  5.3 7.5 %collective-permute-start.1 = (f32[64,512]{1,0:T(8,128)S(1)}, f32[64,512]{1,0:T(8,128)S(1)}, u32[]{:S(2)}, u32[]{:S(2)}) collective-permute-start(f32[64,512]{1,0:T(8,128)S(1)} %get-tuple-element.37), channel_id=1, source_target_pairs={{0,24},{8,0},{16,8},{24,16},{1,25},{9,1},{17,9},{25,17},{2,26},{10... | collective-permute-start | bytes 393224 | tf_op jit(solution)/shard_map/ppermute | solution.py:609
  6.3 5.6 %collective-permute-start.2 = (f32[64,128]{1,0:T(8,128)S(1)}, f32[64,128]{1,0:T(8,128)S(1)}, u32[]{:S(2)}, u32[]{:S(2)}) collective-permute-start(f32[64,128]{1,0:T(8,128)S(1)} %get-tuple-element.38), channel_id=1, source_target_pairs={{0,1},{1,2},{2,3},{3,4},{4,5},{5,6},{6,7},{7,0},{8,9},{9,10},{10,1... | collective-permute-start | bytes 98312 | tf_op jit(solution)/shard_map/ppermute | solution.py:605
  6.3 5.6 %collective-permute-start.3 = (f32[64,128]{1,0:T(8,128)S(1)}, f32[64,128]{1,0:T(8,128)S(1)}, u32[]{:S(2)}, u32[]{:S(2)}) collective-permute-start(f32[64,128]{1,0:T(8,128)S(1)} %get-tuple-element.39), channel_id=1, source_target_pairs={{0,7},{1,0},{2,1},{3,2},{4,3},{5,4},{6,5},{7,6},{8,15},{9,8},{10,9... | collective-permute-start | bytes 98312 | tf_op jit(solution)/shard_map/ppermute | solution.py:609
  13.2 6.5 %collective-permute-start.4 = (f32[64,512]{1,0:T(8,128)S(1)}, f32[64,512]{1,0:T(8,128)S(1)}, u32[]{:S(2)}, u32[]{:S(2)}) collective-permute-start(f32[64,512]{1,0:T(8,128)S(1)} %get-tuple-element.46), channel_id=1, source_target_pairs={{0,24},{8,0},{16,8},{24,16},{1,25},{9,1},{17,9},{25,17},{2,26},{10... | collective-permute-start | bytes 393224 | tf_op jit(solution)/shard_map/ppermute | solution.py:609
  14.6 5.0 %collective-permute-start.5 = (f32[64,256]{1,0:T(8,128)S(1)}, f32[64,256]{1,0:T(8,128)S(1)}, u32[]{:S(2)}, u32[]{:S(2)}) collective-permute-start(f32[64,256]{1,0:T(8,128)S(1)} %get-tuple-element.47), channel_id=1, source_target_pairs={{0,7},{1,0},{2,1},{3,2},{4,3},{5,4},{6,5},{7,6},{8,15},{9,8},{10,9... | collective-permute-start | bytes 196616 | tf_op jit(solution)/shard_map/ppermute | solution.py:609
  20.0 1.4 %collective-permute-start.6 = (f32[224,128]{1,0:T(8,128)S(1)}, f32[224,128]{1,0:T(8,128)S(1)}, u32[]{:S(2)}, u32[]{:S(2)}) collective-permute-start(f32[224,128]{1,0:T(8,128)S(1)} %get-tuple-element.51), channel_id=1, source_target_pairs={{0,1},{1,0},{2,3},{3,2},{4,5},{5,4},{6,7},{7,6},{8,9},{9,8},{10,11... | collective-permute-start | bytes 344072 | tf_op jit(solution)/shard_map/ppermute | solution.py:580
  21.5 4.2 %collective-permute-start.8 = (f32[112,128]{1,0:T(8,128)S(1)}, f32[112,128]{1,0:T(8,128)S(1)}, u32[]{:S(2)}, u32[]{:S(2)}) collective-permute-start(f32[112,128]{1,0:T(8,128)S(1)} %slice_select_fusion.1), channel_id=1, source_target_pairs={{0,16},{1,17},{2,18},{3,19},{4,20},{5,21},{6,22},{7,23},{8,24},{9,... | collective-permute-start | bytes 172040 | tf_op jit(solution)/shard_map/ppermute | solution.py:580
  22.5 5.4 %collective-permute-start.9 = (f32[112,128]{1,0:T(8,128)S(1)}, f32[112,128]{1,0:T(8,128)S(1)}, u32[]{:S(2)}, u32[]{:S(2)}) collective-permute-start(f32[112,128]{1,0:T(8,128)S(1)} %slice_select_fusion.1), channel_id=1, source_target_pairs={{0,24},{1,25},{2,26},{3,27},{4,28},{5,29},{6,30},{7,31},{8,16},{9,... | collective-permute-start | bytes 172040 | tf_op jit(solution)/shard_map/ppermute | solution.py:580
  23.9 4.2 %collective-permute-start.7 = (f32[112,128]{1,0:T(8,128)S(1)}, f32[112,128]{1,0:T(8,128)S(1)}, u32[]{:S(2)}, u32[]{:S(2)}) collective-permute-start(f32[112,128]{1,0:T(8,128)S(1)} %slice_select_fusion.1), channel_id=1, source_target_pairs={{0,8},{1,9},{2,10},{3,11},{4,12},{5,13},{6,14},{7,15},{8,0},{9,1},... | collective-permute-start | bytes 172040 | tf_op jit(solution)/shard_map/ppermute | solution.py:580
  25.0 5.1 %collective-permute-start.10 = (f32[64,128]{1,0:T(8,128)S(1)}, f32[64,128]{1,0:T(8,128)S(1)}, u32[]{:S(2)}, u32[]{:S(2)}) collective-permute-start(f32[64,128]{1,0:T(8,128)S(1)} %get-tuple-element.50.y_last_ref), channel_id=1, source_target_pairs={{0,1},{1,2},{2,3},{3,4},{4,5},{5,6},{6,7},{7,0},{8,9},{9,10},{10,1... | collective-permute-start | bytes 98312 | tf_op jit(solution)/shard_map/ppermute | solution.py:605
  30.1 6.6 %collective-permute-start.15 = (f32[112,128]{1,0:T(8,128)S(1)}, f32[112,128]{1,0:T(8,128)S(1)}, u32[]{:S(2)}, u32[]{:S(2)}) collective-permute-start(f32[112,128]{1,0:T(8,128)S(1)} %add_add_fusion.3), channel_id=1, source_target_pairs={{0,6},{1,7},{2,4},{3,5},{4,2},{5,3},{6,0},{7,1},{8,14},{9,15},{10,... | collective-permute-start | bytes 172040 | tf_op jit(solution)/shard_map/ppermute | solution.py:580
  31.7 6.0 %collective-permute-start.14 = (f32[112,128]{1,0:T(8,128)S(1)}, f32[112,128]{1,0:T(8,128)S(1)}, u32[]{:S(2)}, u32[]{:S(2)}) collective-permute-start(f32[112,128]{1,0:T(8,128)S(1)} %add_add_fusion.3), channel_id=1, source_target_pairs={{0,4},{1,5},{2,6},{3,7},{4,0},{5,1},{6,2},{7,3},{8,12},{9,13},{10,... | collective-permute-start | bytes 172040 | tf_op jit(solution)/shard_map/ppermute | solution.py:580
  31.7 6.0 %collective-permute-start.13 = (f32[112,128]{1,0:T(8,128)S(1)}, f32[112,128]{1,0:T(8,128)S(1)}, u32[]{:S(2)}, u32[]{:S(2)}) collective-permute-start(f32[112,128]{1,0:T(8,128)S(1)} %add_add_fusion.3), channel_id=1, source_target_pairs={{0,2},{1,3},{2,0},{3,1},{4,6},{5,7},{6,4},{7,5},{8,10},{9,11},{10,... | collective-permute-start | bytes 172040 | tf_op jit(solution)/shard_map/ppermute | solution.py:580
  37.7 3.3 %collective-permute-start.16 = (f32[112,128]{1,0:T(8,128)S(1)}, f32[112,128]{1,0:T(8,128)S(1)}, u32[]{:S(2)}, u32[]{:S(2)}) collective-permute-start(f32[112,128]{1,0:T(8,128)S(1)} %add_add_fusion.2), channel_id=1, source_target_pairs={{0,1},{1,0},{2,3},{3,2},{4,5},{5,4},{6,7},{7,6},{8,9},{9,8},{10,11... | collective-permute-start | bytes 172040 | tf_op jit(solution)/shard_map/ppermute | solution.py:580
  37.8 9.9 %collective-permute-start.12 = (f32[64,640]{1,0:T(8,128)S(1)}, f32[64,640]{1,0:T(8,128)S(1)}, u32[]{:S(2)}, u32[]{:S(2)}) collective-permute-start(f32[64,640]{1,0:T(8,128)S(1)} %get-tuple-element.53), channel_id=1, source_target_pairs={{0,8},{8,16},{16,24},{24,0},{1,9},{9,17},{17,25},{25,1},{2,10},{10... | collective-permute-start | bytes 491528 | tf_op jit(solution)/shard_map/ppermute | solution.py:605
  38.6 9.5 %collective-permute-start.11 = (f32[64,640]{1,0:T(8,128)S(1)}, f32[64,640]{1,0:T(8,128)S(1)}, u32[]{:S(2)}, u32[]{:S(2)}) collective-permute-start(f32[64,640]{1,0:T(8,128)S(1)} %shard_map.72), channel_id=1, source_target_pairs={{0,24},{8,0},{16,8},{24,16},{1,25},{9,1},{17,9},{25,17},{2,26},{10... | collective-permute-start | bytes 491528 | tf_op jit(solution)/shard_map/ppermute | solution.py:609
  51.0 1.4 %collective-permute-start.17 = (f32[224,128]{1,0:T(8,128)S(1)}, f32[224,128]{1,0:T(8,128)S(1)}, u32[]{:S(2)}, u32[]{:S(2)}) collective-permute-start(f32[224,128]{1,0:T(8,128)S(1)} %get-tuple-element.59), channel_id=1, source_target_pairs={{0,1},{1,0},{2,3},{3,2},{4,5},{5,4},{6,7},{7,6},{8,9},{9,8},{10,11... | collective-permute-start | bytes 344072 | tf_op jit(solution)/shard_map/ppermute | solution.py:580
  52.4 4.2 %collective-permute-start.19 = (f32[112,128]{1,0:T(8,128)S(1)}, f32[112,128]{1,0:T(8,128)S(1)}, u32[]{:S(2)}, u32[]{:S(2)}) collective-permute-start(f32[112,128]{1,0:T(8,128)S(1)} %slice_select_fusion), channel_id=1, source_target_pairs={{0,16},{1,17},{2,18},{3,19},{4,20},{5,21},{6,22},{7,23},{8,24},{9,... | collective-permute-start | bytes 172040 | tf_op jit(solution)/shard_map/ppermute | solution.py:580
  53.8 5.2 %collective-permute-start.20 = (f32[112,128]{1,0:T(8,128)S(1)}, f32[112,128]{1,0:T(8,128)S(1)}, u32[]{:S(2)}, u32[]{:S(2)}) collective-permute-start(f32[112,128]{1,0:T(8,128)S(1)} %slice_select_fusion), channel_id=1, source_target_pairs={{0,24},{1,25},{2,26},{3,27},{4,28},{5,29},{6,30},{7,31},{8,16},{9,... | collective-permute-start | bytes 172040 | tf_op jit(solution)/shard_map/ppermute | solution.py:580
  54.9 4.2 %collective-permute-start.18 = (f32[112,128]{1,0:T(8,128)S(1)}, f32[112,128]{1,0:T(8,128)S(1)}, u32[]{:S(2)}, u32[]{:S(2)}) collective-permute-start(f32[112,128]{1,0:T(8,128)S(1)} %slice_select_fusion), channel_id=1, source_target_pairs={{0,8},{1,9},{2,10},{3,11},{4,12},{5,13},{6,14},{7,15},{8,0},{9,1},... | collective-permute-start | bytes 172040 | tf_op jit(solution)/shard_map/ppermute | solution.py:580
  59.1 6.4 %collective-permute-start.23 = (f32[112,128]{1,0:T(8,128)S(1)}, f32[112,128]{1,0:T(8,128)S(1)}, u32[]{:S(2)}, u32[]{:S(2)}) collective-permute-start(f32[112,128]{1,0:T(8,128)S(1)} %add_add_fusion.1), channel_id=1, source_target_pairs={{0,6},{1,7},{2,4},{3,5},{4,2},{5,3},{6,0},{7,1},{8,14},{9,15},{10,... | collective-permute-start | bytes 172040 | tf_op jit(solution)/shard_map/ppermute | solution.py:580
  60.9 5.9 %collective-permute-start.22 = (f32[112,128]{1,0:T(8,128)S(1)}, f32[112,128]{1,0:T(8,128)S(1)}, u32[]{:S(2)}, u32[]{:S(2)}) collective-permute-start(f32[112,128]{1,0:T(8,128)S(1)} %add_add_fusion.1), channel_id=1, source_target_pairs={{0,4},{1,5},{2,6},{3,7},{4,0},{5,1},{6,2},{7,3},{8,12},{9,13},{10,... | collective-permute-start | bytes 172040 | tf_op jit(solution)/shard_map/ppermute | solution.py:580
  62.0 4.8 %collective-permute-start.21 = (f32[112,128]{1,0:T(8,128)S(1)}, f32[112,128]{1,0:T(8,128)S(1)}, u32[]{:S(2)}, u32[]{:S(2)}) collective-permute-start(f32[112,128]{1,0:T(8,128)S(1)} %add_add_fusion.1), channel_id=1, source_target_pairs={{0,2},{1,3},{2,0},{3,1},{4,6},{5,7},{6,4},{7,5},{8,10},{9,11},{10,... | collective-permute-start | bytes 172040 | tf_op jit(solution)/shard_map/ppermute | solution.py:580
  (5 other events, 26.5 us)
